TPU v7x, 32 devices: a whole 2x2x4 slice. The times are simulated.
32 devices in a mesh: sky: 4 (over y, x), freq: 8 (over z, core).
Axes of the slice: x: 2, y: 2, z: 4, core: 2. Of those that a mesh axis runs over, the one named last changes fastest.
Arguments:
- pieces: bfloat16 [32, 64, 128, 128], P('sky', 'freq'), may hold values from -120 to 120
- beam: bfloat16 [32, 128, 128], P('sky'), may hold values from 0.099609375 to 1
- destination: int32 [32], P('sky'), may hold values from 0 to 15, as said below
- clip_tenths: int32 [3, 4], replicated, may hold values from 30 to 60
Outputs:
- significance: float32 [64, 512, 512], P('freq', 'sky')
Inputs may be any that keep to these rules, and one draw needn't show every extreme that they name: Among the 8 pieces of one index of sky, at most 4 have destinations in one tile, that is with equal destination // 4. In every draw some tile receives exactly 4 pieces from every index of sky.
All inputs are finite; a program needn't handle non-finite values.
Results may differ from a plain program's by a relative error of at most 0.0036.
Values may be sent and summed in bfloat16 or wider, within the bound.
No kernel may reach another device: no remote copies, remote signals or barrier semaphores. Data moves between devices by JAX's collectives and lax.ppermute only.
A program may use at most 128 MiB of HBM per device.

v0:
```python
import jax
import jax.numpy as jnp
from jax import lax
from jax.sharding import PartitionSpec as P

ROWB = 1
COLB = 4
RIM = 8
EDGE = 7
KERNELS = 3


REGULARIZER = 0.05
EPSILON = 1e-06
KERNEL_FWHM = (3.0, 6.0, 9.0)
HALF_WIDTHS = (0, 1, 3, 7)


def extended(block, sides, width):
    for axis, dim in sides:
        count = lax.axis_size(axis)
        forward = [(i, i + 1) for i in range(count - 1)]
        backward = [(target, source) for source, target in forward]
        low = lax.ppermute(
            lax.slice_in_dim(block, block.shape[dim] - width, None, axis=dim), axis, forward
        )
        high = lax.ppermute(lax.slice_in_dim(block, 0, width, axis=dim), axis, backward)
        block = jnp.concatenate([low, block, high], axis=dim)
    return block


def kernel_taps(kernel):
    offsets = jnp.arange(-RIM, RIM + 1).astype(jnp.float32)
    sigma = KERNEL_FWHM[kernel] / 2.3548
    return jnp.exp(-offsets * offsets / (2.0 * sigma * sigma)).astype(jnp.bfloat16)


def band_matrix(weights, rows_out, rows_in, shift):
    outer = jnp.arange(rows_out)[:, None]
    inner = jnp.arange(rows_in)[None, :]
    offset = inner - shift - outer
    inside = jnp.abs(offset) <= RIM
    picked = weights[jnp.clip(offset + RIM, 0, 2 * RIM)]
    return jnp.where(inside, picked, jnp.zeros_like(picked))


def smooth(padded, kernel):
    weights = kernel_taps(kernel)
    tall = padded.shape[1] - 2 * RIM
    broad = padded.shape[2]
    across_matrix = band_matrix(weights, broad, broad, 0)
    down_matrix = band_matrix(weights, tall, tall + 2 * RIM, RIM)
    across = jnp.einsum(
        "cyx,zx->cyz", padded, across_matrix, preferred_element_type=jnp.float32
    ).astype(jnp.bfloat16)
    return jnp.einsum(
        "vy,cyz->cvz", down_matrix, across, preferred_element_type=jnp.float32
    ).astype(jnp.bfloat16)


def boxcars(layer):
    channels = layer.shape[0] - 2 * EDGE
    running = layer[EDGE : EDGE + channels].astype(jnp.float32)
    found = [running]
    for step in range(1, EDGE + 1):
        running = (
            running
            + layer[EDGE - step : EDGE - step + channels].astype(jnp.float32)
            + layer[EDGE + step : EDGE + step + channels].astype(jnp.float32)
        )
        if step in HALF_WIDTHS:
            found.append(running)
    return found


def kernel_boxcars(layer):
    found = boxcars(layer)
    power = jnp.stack([jnp.sum(item * item, axis=(1, 2)) for item in found])
    return (found, power)


def raise_score(best, found, totals, thresholds, cells):
    noise_level = jnp.sqrt(totals / cells + EPSILON)
    factor = 10.0 / (thresholds.astype(jnp.float32)[:, None] * noise_level)
    for width, running in enumerate(found):
        best = jnp.maximum(best, jnp.abs(running) * factor[width][:, None, None])
    return best


def owner_tables(beams_in, labels_in, tile_blocks):
    onehot = labels_in[None, :] == jnp.arange(tile_blocks)[:, None]
    beam_wide = beams_in.astype(jnp.float32)
    coverage = (
        jnp.einsum(
            "bs,syx->byx",
            onehot.astype(jnp.float32),
            beam_wide * beam_wide,
            precision=lax.Precision.HIGHEST,
        )
        + REGULARIZER
    )
    return (onehot.astype(jnp.bfloat16), coverage)


def block_values(onehot, coverage, arrived):
    numerator = jnp.einsum("bs,scyx->bcyx", onehot, arrived, preferred_element_type=jnp.float32)
    return (numerator / coverage[:, None]).astype(jnp.bfloat16)


def shards(pieces, beam, destination, clip_tenths):
    sky_count = lax.axis_size("sky")
    piece_count, channels, block_size, _ = pieces.shape
    tile_blocks = ROWB * COLB
    capacity = max(2, 2 * piece_count // sky_count)
    slot_total = sky_count * capacity
    owners = destination // tile_blocks
    numbering = jnp.arange(piece_count)
    earlier = (owners[None, :] == owners[:, None]) & (numbering[None, :] < numbering[:, None])
    position = jnp.sum(earlier.astype(jnp.int32), axis=1)
    slot_index = owners * capacity + position
    weighted = (beam[:, None].astype(jnp.float32) * pieces.astype(jnp.float32)).astype(jnp.bfloat16)
    outgoing = (
        jnp.zeros((slot_total, channels, block_size, block_size), jnp.bfloat16)
        .at[slot_index]
        .set(weighted)
    )
    beams_out = (
        jnp.zeros((slot_total, block_size, block_size), jnp.bfloat16).at[slot_index].set(beam)
    )
    labels_out = (
        jnp.full((slot_total,), -1, jnp.int32).at[slot_index].set(destination % tile_blocks)
    )
    arrived, beams_in, labels_in = (
        lax.all_to_all(outgoing, "sky", split_axis=0, concat_axis=0, tiled=True),
        lax.all_to_all(beams_out, "sky", split_axis=0, concat_axis=0, tiled=True),
        lax.all_to_all(labels_out, "sky", split_axis=0, concat_axis=0, tiled=True),
    )
    onehot, coverage = owner_tables(beams_in, labels_in, tile_blocks)
    tile_values = block_values(onehot, coverage, arrived)
    combined = tile_values.reshape(ROWB, COLB, channels, block_size, block_size).transpose(
        2, 0, 3, 1, 4
    )
    combined = combined.reshape(channels, ROWB * block_size, COLB * block_size)
    padded = extended(combined, (("sky", 1),), RIM)
    smoothed = jnp.stack([smooth(padded, kernel) for kernel in range(KERNELS)])
    planes = extended(smoothed, (("freq", 1),), EDGE)
    cells = float(sky_count * ROWB * block_size * COLB * block_size)
    best = jnp.zeros((channels, ROWB * block_size, COLB * block_size), jnp.float32)
    results = [kernel_boxcars(planes[kernel]) for kernel in range(KERNELS)]
    powers = jnp.stack([item[1] for item in results])
    totals = lax.psum(powers, "sky")
    for kernel in range(KERNELS):
        best = raise_score(best, results[kernel][0], totals[kernel], clip_tenths[kernel], cells)
    return best


def solution(mesh):
    return jax.shard_map(
        shards,
        mesh=mesh,
        in_specs=(P("sky", "freq", None, None), P("sky", None, None), P("sky"), P()),
        out_specs=P("freq", "sky", None),
        check_vma=False,
    )
```

profile of v0, /device:TPU:1, one launch (start us, length us, event | category | flops | bytes accessed | tf_op | source)
XLA Modules:
  0.0 202.2 jit_solution(10415135661566152266)
XLA Ops:
  0.0 0.7 and_select_fusion
  0.7 0.2 convert_reduce_fusion
  0.9 0.6 scatter_custom_fusion
  1.5 0.7 all_to_all.12
  2.2 4.3 %all-to-all-start = ((s32[4,4,1]{1,2,0:T(1,128)}), s32[4,4,1]{1,2,0:T(1,128)S(1)}, u32[]{:S(2)}, u32[]{:S(2)}) async-start(s32[4,4,1]{1,2,0:T(1,128)} %bitcast), calls=%async_computation | async-start | bytes 4096 | tf_op jit(solution)/shard_map/all_to_all | solution.py:136
  6.5 0.9 broadcast_in_dim.10
  7.3 2.4 %scatter_fusion.1 = bf16[16,128,128]{2,1,0:T(8,128)(2,1)} fusion(bf16[16,128,128]{2,1,0:T(8,128)(2,1)} %broadcast_in_dim.10, s32[8]{0:T(128)S(1)} %compare_select_fusion.2, bf16[8,128,128]{2,1,0:T(8,128)(2,1)} %param.5), kind=kCustom, calls=%fused_computation.2 | custom fusion | bytes 786464 | tf_op jit(solution)/shard_map/scatter | solution.py:128
  9.8 0.2 all-to-all-done
  9.9 3.5 %all-to-all-start.2 = ((bf16[16,128,128]{2,1,0:T(8,128)(2,1)}), bf16[16,128,128]{2,1,0:T(8,128)(2,1)S(1)}, u32[]{:S(2)}, u32[]{:S(2)}) async-start(bf16[16,128,128]{2,1,0:T(8,128)(2,1)} %scatter_fusion.1), calls=%async_computation.2 | async-start | bytes 1048576 | tf_op jit(solution)/shard_map/all_to_all | solution.py:135
  13.5 2.2 %multiply_convert_fusion = bf16[8,8,128,128]{3,2,1,0:T(8,128)(2,1)S(1)} fusion(bf16[8,8,128,128]{3,2,1,0:T(8,128)(2,1)} %param.4, f32[8,128,128]{2,1,0:T(8,128)S(1)} %convert_element_type.370), kind=kLoop, calls=%fused_computation.7 | loop fusion | flops 3145728 | bytes 4718592 | tf_op jit(solution)/shard_map/convert_element_type | solution.py:121
  15.7 3.0 %broadcast_in_dim.9 = bf16[16,8,128,128]{3,2,1,0:T(8,128)(2,1)} broadcast(bf16[]{:T(256)} %constant.32.clone.1), dimensions={} | broadcast | bytes 4194306 | tf_op jit(solution)/shard_map/broadcast_in_dim | solution.py:123
  18.7 5.0 %scatter_fusion = bf16[16,8,128,128]{3,2,1,0:T(8,128)(2,1)} fusion(bf16[16,8,128,128]{3,2,1,0:T(8,128)(2,1)} %broadcast_in_dim.9, s32[8]{0:T(128)S(1)} %compare_select_fusion.2, bf16[8,8,128,128]{3,2,1,0:T(8,128)(2,1)S(1)} %multiply_convert_fusion), kind=kCustom, calls=%fused_computation.1 | custom fusion | bytes 6291488 | tf_op jit(solution)/shard_map/scatter | solution.py:125
  23.7 0.0 all-to-all-done.2
  23.7 4.9 %all-to-all-start.1 = ((bf16[16,8,128,128]{3,2,1,0:T(8,128)(2,1)}), bf16[16,8,128,128]{3,2,1,0:T(8,128)(2,1)}, u32[]{:S(2)}, u32[]{:S(2)}) async-start(bf16[16,8,128,128]{3,2,1,0:T(8,128)(2,1)} %scatter_fusion), calls=%async_computation.1 | async-start | bytes 8388608 | tf_op jit(solution)/shard_map/all_to_all | solution.py:134
  28.6 0.7 fusion.679
  29.4 0.7 fusion.678
  30.1 0.7 fusion.677
  30.8 0.5 broadcast.2179
  31.3 0.7 reduce.3
  32.0 0.1 eq.33
  32.1 0.1 convert_multiply_fusion.3
  32.2 1.1 convolution_add_fusion
  33.2 42.2 %all-to-all-done.1 = bf16[16,8,128,128]{3,2,1,0:T(8,128)(2,1)} async-done(((bf16[16,8,128,128]{3,2,1,0:T(8,128)(2,1)}), bf16[16,8,128,128]{3,2,1,0:T(8,128)(2,1)}, u32[]{:S(2)}, u32[]{:S(2)}) %all-to-all-start.1) | async-done | bytes 4194336 | tf_op jit(solution)/shard_map/all_to_all | solution.py:134
  75.4 4.8 %fusion.25 = bf16[8,1,128,4,128]{4,3,2,0,1:T(4,128)(2,1)S(1)} fusion(bf16[16,8,128,128]{3,2,1,0:T(8,128)(2,1)} %all-to-all-done.1, f32[4,128,128]{2,0,1:T(4,128)S(1)} %convolution_add_fusion, s32[16]{0:T(128)S(1)} %eq.33), kind=kOutput, calls=%fused_computation.93 | convolution fusion | flops 17825856 | bytes 5505088 | tf_op jit(solution)/shard_map/bs,scyx->bcyx/dot_general | solution.py:106
  80.3 0.4 reshape.273
  80.7 1.7 collective-permute-start
  82.4 1.5 collective-permute-start.1
  83.9 0.1 constant_dynamic-update-slice_fusion.1
  84.0 3.4 %collective-permute-done.1 = bf16[8,8,512]{2,1,0:T(8,128)(2,1)S(1)} collective-permute-done((bf16[8,8,512]{2,1,0:T(8,128)(2,1)S(1)}, bf16[8,8,512]{2,1,0:T(8,128)(2,1)S(1)}, u32[]{:S(2)}, u32[]{:S(2)}) %collective-permute-start.1) | collective-permute-done | bytes 65568 | tf_op jit(solution)/shard_map/ppermute | solution.py:27
  87.5 12.2 %convolution_convert_fusion.4 = bf16[8,512,128]{2,1,0:T(8,128)(2,1)S(1)} fusion(bf16[8,144,512]{2,1,0:T(8,128)(2,1)S(1)} %constant_dynamic-update-slice_fusion, bf16[]{:T(256)} %bitcast.61, bf16[]{:T(256)} %bitcast.62, bf16[]{:T(256)} %bitcast.63, bf16[]{:T(256)} %bitcast.64, bf16[]{:T(256)} %bitcast.65, bf16[]{:T(256)} %bitcast.67, bf16[]{:T(256)} %bitcast.66, ...), kind=kOutput, calls=%fused_computation.90 | convolution fusion | flops 767873024 | bytes 2228834 | tf_op jit(solution)/shard_map/vy,cyz->cvz/dot_general | solution.py:56
  99.7 12.0 %convolution_convert_fusion.5 = bf16[8,512,128]{2,1,0:T(8,128)(2,1)S(1)} fusion(bf16[8,144,512]{2,1,0:T(8,128)(2,1)S(1)} %constant_dynamic-update-slice_fusion, bf16[]{:T(256)} %bitcast.26, bf16[]{:T(256)} %bitcast.27, bf16[]{:T(256)} %bitcast.28, bf16[]{:T(256)} %bitcast.29, bf16[]{:T(256)} %bitcast.30, bf16[]{:T(256)} %bitcast.32, bf16[]{:T(256)} %bitcast.31, ...), kind=kOutput, calls=%fused_computation.91 | convolution fusion | flops 767873024 | bytes 2228834 | tf_op jit(solution)/shard_map/vy,cyz->cvz/dot_general | solution.py:56
  111.7 13.5 %convolution_convert_fusion.3 = bf16[8,512,128]{2,1,0:T(8,128)(2,1)S(1)} fusion(bf16[8,144,512]{2,1,0:T(8,128)(2,1)} %copy-done.6, bf16[]{:T(256)} %bitcast.84, bf16[]{:T(256)} %bitcast.85, bf16[]{:T(256)} %bitcast.86, bf16[]{:T(256)} %bitcast.87, bf16[]{:T(256)} %bitcast.88, bf16[]{:T(256)} %bitcast.90, bf16[]{:T(256)} %bitcast.89, bf16[]{:T(256)} %bitcast.74, ...), kind=kOutput, calls=%fused_computation.89 | convolution fusion | flops 767873024 | bytes 2228834 | tf_op jit(solution)/shard_map/vy,cyz->cvz/dot_general | solution.py:56
  125.3 0.3 pad_maximum_fusion.1
  125.6 0.0 copy-start.7
  125.6 1.2 fusion.675
  126.9 7.4 %collective-permute-start.2 = (bf16[3,7,128,512]{2,3,1,0:T(8,128)(2,1)S(1)}, bf16[3,7,128,512]{2,3,1,0:T(8,128)(2,1)S(1)}, u32[]{:S(2)}, u32[]{:S(2)}) collective-permute-start(bf16[3,7,128,512]{2,3,1,0:T(8,128)(2,1)S(1)} %get-tuple-element.31), channel_id=1, source_target_pairs={{0,1},{1,2},{2,3},{3,4},{4,5},{5,6},{6,7},{8,9},{9,10},{10,11},{11... | collective-permute-start | bytes 8257544 | tf_op jit(solution)/shard_map/ppermute | solution.py:24
  134.3 2.1 %collective-permute-start.3 = (bf16[3,7,128,512]{2,3,1,0:T(8,128)(2,1)S(1)}, bf16[3,7,128,512]{2,3,1,0:T(8,128)(2,1)S(1)}, u32[]{:S(2)}, u32[]{:S(2)}) collective-permute-start(bf16[3,7,128,512]{2,3,1,0:T(8,128)(2,1)S(1)} %get-tuple-element.32), channel_id=1, source_target_pairs={{1,0},{2,1},{3,2},{4,3},{5,4},{6,5},{7,6},{9,8},{10,9},{11,10},{12... | collective-permute-start | bytes 8257544 | tf_op jit(solution)/shard_map/ppermute | solution.py:27
  136.4 27.8 %collective-permute-done.2 = bf16[3,7,128,512]{2,3,1,0:T(8,128)(2,1)S(1)} collective-permute-done((bf16[3,7,128,512]{2,3,1,0:T(8,128)(2,1)S(1)}, bf16[3,7,128,512]{2,3,1,0:T(8,128)(2,1)S(1)}, u32[]{:S(2)}, u32[]{:S(2)}) %collective-permute-start.2) | collective-permute-done | bytes 2752544 | tf_op jit(solution)/shard_map/ppermute | solution.py:24
  164.2 4.4 %collective-permute-done.3 = bf16[3,7,128,512]{2,3,1,0:T(8,128)(2,1)S(1)} collective-permute-done((bf16[3,7,128,512]{2,3,1,0:T(8,128)(2,1)S(1)}, bf16[3,7,128,512]{2,3,1,0:T(8,128)(2,1)S(1)}, u32[]{:S(2)}, u32[]{:S(2)}) %collective-permute-start.3) | collective-permute-done | bytes 2752544 | tf_op jit(solution)/shard_map/ppermute | solution.py:27
  168.6 1.2 maximum_maximum_fusion
  169.8 1.2 multiply_reduce_fusion.4
  171.1 3.1 %multiply_reduce_fusion.8 = (f32[8]{0:T(128)S(1)}, f32[8]{0:T(128)S(1)}, f32[8]{0:T(128)S(1)}, f32[8]{0:T(128)S(1)}, f32[8]{0:T(128)S(1)}, /*index=5*/f32[8]{0:T(128)S(1)}, f32[8]{0:T(128)S(1)}, f32[8,128,512]{1,2,0:T(8,128)S(1)}) fusion(bf16[3,15,128,512]{2,3,1,0:T(8,128)(2,1)S(1)} %get-tuple-element.30, ...), kind=kLoop, calls=%fused_computation.84 | loop fusion | flops 19398600 | bytes 15728864 | tf_op jit(solution)/shard_map/reduce_sum | solution.py:78
  174.2 3.6 %multiply_reduce_fusion.7 = (f32[8]{0:T(128)S(1)}, f32[8,128,512]{1,2,0:T(8,128)S(1)}, f32[8]{0:T(128)S(1)}, f32[8,128,512]{1,2,0:T(8,128)}) fusion(bf16[3,15,128,512]{2,3,1,0:T(8,128)(2,1)S(1)} %get-tuple-element.30, bf16[3,15,128,512]{2,3,1,0:T(8,128)(2,1)S(1)} %get-tuple-element.29, bf16[8,512,128]{2,1,0:T(8,128)(2,1)S(1)} %convolution_convert_fusion.5, ...), kind=kLoop, calls=%fused_computation.83 | loop fusion | flops 17301488 | bytes 22020160 | tf_op jit(solution)/shard_map/reduce_sum | solution.py:78
  177.8 4.1 %multiply_reduce_fusion.6 = (f32[8]{0:T(128)S(1)}, f32[8,128,512]{1,2,0:T(8,128)}, f32[8]{0:T(128)S(1)}, f32[8,128,512]{1,2,0:T(8,128)}) fusion(bf16[3,15,128,512]{2,3,1,0:T(8,128)(2,1)S(1)} %get-tuple-element.30, bf16[3,15,128,512]{2,3,1,0:T(8,128)(2,1)S(1)} %get-tuple-element.29, f32[8,128,512]{1,2,0:T(8,128)S(1)} %get-tuple-element.12, ...), kind=kLoop, calls=%fused_computation.82 | loop fusion | flops 18874352 | bytes 25165888 | tf_op jit(solution)/shard_map/reduce_sum | solution.py:78
  182.0 8.0 %psum.7 = f32[3,4,8]{2,1,0:T(4,128)S(1)} all-reduce(f32[3,4,8]{2,1,0:T(4,128)S(1)} %pad_maximum_fusion.2), channel_id=1, replica_groups=mesh['sky'=4,'freq'=8] {'sky'}, use_global_device_ids=true, to_apply=%region_16.17 | all-reduce | flops 96 | bytes 768 | tf_op jit(solution)/shard_map/psum | solution.py:151
  190.0 0.1 fusion.552
  190.1 9.2 %fusion.14 = f32[8,128,512]{1,2,0:T(8,128)} fusion(f32[8,128,512]{1,2,0:T(8,128)} %get-tuple-element.26, f32[8,128,512]{1,2,0:T(8,128)} %copy-done.2, f32[8,128,512]{1,2,0:T(8,128)} %get-tuple-element.28, f32[8,128,512]{1,2,0:T(8,128)} %copy-done.3, f32[8,128,512]{1,2,0:T(8,128)} %get-tuple-element.14, f32[8,128,512]{1,2,0:T(8,128)} %copy-done.4, ...), kind=kLoop, calls=%fused_computation.31 | loop fusion | flops 26738688 | bytes 24117632 | tf_op jit(solution)/shard_map/max | solution.py:86
  199.3 2.9 %copy.18 = f32[8,128,512]{2,1,0:T(8,128)} copy(f32[8,128,512]{1,2,0:T(8,128)} %fusion.14) | data formatting | bytes 4194304 | tf_op jit(solution)/shard_map/max | solution.py:86
  (32 shorter events, 0.2 us)
Async XLA Ops:
  0.0 13.4 %copy-start.5 = (bf16[8,128,128]{2,1,0:T(8,128)(2,1)S(1)}, bf16[8,128,128]{2,1,0:T(8,128)(2,1)}, u32[]{:S(2)}) copy-start(bf16[8,128,128]{2,1,0:T(8,128)(2,1)} %param.5) | copy-start | bytes 786436
  2.2 7.8 %all-to-all-start = ((s32[4,4,1]{1,2,0:T(1,128)}), s32[4,4,1]{1,2,0:T(1,128)S(1)}, u32[]{:S(2)}, u32[]{:S(2)}) async-start(s32[4,4,1]{1,2,0:T(1,128)} %bitcast), calls=%async_computation | async-start | bytes 4096 | tf_op jit(solution)/shard_map/all_to_all | solution.py:136
  9.9 13.8 %all-to-all-start.2 = ((bf16[16,128,128]{2,1,0:T(8,128)(2,1)}), bf16[16,128,128]{2,1,0:T(8,128)(2,1)S(1)}, u32[]{:S(2)}, u32[]{:S(2)}) async-start(bf16[16,128,128]{2,1,0:T(8,128)(2,1)} %scatter_fusion.1), calls=%async_computation.2 | async-start | bytes 1048576 | tf_op jit(solution)/shard_map/all_to_all | solution.py:135
  23.7 51.7 %all-to-all-start.1 = ((bf16[16,8,128,128]{3,2,1,0:T(8,128)(2,1)}), bf16[16,8,128,128]{3,2,1,0:T(8,128)(2,1)}, u32[]{:S(2)}, u32[]{:S(2)}) async-start(bf16[16,8,128,128]{3,2,1,0:T(8,128)(2,1)} %scatter_fusion), calls=%async_computation.1 | async-start | bytes 8388608 | tf_op jit(solution)/shard_map/all_to_all | solution.py:134
  80.7 3.2 %collective-permute-start = (bf16[8,8,512]{2,1,0:T(8,128)(2,1)S(1)}, bf16[8,8,512]{2,1,0:T(8,128)(2,1)S(1)}, u32[]{:S(2)}, u32[]{:S(2)}) collective-permute-start(bf16[8,8,512]{2,1,0:T(8,128)(2,1)S(1)} %get-tuple-element.34), channel_id=1, source_target_pairs={{0,8},{8,16},{16,24},{1,9},{9,17},{17,25},{2,10},{10,18},{18,26},{... | collective-permute-start | bytes 196616 | tf_op jit(solution)/shard_map/ppermute | solution.py:24
  82.4 5.0 %collective-permute-start.1 = (bf16[8,8,512]{2,1,0:T(8,128)(2,1)S(1)}, bf16[8,8,512]{2,1,0:T(8,128)(2,1)S(1)}, u32[]{:S(2)}, u32[]{:S(2)}) collective-permute-start(bf16[8,8,512]{2,1,0:T(8,128)(2,1)S(1)} %get-tuple-element.33), channel_id=1, source_target_pairs={{8,0},{16,8},{24,16},{9,1},{17,9},{25,17},{10,2},{18,10},{26,18},{... | collective-permute-start | bytes 196616 | tf_op jit(solution)/shard_map/ppermute | solution.py:27
  87.5 12.2 %copy-start.6 = (bf16[8,144,512]{2,1,0:T(8,128)(2,1)}, bf16[8,144,512]{2,1,0:T(8,128)(2,1)S(1)}, u32[]{:S(2)}) copy-start(bf16[8,144,512]{2,1,0:T(8,128)(2,1)S(1)} %constant_dynamic-update-slice_fusion) | copy-start | bytes 3538948
  125.6 10.8 %copy-start.7 = (s32[3,4]{1,0:T(4,128)S(1)}, s32[3,4]{1,0:T(4,128)}, u32[]{:S(2)}) copy-start(s32[3,4]{1,0:T(4,128)} %param.7) | copy-start | bytes 148
  126.9 37.4 %collective-permute-start.2 = (bf16[3,7,128,512]{2,3,1,0:T(8,128)(2,1)S(1)}, bf16[3,7,128,512]{2,3,1,0:T(8,128)(2,1)S(1)}, u32[]{:S(2)}, u32[]{:S(2)}) collective-permute-start(bf16[3,7,128,512]{2,3,1,0:T(8,128)(2,1)S(1)} %get-tuple-element.31), channel_id=1, source_target_pairs={{0,1},{1,2},{2,3},{3,4},{4,5},{5,6},{6,7},{8,9},{9,10},{10,11},{11... | collective-permute-start | bytes 8257544 | tf_op jit(solution)/shard_map/ppermute | solution.py:24
  134.3 34.4 %collective-permute-start.3 = (bf16[3,7,128,512]{2,3,1,0:T(8,128)(2,1)S(1)}, bf16[3,7,128,512]{2,3,1,0:T(8,128)(2,1)S(1)}, u32[]{:S(2)}, u32[]{:S(2)}) collective-permute-start(bf16[3,7,128,512]{2,3,1,0:T(8,128)(2,1)S(1)} %get-tuple-element.32), channel_id=1, source_target_pairs={{1,0},{2,1},{3,2},{4,3},{5,4},{6,5},{7,6},{9,8},{10,9},{11,10},{12... | collective-permute-start | bytes 8257544 | tf_op jit(solution)/shard_map/ppermute | solution.py:27
  169.8 8.0 %copy-start = (bf16[3,15,128,512]{2,3,1,0:T(8,128)(2,1)}, bf16[3,15,128,512]{2,3,1,0:T(8,128)(2,1)S(1)}, u32[]{:S(2)}) copy-start(bf16[3,15,128,512]{2,3,1,0:T(8,128)(2,1)S(1)} %get-tuple-element.29) | copy-start | bytes 17694724
  169.8 8.0 %copy-start.1 = (bf16[3,15,128,512]{2,3,1,0:T(8,128)(2,1)}, bf16[3,15,128,512]{2,3,1,0:T(8,128)(2,1)S(1)}, u32[]{:S(2)}) copy-start(bf16[3,15,128,512]{2,3,1,0:T(8,128)(2,1)S(1)} %get-tuple-element.30) | copy-start | bytes 17694724
  171.1 3.1 %copy-start.3 = (f32[8,128,512]{1,2,0:T(8,128)}, f32[8,128,512]{1,2,0:T(8,128)S(1)}, u32[]{:S(2)}) copy-start(f32[8,128,512]{1,2,0:T(8,128)S(1)} %get-tuple-element.16) | copy-start | bytes 6291460
  174.2 3.6 %copy-start.2 = (f32[8,128,512]{1,2,0:T(8,128)}, f32[8,128,512]{1,2,0:T(8,128)S(1)}, u32[]{:S(2)}) copy-start(f32[8,128,512]{1,2,0:T(8,128)S(1)} %get-tuple-element.24) | copy-start | bytes 6291460
  177.8 4.2 %copy-start.4 = (f32[8,128,512]{1,2,0:T(8,128)}, f32[8,128,512]{1,2,0:T(8,128)S(1)}, u32[]{:S(2)}) copy-start(f32[8,128,512]{1,2,0:T(8,128)S(1)} %get-tuple-element.12) | copy-start | bytes 6291460
where the time goes:
time: 203 us; the launch traced here: 202 us
  waiting for transfers between devices  78 us (38%)
  matrix products  43.7 us (22%)
  other arithmetic  26.8 us (13%)
  starting transfers between devices  25.3 us (12%)
  local copies, waits for them, and re-layouts  20.1 us (10%)
  blocking collectives  8 us (4%)
    all_to_all x1, waiting for transfers between devices, shards(): lax.all_to_all(outgoing, 'sky', split_axis=0, concat_axis=0, tiled=True)  42.2 us
    dot_general x3, matrix products, smooth(): jnp.einsum('vy,cyz->cvz', down_matrix, across, preferred_element_type=jnp...  37.8 us
    ppermute x2, waiting for transfers between devices, extended(): lax.ppermute(lax.slice_in_dim(block, block.shape[dim] - width, None, axis...  27.8 us
    reduce_sum x4, other arithmetic, kernel_boxcars(): power = jnp.stack([jnp.sum(item * item, axis=(1, 2)) for item in found])  12 us
    max x1, other arithmetic, raise_score(): best = jnp.maximum(best, jnp.abs(running) * factor[width][:, None, None])  9.23 us
    ppermute x2, starting transfers between devices, extended(): lax.ppermute(lax.slice_in_dim(block, block.shape[dim] - width, None, axis...  9.08 us
    psum x1, blocking collectives, shards(): totals = lax.psum(powers, 'sky')  8 us
    ppermute x2, waiting for transfers between devices, extended(): lax.ppermute(lax.slice_in_dim(block, 0, width, axis=dim), axis, backward)  7.8 us
  transfers between devices with their start and end apart: 7, of which 5 were waited for; matrix products, arithmetic and copies ran while one was open for 9% of the time, Pallas kernels for 0%

commit v1 on v0

v1 whole, which is shorter than its diff:
```python
import functools

import jax
import jax.numpy as jnp
import ml_dtypes
import numpy as np
from jax import lax
from jax.experimental import pallas as pl
from jax.experimental.pallas import tpu as pltpu
from jax.sharding import PartitionSpec as P

ROWB = 1
COLB = 4
RIM = 8
EDGE = 7
KERNELS = 3
WIDTHS = 4

REGULARIZER = 0.05
EPSILON = 1e-06
KERNEL_FWHM = (3.0, 6.0, 9.0)
HALF_WIDTHS = (0, 1, 3, 7)

LANES = 128
MIB = 1 << 20
F32 = jnp.float32
BF16 = jnp.bfloat16
SMEM = pl.BlockSpec(memory_space=pltpu.SMEM)
VMEM = pl.BlockSpec(memory_space=pltpu.VMEM)


def params(mib):
    return pltpu.CompilerParams(vmem_limit_bytes=mib * MIB)


def cost(flops, moved):
    return pl.CostEstimate(flops=int(flops), bytes_accessed=int(moved), transcendentals=0)


def tap_table(distance):
    offsets = np.arange(-RIM, RIM + 1).astype(np.float32)
    near = np.abs(distance) <= RIM
    index = np.clip(distance + RIM, 0, 2 * RIM)
    found = []
    for fwhm in KERNEL_FWHM:
        sigma = np.float32(fwhm / 2.3548)
        taps = np.exp(-offsets * offsets / (np.float32(2.0) * sigma * sigma)).astype(ml_dtypes.bfloat16)
        found.append(np.where(near, taps[index], np.zeros((), ml_dtypes.bfloat16)))
    return np.stack(found)


def across_matrices(broad):
    cells = np.arange(broad)
    return tap_table(cells[:, None] - cells[None, :])


def down_matrices(count, strip):
    tall = count * strip
    found = []
    for me in range(count):
        rows = [(me ^ k) * strip + np.arange(strip) for k in range(count)]
        rows += [np.arange(-RIM, 0), np.arange(tall, tall + RIM)]
        rows = np.concatenate(rows)
        found.append(tap_table(rows[None, :] - np.arange(tall)[:, None]).reshape(KERNELS * tall, tall + 2 * RIM))
    return np.stack(found)


def exchange(block, axis, k):
    count = lax.axis_size(axis)
    return lax.ppermute(block, axis, [(i, i ^ k) for i in range(count)])


def pack_kernel(me_ref, pieces_ref, beam_ref, *outs):
    channels = pieces_ref.shape[1]
    me = me_ref[0]
    for k, out in enumerate(outs):
        strip = me ^ k
        beam = beam_ref[:, strip]
        wide = beam.astype(F32)
        for c in range(channels):
            out[:, c] = (wide * pieces_ref[:, c, strip].astype(F32)).astype(BF16)
        out[:, channels] = beam


def pack(me, pieces, beam, count):
    piece_count, channels, size, _ = pieces.shape
    strip = size // count
    step = 2
    parts = pieces.reshape(piece_count, channels, count, strip, LANES)
    beams = beam.reshape(piece_count, count, strip, LANES)
    out = jax.ShapeDtypeStruct((piece_count, channels + 1, strip, LANES), BF16)
    return pl.pallas_call(
        pack_kernel,
        grid=(piece_count // step,),
        in_specs=[
            SMEM,
            pl.BlockSpec((step, channels, count, strip, LANES), lambda i: (i, 0, 0, 0, 0)),
            pl.BlockSpec((step, count, strip, LANES), lambda i: (i, 0, 0, 0)),
        ],
        out_specs=[pl.BlockSpec((step, channels + 1, strip, LANES), lambda i: (i, 0, 0, 0))] * count,
        out_shape=[out] * count,
        compiler_params=params(24),
        cost_estimate=cost(pieces.size, 4 * pieces.size),
        name="pack_pieces",
    )(me, parts, beams)


def combine_kernel(count, me_ref, owner_ref, *refs):
    parts, outs = refs[:count], refs[count : 2 * count]
    total, cover = refs[2 * count :]
    piece_count, planes, strip, _ = parts[0].shape
    channels = planes - 1
    me = me_ref[0]
    total[...] = jnp.zeros_like(total)
    cover[...] = jnp.full(cover.shape, REGULARIZER, F32)
    for k, part in enumerate(parts):
        source = me ^ k

        def add(p, _, part=part, source=source):
            block = owner_ref[source, p]
            beam = part[p, channels].astype(F32)
            cover[block] += beam * beam
            total[block] += part[p, :channels].astype(F32)
            return 0

        lax.fori_loop(0, piece_count, add, 0)
    first = me == 0
    last = me == count - 1
    for k, out in enumerate(outs):
        tile = me ^ k
        other = jnp.where(last, tile - 1, tile + 1)
        valid = jnp.logical_or(
            jnp.logical_and(last, tile > 0), jnp.logical_and(first, tile < count - 1)
        )
        other = jnp.clip(other, 0, count - 1)
        for column in range(COLB):
            lanes = slice(column * LANES, (column + 1) * LANES)
            block = tile * COLB + column
            scale = 1.0 / cover[block]
            for c in range(channels):
                out[c, :, lanes] = (total[block, c] * scale).astype(BF16)
            block = other * COLB + column
            rows = []
            for c in range(channels):
                high = total[block, c, strip - RIM :] / cover[block, strip - RIM :]
                low = total[block, c, :RIM] / cover[block, :RIM]
                rows.append(jnp.where(valid, jnp.where(last, high, low), 0.0))
            rims = jnp.concatenate(rows, axis=0)
            for e in range(channels * RIM // strip):
                out[channels + e, :, lanes] = rims[e * strip : (e + 1) * strip].astype(BF16)


def combine(me, owners, parts, count):
    piece_count, planes, strip, _ = parts[0].shape
    channels = planes - 1
    out = jax.ShapeDtypeStruct((channels + channels * RIM // strip, strip, COLB * LANES), BF16)
    blocks = count * COLB
    return pl.pallas_call(
        functools.partial(combine_kernel, count),
        in_specs=[SMEM, SMEM] + [VMEM] * count,
        out_specs=[VMEM] * count,
        out_shape=[out] * count,
        scratch_shapes=[
            pltpu.VMEM((blocks, channels, strip, LANES), F32),
            pltpu.VMEM((blocks, strip, LANES), F32),
        ],
        compiler_params=params(32),
        cost_estimate=cost(4 * count * parts[0].size, 4 * count * parts[0].size),
        name="combine_strips",
    )(me, owners, *parts)


def assemble_kernel(count, me_ref, *refs):
    parts, (full, lower, upper) = refs[:count], refs[count:]
    channels, tall, broad = full.shape
    strip = parts[0].shape[1]
    me = me_ref[0]

    def place(c, value, start):
        size = value.shape[0]
        full[c, start : start + size] = value
        if c < EDGE:
            lower[c, start : start + size] = value
        if c >= channels - EDGE:
            upper[c - (channels - EDGE), start : start + size] = value

    rims = [part[channels:].astype(F32).reshape(channels, RIM, broad) for part in parts]
    for c in range(channels):
        above = jnp.zeros((RIM, broad), F32)
        below = jnp.zeros((RIM, broad), F32)
        for k, rim in enumerate(rims):
            source = me ^ k
            above = jnp.where(source == count - 1, rim[c], above)
            below = jnp.where(source == 0, rim[c], below)
        edges = jnp.concatenate([above, below], axis=0).astype(BF16)
        if strip % 16 == 0:
            for k, part in enumerate(parts):
                place(c, part[c], k * strip)
        else:
            body = jnp.concatenate([part[c].astype(F32) for part in parts], axis=0)
            place(c, body.astype(BF16), 0)
        place(c, edges, count * strip)


def assemble(me, parts, channels, count):
    _, strip, broad = parts[0].shape
    tall = count * strip + 2 * RIM
    full = jax.ShapeDtypeStruct((channels, tall, broad), BF16)
    side = jax.ShapeDtypeStruct((EDGE, tall, broad), BF16)
    return pl.pallas_call(
        functools.partial(assemble_kernel, count),
        in_specs=[SMEM] + [VMEM] * count,
        out_specs=[VMEM] * 3,
        out_shape=[full, side, side],
        compiler_params=params(24),
        cost_estimate=cost(full.size, 8 * full.size),
        name="assemble_tile",
    )(me, *parts)


def smooth_planes(source, down, across, middle, write):
    planes, _, broad = source.shape
    tall = down.shape[0] // KERNELS

    def rows(c, _):
        found = jnp.dot(down[...], source[c], preferred_element_type=F32).astype(BF16)
        for k in range(KERNELS):
            middle[k, c] = found[k * tall : (k + 1) * tall]
        return 0

    def columns(c, _):
        for k in range(KERNELS):
            write(k, c, jnp.dot(middle[k, c], across[k], preferred_element_type=F32).astype(BF16))
        return 0

    lax.fori_loop(0, planes, rows, 0)
    lax.fori_loop(0, planes, columns, 0)


def smooth_kernel(source, down, across, out, middle):
    def write(k, c, value):
        out[k, c] = value

    smooth_planes(source, down, across, middle, write)


def smooth(source, down, across):
    planes, _, broad = source.shape
    tall = down.shape[0] // KERNELS
    out = jax.ShapeDtypeStruct((KERNELS, planes, tall, broad), BF16)
    return pl.pallas_call(
        smooth_kernel,
        in_specs=[VMEM] * 3,
        out_specs=VMEM,
        out_shape=out,
        scratch_shapes=[pltpu.VMEM((KERNELS, planes, tall, broad), BF16)],
        compiler_params=params(32),
        cost_estimate=cost(2 * out.size * (broad + 256), 4 * out.size),
        name="smooth_own",
    )(source, down, across)


def boxcars(layers):
    channels = len(layers) - 2 * EDGE

    @functools.cache
    def run(length, i):
        if length == 1:
            return layers[i]
        half = length // 2
        return run(half, i) + run(half, i + half)

    @functools.cache
    def box(half, i):
        if half == 0:
            return layers[i]
        return run(half + 1, i - half) + box(half // 2, i + (half + 1) // 2)

    return [[box(half, c + EDGE) for c in range(channels)] for half in HALF_WIDTHS]


def load_layers(own, halo, k, rows, lanes):
    channels = own.shape[1]
    refs = [(halo, c) for c in range(EDGE)]
    refs += [(own, c) for c in range(channels)]
    refs += [(halo, c) for c in range(EDGE, 2 * EDGE)]
    return [ref[k, c, rows, lanes].astype(F32).reshape(-1, 8, LANES) for ref, c in refs]


def power_kernel(low, high, own, down, across, halo, power, middle, sums):
    tall, broad = own.shape[2:]
    channels = own.shape[1]
    for side, start in ((low, 0), (high, EDGE)):

        def write(k, c, value, start=start):
            halo[k, start + c] = value

        smooth_planes(side, down, across, middle, write)
    sums[...] = jnp.zeros_like(sums)
    groups = broad // LANES

    def add(step, _):
        rows = pl.ds(pl.multiple_of(step // groups * 16, 16), 16)
        lanes = pl.ds(pl.multiple_of(step % groups * LANES, LANES), LANES)
        for k in range(KERNELS):
            found = boxcars(load_layers(own, halo, k, rows, lanes))
            for w in range(WIDTHS):
                for c in range(channels):
                    square = found[w][c] * found[w][c]
                    sums[(k * WIDTHS + w) * channels + c] += jnp.sum(square, axis=0)
        return 0

    lax.fori_loop(0, tall // 16 * groups, add, 0)
    total = jnp.sum(jnp.sum(sums[...], axis=1), axis=1, keepdims=True)
    power[...] = jnp.broadcast_to(total, power.shape)


def smooth_halo_power(low, high, own, down, across):
    _, channels, tall, broad = own.shape
    pairs = KERNELS * WIDTHS * channels
    halo = jax.ShapeDtypeStruct((KERNELS, 2 * EDGE, tall, broad), BF16)
    return pl.pallas_call(
        power_kernel,
        in_specs=[VMEM] * 5,
        out_specs=[VMEM] * 2,
        out_shape=[halo, jax.ShapeDtypeStruct((pairs, LANES), F32)],
        scratch_shapes=[
            pltpu.VMEM((KERNELS, EDGE, tall, broad), BF16),
            pltpu.VMEM((pairs, 8, LANES), F32),
        ],
        compiler_params=params(48),
        cost_estimate=cost(2 * halo.size * (broad + 256), 8 * halo.size),
        name="smooth_halo_power",
    )(low, high, own, down, across)


def score_kernel(count, cells, own, halo, clips, *refs):
    powers, (out, factor) = refs[:count], refs[count:]
    channels, tall, broad = out.shape

    @pl.when(pl.program_id(0) == 0)
    def _():
        total = powers[0][...]
        for item in powers[1:]:
            total = total + item[...]
        scale = 10.0 / (clips[...] * jnp.sqrt(total / cells + EPSILON))
        factor[...] = jnp.broadcast_to(scale[:, None], factor.shape)

    groups = broad // LANES

    def score(step, _):
        rows = pl.ds(pl.multiple_of(step // groups * 16, 16), 16)
        lanes = pl.ds(pl.multiple_of(step % groups * LANES, LANES), LANES)
        best = [None] * channels
        for k in range(KERNELS):
            found = boxcars(load_layers(own, halo, k, rows, lanes))
            for w in range(WIDTHS):
                for c in range(channels):
                    value = jnp.abs(found[w][c]) * factor[(k * WIDTHS + w) * channels + c]
                    best[c] = value if best[c] is None else jnp.maximum(best[c], value)
        for c in range(channels):
            out[c, rows, lanes] = best[c].reshape(16, LANES)
        return 0

    lax.fori_loop(0, tall // 16 * groups, score, 0)


def score(own, halo, clips, powers, cells):
    _, channels, tall, broad = own.shape
    pairs = KERNELS * WIDTHS * channels
    count = len(powers)
    step = 32
    return pl.pallas_call(
        functools.partial(score_kernel, count, cells),
        grid=(tall // step,),
        in_specs=[
            pl.BlockSpec((KERNELS, channels, step, broad), lambda i: (0, 0, i, 0)),
            pl.BlockSpec((KERNELS, 2 * EDGE, step, broad), lambda i: (0, 0, i, 0)),
        ]
        + [pl.BlockSpec((pairs, LANES), lambda i: (0, 0))] * (1 + count),
        out_specs=pl.BlockSpec((channels, step, broad), lambda i: (0, i, 0)),
        out_shape=jax.ShapeDtypeStruct((channels, tall, broad), F32),
        scratch_shapes=[pltpu.VMEM((pairs, 8, LANES), F32)],
        compiler_params=params(40),
        cost_estimate=cost(40 * KERNELS * own.size, 8 * own.size),
        name="score_cells",
    )(own, halo, clips, *powers)


def shards(across_table, down_table, pieces, beam, destination, clip_tenths):
    count = lax.axis_size("sky")
    links = lax.axis_size("freq")
    channels = pieces.shape[1]
    me = lax.axis_index("sky")
    place = me.astype(jnp.int32).reshape(1)
    owners = lax.all_gather(destination, "sky")
    packed = pack(place, pieces, beam, count)
    arrived = [packed[0]] + [exchange(packed[k], "sky", k) for k in range(1, count)]
    strips = combine(place, owners, arrived, count)
    tiles = [strips[0]] + [exchange(strips[k], "sky", k) for k in range(1, count)]
    full, lower, upper = assemble(place, tiles, channels, count)
    low = lax.ppermute(upper, "freq", [(i, i + 1) for i in range(links - 1)])
    high = lax.ppermute(lower, "freq", [(i + 1, i) for i in range(links - 1)])
    across = jnp.asarray(across_table)
    down = lax.dynamic_index_in_dim(jnp.asarray(down_table), me, 0, keepdims=False)
    own = smooth(full, down, across)
    halo, power = smooth_halo_power(low, high, own, down, across)
    powers = [power] + [exchange(power, "sky", k) for k in range(1, count)]
    clips = jnp.repeat(clip_tenths.astype(F32).reshape(-1), channels)
    clips = jnp.broadcast_to(clips[:, None], power.shape)
    cells = float(count * ROWB * LANES * COLB * LANES)
    return score(own, halo, clips, powers, cells)


def solution(mesh):
    count = mesh.shape["sky"]
    body = functools.partial(
        shards, across_matrices(COLB * LANES), down_matrices(count, ROWB * LANES // count)
    )
    return jax.shard_map(
        body,
        mesh=mesh,
        in_specs=(P("sky", "freq", None, None), P("sky", None, None), P("sky"), P()),
        out_specs=P("freq", "sky", None),
        check_vma=False,
    )
```

time: 203 us -> 109 us (0.54)
  waiting for transfers between devices: 78 us -> 18 us
  matrix products: 43.7 us -> 0 us
  Pallas kernels: 0 us -> 35 us
  other arithmetic: 26.8 us -> 0.01 us
  blocking collectives: 8 us -> 25.3 us
  starting transfers between devices: 25.3 us -> 17 us
  local copies, waits for them, and re-layouts: 20.1 us -> 12.7 us
    dot_general x5 -> x0, matrix products: 43.7 us -> none  [the longest x3 37.8 us: smooth(): jnp.einsum('vy,cyz->cvz', down_matrix, across, preferred_element_type=jnp...]
    all_to_all x3 -> x0, waiting for transfers between devices: 42.4 us -> none  [the longest x1 42.2 us: shards(): lax.all_to_all(outgoing, 'sky', split_axis=0, concat_axis=0, tiled=True)]
    pallas_call x0 -> x6, Pallas kernels: none -> 35 us  [the longest x1 18 us: smooth_halo_power(): pl.pallas_call(power_kernel, in_specs=[VMEM] * 5, out_specs=[VMEM] * 2, o...]
    unnamed x0 -> x1, blocking collectives: none -> 25.3 us
    ppermute x4 -> x11, waiting for transfers between devices: 35.6 us -> 18 us  [the longest x9 13.9 us: exchange(): return lax.ppermute(block, axis, [(i, i ^ k) for i in range(count)])]
    all_to_all x3 -> x0, starting transfers between devices: 12.6 us -> none  [the longest x1 4.86 us: shards(): lax.all_to_all(outgoing, 'sky', split_axis=0, concat_axis=0, tiled=True)]
    reduce_sum x5 -> x0, other arithmetic: 12.2 us -> none  [the longest x4 12 us: kernel_boxcars(): power = jnp.stack([jnp.sum(item * item, axis=(1, 2)) for item in found])]
    unnamed x18 -> x27, local copies, waits for them, and re-layouts: 0.13 us -> 11.3 us
  transfers between devices with their start and end apart: 7 -> 11, of which waited for: 5 -> 7; matrix products, arithmetic and copies ran while one was open for 9% -> 2% of each run, Pallas kernels for 0% -> 5%
where the time goes in v1:
time: 109 us
  Pallas kernels  35 us (32%)
  blocking collectives  25.3 us (23%)
  waiting for transfers between devices  18 us (17%)
  starting transfers between devices  17 us (16%)
  local copies, waits for them, and re-layouts  12.7 us (12%)
    unnamed x1, blocking collectives  25.3 us
    pallas_call x1, Pallas kernels, smooth_halo_power(): pl.pallas_call(power_kernel, in_specs=[VMEM] * 5, out_specs=[VMEM] * 2, o...  18 us
    ppermute x9, waiting for transfers between devices, exchange(): return lax.ppermute(block, axis, [(i, i ^ k) for i in range(count)])  13.9 us
    unnamed x27, local copies, waits for them, and re-layouts  11.3 us
    ppermute x9, starting transfers between devices, exchange(): return lax.ppermute(block, axis, [(i, i ^ k) for i in range(count)])  8.64 us
    pallas_call x1, Pallas kernels, score(): pl.pallas_call(functools.partial(score_kernel, count, cells), grid=(tall...  7.76 us
    ppermute x1, starting transfers between devices, shards(): low = lax.ppermute(upper, 'freq', [(i, i + 1) for i in range(links - 1)])  6.41 us
    pallas_call x1, Pallas kernels, smooth(): pl.pallas_call(smooth_kernel, in_specs=[VMEM] * 3, out_specs=VMEM, out_sh...  4.99 us
  transfers between devices with their start and end apart: 11, of which 7 were waited for; matrix products, arithmetic and copies ran while one was open for 2% of the time, Pallas kernels for 5%

profile of v1, /device:TPU:1, one launch (start us, length us, event | category | flops | bytes accessed | tf_op | source)
XLA Modules:
  0.0 108.8 jit_solution(6354229202487864722)
XLA Ops:
  0.0 1.6 %copy-done.3 = bf16[8,8,128,128]{3,2,1,0:T(8,128)(2,1)S(1)} copy-done((bf16[8,8,128,128]{3,2,1,0:T(8,128)(2,1)S(1)}, bf16[8,8,128,128]{3,2,1,0:T(8,128)(2,1)}, u32[]{:S(2)}) %copy-start.3) | copy-done | bytes 2097176
  1.6 0.9 copy-done.4
  2.6 1.5 %pack_pieces.1 = (bf16[8,9,32,128]{3,2,1,0:T(8,128)(2,1)S(1)}, bf16[8,9,32,128]{3,2,1,0:T(8,128)(2,1)}, bf16[8,9,32,128]{3,2,1,0:T(8,128)(2,1)S(1)}, bf16[8,9,32,128]{3,2,1,0:T(8,128)(2,1)S(1)}) custom-call(s32[1]{0:T(128)} %bitcast.me_ref, bf16[8,8,4,32,128]{4,3,2,1,0:T(8,128)(2,1)S(1)} %bitcast.6, bf16[8,4,32,128]{3,2,1,0:T(8,128)(2,1)S(1)} %bitcast.7), custom_call_target="tpu_custom_call" | custom-call | flops 1048576 | bytes 4194304 | tf_op jit(solution)/shard_map/pack_pieces/pallas_call | solution.py:92
  4.1 2.0 %collective-permute-start = (bf16[8,9,32,128]{3,2,1,0:T(8,128)(2,1)}, bf16[8,9,32,128]{3,2,1,0:T(8,128)(2,1)S(1)}, u32[]{:S(2)}, u32[]{:S(2)}) collective-permute-start(bf16[8,9,32,128]{3,2,1,0:T(8,128)(2,1)} %get-tuple-element.19), channel_id=1, source_target_pairs={{0,8},{8,0},{16,24},{24,16},{1,9},{9,1},{17,25},{25,17},{2,10},{10... | collective-permute-start | bytes 1769480 | tf_op jit(solution)/shard_map/ppermute | solution.py:70
  6.1 1.2 %collective-permute-start.1 = (bf16[8,9,32,128]{3,2,1,0:T(8,128)(2,1)S(1)}, bf16[8,9,32,128]{3,2,1,0:T(8,128)(2,1)S(1)}, u32[]{:S(2)}, u32[]{:S(2)}) collective-permute-start(bf16[8,9,32,128]{3,2,1,0:T(8,128)(2,1)S(1)} %get-tuple-element.20), channel_id=1, source_target_pairs={{0,16},{8,24},{16,0},{24,8},{1,17},{9,25},{17,1},{25,9},{2,18},{10... | collective-permute-start | bytes 1769480 | tf_op jit(solution)/shard_map/ppermute | solution.py:70
  7.4 0.0 collective-permute-start.2
  7.4 0.0 copy-done.11
  7.4 0.7 dynamic-slice
  8.7 0.0 copy-done.10
  8.7 0.2 dynamic-update-slice
  9.0 25.3 %all-reduce = s32[32]{0:T(128)S(1)} all-reduce(s32[32]{0:T(128)S(1)} %dynamic-update-slice), channel_id=2, replica_groups=mesh['sky'=4,'freq'=8] {'sky'}, use_global_device_ids=true, to_apply=%add | all-reduce | flops 32 | bytes 256
  34.3 0.1 reshape.17.owner_ref
  34.4 0.0 collective-permute-done.refs_1_
  34.4 0.0 collective-permute-done.1.refs_2_
  34.4 0.0 collective-permute-done.2.refs_3_
  34.4 1.6 %combine_strips.1 = (bf16[10,32,512]{2,1,0:T(8,128)(2,1)S(1)}, bf16[10,32,512]{2,1,0:T(8,128)(2,1)S(1)}, bf16[10,32,512]{2,1,0:T(8,128)(2,1)S(1)}, bf16[10,32,512]{2,1,0:T(8,128)(2,1)S(1)}) custom-call(s32[1]{0:T(128)} %bitcast.me_ref, s32[4,8]{1,0:T(4,128)S(1)} %reshape.17.owner_ref, bf16[8,9,32,128]{3,2,1,0:T(8,128)(2,1)S(1)} %get-tuple-element.18.refs_0_, ...), custom_call_target="tpu_custom_call" | custom-call | flops 4718592 | bytes 4718592 | tf_op jit(solution)/shard_map/combine_strips/pallas_call | solution.py:158
  36.0 1.3 %collective-permute-start.3 = (bf16[10,32,512]{2,1,0:T(8,128)(2,1)S(1)}, bf16[10,32,512]{2,1,0:T(8,128)(2,1)S(1)}, u32[]{:S(2)}, u32[]{:S(2)}) collective-permute-start(bf16[10,32,512]{2,1,0:T(8,128)(2,1)S(1)} %get-tuple-element.23), channel_id=1, source_target_pairs={{0,8},{8,0},{16,24},{24,16},{1,9},{9,1},{17,25},{25,17},{2,10},{10... | collective-permute-start | bytes 983048 | tf_op jit(solution)/shard_map/ppermute | solution.py:70
  37.2 0.3 collective-permute-start.4
  37.5 1.2 %collective-permute-start.5 = (bf16[10,32,512]{2,1,0:T(8,128)(2,1)S(1)}, bf16[10,32,512]{2,1,0:T(8,128)(2,1)S(1)}, u32[]{:S(2)}, u32[]{:S(2)}) collective-permute-start(bf16[10,32,512]{2,1,0:T(8,128)(2,1)S(1)} %get-tuple-element.25), channel_id=1, source_target_pairs={{0,24},{8,16},{16,8},{24,0},{1,25},{9,17},{17,9},{25,1},{2,26},{10... | collective-permute-start | bytes 983048 | tf_op jit(solution)/shard_map/ppermute | solution.py:70
  38.7 4.1 %collective-permute-done.3.refs_1_ = bf16[10,32,512]{2,1,0:T(8,128)(2,1)S(1)} collective-permute-done((bf16[10,32,512]{2,1,0:T(8,128)(2,1)S(1)}, bf16[10,32,512]{2,1,0:T(8,128)(2,1)S(1)}, u32[]{:S(2)}, u32[]{:S(2)}) %collective-permute-start.3) | collective-permute-done | bytes 327712 | tf_op jit(solution)/shard_map/ppermute | solution.py:70
  42.8 0.9 collective-permute-done.4.refs_2_
  43.7 7.3 %collective-permute-done.5.refs_3_ = bf16[10,32,512]{2,1,0:T(8,128)(2,1)S(1)} collective-permute-done((bf16[10,32,512]{2,1,0:T(8,128)(2,1)S(1)}, bf16[10,32,512]{2,1,0:T(8,128)(2,1)S(1)}, u32[]{:S(2)}, u32[]{:S(2)}) %collective-permute-start.5) | collective-permute-done | bytes 327712 | tf_op jit(solution)/shard_map/ppermute | solution.py:70
  51.1 1.2 %assemble_tile.1 = (bf16[8,144,512]{2,1,0:T(8,128)(2,1)S(1)}, bf16[7,144,512]{2,1,0:T(8,128)(2,1)S(1)}, bf16[7,144,512]{2,1,0:T(8,128)(2,1)}) custom-call(s32[1]{0:T(128)} %bitcast.me_ref, bf16[10,32,512]{2,1,0:T(8,128)(2,1)S(1)} %get-tuple-element.22.refs_0_, bf16[10,32,512]{2,1,0:T(8,128)(2,1)S(1)} %collective-permute-done.3.refs_1_, ...), custom_call_target="tpu_custom_call" | custom-call | flops 589824 | bytes 4718592 | tf_op jit(solution)/shard_map/assemble_tile/pallas_call | solution.py:210
  52.2 6.4 %collective-permute-start.6 = (bf16[7,144,512]{2,1,0:T(8,128)(2,1)}, bf16[7,144,512]{2,1,0:T(8,128)(2,1)S(1)}, u32[]{:S(2)}, u32[]{:S(2)}) collective-permute-start(bf16[7,144,512]{2,1,0:T(8,128)(2,1)} %get-tuple-element.27), channel_id=1, source_target_pairs={{0,1},{1,2},{2,3},{3,4},{4,5},{5,6},{6,7},{8,9},{9,10},{10,11},{11... | collective-permute-start | bytes 3096584 | tf_op jit(solution)/shard_map/ppermute | solution.py:402
  58.6 1.9 %collective-permute-start.7 = (bf16[7,144,512]{2,1,0:T(8,128)(2,1)S(1)}, bf16[7,144,512]{2,1,0:T(8,128)(2,1)}, u32[]{:S(2)}, u32[]{:S(2)}) collective-permute-start(bf16[7,144,512]{2,1,0:T(8,128)(2,1)S(1)} %get-tuple-element.28), channel_id=1, source_target_pairs={{1,0},{2,1},{3,2},{4,3},{5,4},{6,5},{7,6},{9,8},{10,9},{11,10},{12... | collective-permute-start | bytes 3096584 | tf_op jit(solution)/shard_map/ppermute | solution.py:403
  60.6 0.9 dynamic-slice_bitcast_fusion.down
  61.5 0.0 copy-start.7
  61.5 1.4 %copy-done.7 = bf16[3,512,512]{2,1,0:T(8,128)(2,1)S(1)} copy-done((bf16[3,512,512]{2,1,0:T(8,128)(2,1)S(1)}, bf16[3,512,512]{2,1,0:T(8,128)(2,1)}, u32[]{:S(2)}) %copy-start.7) | copy-done | bytes 1572888
  62.9 5.0 %smooth_own.1.own = bf16[3,8,128,512]{3,2,1,0:T(8,128)(2,1)S(1)} custom-call(bf16[8,144,512]{2,1,0:T(8,128)(2,1)S(1)} %get-tuple-element.26.source, bf16[384,144]{1,0:T(8,128)(2,1)S(1)} %dynamic-slice_bitcast_fusion.down, bf16[3,512,512]{2,1,0:T(8,128)(2,1)S(1)} %copy-done.7), custom_call_target="tpu_custom_call" | custom-call | flops 2415919104 | bytes 6291456 | tf_op jit(solution)/shard_map/smooth_own/pallas_call | solution.py:251
  67.9 0.0 copy-start.1
  67.9 1.7 %copy-done.1 = bf16[3,8,128,512]{3,2,1,0:T(8,128)(2,1)} copy-done((bf16[3,8,128,512]{3,2,1,0:T(8,128)(2,1)}, bf16[3,8,128,512]{3,2,1,0:T(8,128)(2,1)S(1)}, u32[]{:S(2)}) %copy-start.1) | copy-done | bytes 3145752
  69.6 0.9 collective-permute-done.6.low
  70.5 1.0 copy-done.5
  71.5 3.2 %collective-permute-done.7.high = bf16[7,144,512]{2,1,0:T(8,128)(2,1)} collective-permute-done((bf16[7,144,512]{2,1,0:T(8,128)(2,1)S(1)}, bf16[7,144,512]{2,1,0:T(8,128)(2,1)}, u32[]{:S(2)}, u32[]{:S(2)}) %collective-permute-start.7) | collective-permute-done | bytes 1032224 | tf_op jit(solution)/shard_map/ppermute | solution.py:403
  74.7 1.2 %copy-done.6 = bf16[7,144,512]{2,1,0:T(8,128)(2,1)S(1)} copy-done((bf16[7,144,512]{2,1,0:T(8,128)(2,1)S(1)}, bf16[7,144,512]{2,1,0:T(8,128)(2,1)}, u32[]{:S(2)}) %copy-start.6) | copy-done | bytes 1032216
  75.9 18.0 %smooth_halo_power.1 = (bf16[3,14,128,512]{3,2,1,0:T(8,128)(2,1)}, f32[96,128]{1,0:T(8,128)S(1)}) custom-call(bf16[7,144,512]{2,1,0:T(8,128)(2,1)S(1)} %copy-done.6, bf16[7,144,512]{2,1,0:T(8,128)(2,1)} %collective-permute-done.7.high, bf16[3,8,128,512]{3,2,1,0:T(8,128)(2,1)} %copy-done.1, bf16[384,144]{1,0:T(8,128)(2,1)S(1)} %dynamic-slice_bitcast_fusion.down, ...), custom_call_target="tpu_custom_call" | custom-call | flops 4227858432 | bytes 22020096 | tf_op jit(solution)/shard_map/smooth_halo_power/pallas_call | solution.py:322
  94.0 0.9 collective-permute-start.10
  94.8 0.6 collective-permute-start.8
  95.4 1.2 %collective-permute-start.9 = (f32[96,128]{1,0:T(8,128)S(1)}, f32[96,128]{1,0:T(8,128)S(1)}, u32[]{:S(2)}, u32[]{:S(2)}) collective-permute-start(f32[96,128]{1,0:T(8,128)S(1)} %get-tuple-element.30.refs_0_), channel_id=1, source_target_pairs={{0,16},{8,24},{16,0},{24,8},{1,17},{9,25},{17,1},{25,9},{2,18},{10... | collective-permute-start | bytes 147464 | tf_op jit(solution)/shard_map/ppermute | solution.py:70
  96.6 0.1 reshape.16
  96.7 0.1 broadcast_in_dim.10
  96.8 0.1 broadcast_in_dim.11
  96.9 0.9 collective-permute-done.10.refs_3_
  97.8 0.0 collective-permute-done.8.refs_1_
  97.8 0.5 collective-permute-done.9.refs_2_
  98.3 0.1 broadcast_in_dim.12.clips
  98.4 2.6 %copy-done = bf16[3,14,128,512]{3,2,1,0:T(8,128)(2,1)S(1)} copy-done((bf16[3,14,128,512]{3,2,1,0:T(8,128)(2,1)S(1)}, bf16[3,14,128,512]{3,2,1,0:T(8,128)(2,1)}, u32[]{:S(2)}) %copy-start) | copy-done | bytes 5505048
  101.0 7.8 %score_cells.1 = f32[8,128,512]{2,1,0:T(8,128)} custom-call(bf16[3,8,128,512]{3,2,1,0:T(8,128)(2,1)S(1)} %copy-done.2, bf16[3,14,128,512]{3,2,1,0:T(8,128)(2,1)S(1)} %copy-done, f32[96,128]{1,0:T(8,128)S(1)} %broadcast_in_dim.12.clips, f32[96,128]{1,0:T(8,128)S(1)} %get-tuple-element.30.refs_0_, f32[96,128]{1,0:T(8,128)S(1)} %collective-permute-done.8.refs_1_, ...), custom_call_target="tpu_custom_call" | custom-call | flops 188743680 | bytes 12582912 | tf_op jit(solution)/shard_map/score_cells/pallas_call | solution.py:373
  (15 shorter events, 0.0 us)
Async XLA Ops:
  0.0 7.4 %copy-start.11 = (u32[32]{0:T(128)S(1)}, u32[32]{0:T(128)}, u32[]{:S(2)}) copy-start(u32[32]{0:T(128)} %constant.19) | copy-start | bytes 388
  0.0 8.7 %copy-start.10 = (s32[8]{0:T(128)S(1)}, s32[8]{0:T(128)}, u32[]{:S(2)}) copy-start(s32[8]{0:T(128)} %param.8) | copy-start | bytes 100
  0.0 1.6 %copy-start.3 = (bf16[8,8,128,128]{3,2,1,0:T(8,128)(2,1)S(1)}, bf16[8,8,128,128]{3,2,1,0:T(8,128)(2,1)}, u32[]{:S(2)}) copy-start(bf16[8,8,128,128]{3,2,1,0:T(8,128)(2,1)} %param.6) | copy-start | bytes 6291460
  1.6 0.9 copy-start.4
  4.1 30.3 %collective-permute-start = (bf16[8,9,32,128]{3,2,1,0:T(8,128)(2,1)}, bf16[8,9,32,128]{3,2,1,0:T(8,128)(2,1)S(1)}, u32[]{:S(2)}, u32[]{:S(2)}) collective-permute-start(bf16[8,9,32,128]{3,2,1,0:T(8,128)(2,1)} %get-tuple-element.19), channel_id=1, source_target_pairs={{0,8},{8,0},{16,24},{24,16},{1,9},{9,1},{17,25},{25,17},{2,10},{10... | collective-permute-start | bytes 1769480 | tf_op jit(solution)/shard_map/ppermute | solution.py:70
  6.1 28.3 %collective-permute-start.1 = (bf16[8,9,32,128]{3,2,1,0:T(8,128)(2,1)S(1)}, bf16[8,9,32,128]{3,2,1,0:T(8,128)(2,1)S(1)}, u32[]{:S(2)}, u32[]{:S(2)}) collective-permute-start(bf16[8,9,32,128]{3,2,1,0:T(8,128)(2,1)S(1)} %get-tuple-element.20), channel_id=1, source_target_pairs={{0,16},{8,24},{16,0},{24,8},{1,17},{9,25},{17,1},{25,9},{2,18},{10... | collective-permute-start | bytes 1769480 | tf_op jit(solution)/shard_map/ppermute | solution.py:70
  7.4 27.0 %collective-permute-start.2 = (bf16[8,9,32,128]{3,2,1,0:T(8,128)(2,1)S(1)}, bf16[8,9,32,128]{3,2,1,0:T(8,128)(2,1)S(1)}, u32[]{:S(2)}, u32[]{:S(2)}) collective-permute-start(bf16[8,9,32,128]{3,2,1,0:T(8,128)(2,1)S(1)} %get-tuple-element.21), channel_id=1, source_target_pairs={{0,24},{8,16},{16,8},{24,0},{1,25},{9,17},{17,9},{25,1},{2,26},{10... | collective-permute-start | bytes 1769480 | tf_op jit(solution)/shard_map/ppermute | solution.py:70
  36.0 6.8 %collective-permute-start.3 = (bf16[10,32,512]{2,1,0:T(8,128)(2,1)S(1)}, bf16[10,32,512]{2,1,0:T(8,128)(2,1)S(1)}, u32[]{:S(2)}, u32[]{:S(2)}) collective-permute-start(bf16[10,32,512]{2,1,0:T(8,128)(2,1)S(1)} %get-tuple-element.23), channel_id=1, source_target_pairs={{0,8},{8,0},{16,24},{24,16},{1,9},{9,1},{17,25},{25,17},{2,10},{10... | collective-permute-start | bytes 983048 | tf_op jit(solution)/shard_map/ppermute | solution.py:70
  37.2 6.5 %collective-permute-start.4 = (bf16[10,32,512]{2,1,0:T(8,128)(2,1)S(1)}, bf16[10,32,512]{2,1,0:T(8,128)(2,1)S(1)}, u32[]{:S(2)}, u32[]{:S(2)}) collective-permute-start(bf16[10,32,512]{2,1,0:T(8,128)(2,1)S(1)} %get-tuple-element.24), channel_id=1, source_target_pairs={{0,16},{8,24},{16,0},{24,8},{1,17},{9,25},{17,1},{25,9},{2,18},{10... | collective-permute-start | bytes 983048 | tf_op jit(solution)/shard_map/ppermute | solution.py:70
  37.5 13.5 %collective-permute-start.5 = (bf16[10,32,512]{2,1,0:T(8,128)(2,1)S(1)}, bf16[10,32,512]{2,1,0:T(8,128)(2,1)S(1)}, u32[]{:S(2)}, u32[]{:S(2)}) collective-permute-start(bf16[10,32,512]{2,1,0:T(8,128)(2,1)S(1)} %get-tuple-element.25), channel_id=1, source_target_pairs={{0,24},{8,16},{16,8},{24,0},{1,25},{9,17},{17,9},{25,1},{2,26},{10... | collective-permute-start | bytes 983048 | tf_op jit(solution)/shard_map/ppermute | solution.py:70
  52.2 18.3 %collective-permute-start.6 = (bf16[7,144,512]{2,1,0:T(8,128)(2,1)}, bf16[7,144,512]{2,1,0:T(8,128)(2,1)S(1)}, u32[]{:S(2)}, u32[]{:S(2)}) collective-permute-start(bf16[7,144,512]{2,1,0:T(8,128)(2,1)} %get-tuple-element.27), channel_id=1, source_target_pairs={{0,1},{1,2},{2,3},{3,4},{4,5},{5,6},{6,7},{8,9},{9,10},{10,11},{11... | collective-permute-start | bytes 3096584 | tf_op jit(solution)/shard_map/ppermute | solution.py:402
  58.6 16.0 %collective-permute-start.7 = (bf16[7,144,512]{2,1,0:T(8,128)(2,1)S(1)}, bf16[7,144,512]{2,1,0:T(8,128)(2,1)}, u32[]{:S(2)}, u32[]{:S(2)}) collective-permute-start(bf16[7,144,512]{2,1,0:T(8,128)(2,1)S(1)} %get-tuple-element.28), channel_id=1, source_target_pairs={{1,0},{2,1},{3,2},{4,3},{5,4},{6,5},{7,6},{9,8},{10,9},{11,10},{12... | collective-permute-start | bytes 3096584 | tf_op jit(solution)/shard_map/ppermute | solution.py:403
  61.5 1.4 %copy-start.7 = (bf16[3,512,512]{2,1,0:T(8,128)(2,1)S(1)}, bf16[3,512,512]{2,1,0:T(8,128)(2,1)}, u32[]{:S(2)}) copy-start(bf16[3,512,512]{2,1,0:T(8,128)(2,1)} %constant.15.clone.across) | copy-start | bytes 4718596
  62.9 11.8 %copy-start.8 = (bf16[3,512,512]{2,1,0:T(8,128)(2,1)S(1)}, bf16[3,512,512]{2,1,0:T(8,128)(2,1)}, u32[]{:S(2)}) copy-start(bf16[3,512,512]{2,1,0:T(8,128)(2,1)} %constant.15.clone.across) | copy-start | bytes 4718596
  62.9 33.7 %copy-start.9 = (s32[3,4]{1,0:T(4,128)S(1)}, s32[3,4]{1,0:T(4,128)}, u32[]{:S(2)}) copy-start(s32[3,4]{1,0:T(4,128)} %param.9) | copy-start | bytes 148
  67.9 1.7 %copy-start.1 = (bf16[3,8,128,512]{3,2,1,0:T(8,128)(2,1)}, bf16[3,8,128,512]{3,2,1,0:T(8,128)(2,1)S(1)}, u32[]{:S(2)}) copy-start(bf16[3,8,128,512]{3,2,1,0:T(8,128)(2,1)S(1)} %smooth_own.1.own) | copy-start | bytes 9437188
  70.5 1.0 copy-start.5
  74.7 1.2 %copy-start.6 = (bf16[7,144,512]{2,1,0:T(8,128)(2,1)S(1)}, bf16[7,144,512]{2,1,0:T(8,128)(2,1)}, u32[]{:S(2)}) copy-start(bf16[7,144,512]{2,1,0:T(8,128)(2,1)} %copy-done.5) | copy-start | bytes 3096580
  75.9 22.5 %copy-start.2 = (bf16[3,8,128,512]{3,2,1,0:T(8,128)(2,1)S(1)}, bf16[3,8,128,512]{3,2,1,0:T(8,128)(2,1)}, u32[]{:S(2)}) copy-start(bf16[3,8,128,512]{3,2,1,0:T(8,128)(2,1)} %copy-done.1) | copy-start | bytes 9437188
  94.0 3.8 %collective-permute-start.10 = (f32[96,128]{1,0:T(8,128)S(1)}, f32[96,128]{1,0:T(8,128)S(1)}, u32[]{:S(2)}, u32[]{:S(2)}) collective-permute-start(f32[96,128]{1,0:T(8,128)S(1)} %get-tuple-element.30.refs_0_), channel_id=1, source_target_pairs={{0,24},{8,16},{16,8},{24,0},{1,25},{9,17},{17,9},{25,1},{2,26},{10... | collective-permute-start | bytes 147464 | tf_op jit(solution)/shard_map/ppermute | solution.py:70
  94.8 3.0 %collective-permute-start.8 = (f32[96,128]{1,0:T(8,128)S(1)}, f32[96,128]{1,0:T(8,128)S(1)}, u32[]{:S(2)}, u32[]{:S(2)}) collective-permute-start(f32[96,128]{1,0:T(8,128)S(1)} %get-tuple-element.30.refs_0_), channel_id=1, source_target_pairs={{0,8},{8,0},{16,24},{24,16},{1,9},{9,1},{17,25},{25,17},{2,10},{10... | collective-permute-start | bytes 147464 | tf_op jit(solution)/shard_map/ppermute | solution.py:70
  95.4 2.9 %collective-permute-start.9 = (f32[96,128]{1,0:T(8,128)S(1)}, f32[96,128]{1,0:T(8,128)S(1)}, u32[]{:S(2)}, u32[]{:S(2)}) collective-permute-start(f32[96,128]{1,0:T(8,128)S(1)} %get-tuple-element.30.refs_0_), channel_id=1, source_target_pairs={{0,16},{8,24},{16,0},{24,8},{1,17},{9,25},{17,1},{25,9},{2,18},{10... | collective-permute-start | bytes 147464 | tf_op jit(solution)/shard_map/ppermute | solution.py:70
  98.4 2.6 %copy-start = (bf16[3,14,128,512]{3,2,1,0:T(8,128)(2,1)S(1)}, bf16[3,14,128,512]{3,2,1,0:T(8,128)(2,1)}, u32[]{:S(2)}) copy-start(bf16[3,14,128,512]{3,2,1,0:T(8,128)(2,1)} %get-tuple-element.29.halo) | copy-start | bytes 16515076

commit v2 on v1

v2 whole, which is shorter than its diff:
```python
import functools

import jax
import jax.numpy as jnp
import ml_dtypes
import numpy as np
from jax import lax
from jax.experimental import pallas as pl
from jax.experimental.pallas import tpu as pltpu
from jax.sharding import PartitionSpec as P

ROWB = 1
COLB = 4
RIM = 8
EDGE = 7
KERNELS = 3
WIDTHS = 4

REGULARIZER = 0.05
EPSILON = 1e-06
KERNEL_FWHM = (3.0, 6.0, 9.0)
HALF_WIDTHS = (0, 1, 3, 7)

LANES = 128
MIB = 1 << 20
F32 = jnp.float32
BF16 = jnp.bfloat16
SMEM = pl.BlockSpec(memory_space=pltpu.SMEM)
VMEM = pl.BlockSpec(memory_space=pltpu.VMEM)


def params(mib):
    return pltpu.CompilerParams(vmem_limit_bytes=mib * MIB)


def cost(flops, moved):
    return pl.CostEstimate(flops=int(flops), bytes_accessed=int(moved), transcendentals=0)


def tap_table(distance):
    offsets = np.arange(-RIM, RIM + 1).astype(np.float32)
    near = np.abs(distance) <= RIM
    index = np.clip(distance + RIM, 0, 2 * RIM)
    found = []
    for fwhm in KERNEL_FWHM:
        sigma = np.float32(fwhm / 2.3548)
        taps = np.exp(-offsets * offsets / (np.float32(2.0) * sigma * sigma)).astype(ml_dtypes.bfloat16)
        found.append(np.where(near, taps[index], np.zeros((), ml_dtypes.bfloat16)))
    return np.stack(found)


def across_matrices(broad):
    half = broad // 2
    cells = np.arange(broad)
    table = tap_table(cells[:, None] - cells[None, :])
    middle = slice(half // 2, half // 2 + half)
    seam = (cells[middle, None] < half) != (cells[None, middle] < half)
    crossing = np.where(seam[None], table[:, middle, middle], np.zeros((), ml_dtypes.bfloat16))
    return np.stack([table[:, :half, :half], table[:, half:, half:], crossing], axis=1)


def down_matrices(count, strip):
    tall = count * strip
    found = []
    for me in range(count):
        rows = [(me ^ k) * strip + np.arange(strip) for k in range(count)]
        rows += [np.arange(-RIM, 0), np.arange(tall, tall + RIM)]
        rows = np.concatenate(rows)
        found.append(tap_table(rows[None, :] - np.arange(tall)[:, None]).reshape(KERNELS * tall, tall + 2 * RIM))
    return np.stack(found)


def exchange(block, axis, k):
    count = lax.axis_size(axis)
    return lax.ppermute(block, axis, [(i, i ^ k) for i in range(count)])


def pack_kernel(count, groups, me_ref, owner_ref, pieces_ref, beam_ref, *outs):
    step, channels = pieces_ref.shape[:2]
    strip = pieces_ref.shape[3]
    me = me_ref[0]
    wide_group = channels // groups
    i = pl.program_id(0)

    for k in range(count):
        target = me ^ k
        for p in range(step):
            beam = beam_ref[p, target]
            wide = beam.astype(F32)
            piece = i * step + p
            for g in range(groups):
                out = outs[g * count + k]
                planes = wide_group + (g == 0)
                for c in range(wide_group):
                    value = wide * pieces_ref[p, g * wide_group + c, target].astype(F32)
                    out[piece * planes + c] = value.astype(BF16)
                if g == 0:
                    out[piece * planes + wide_group] = beam

    @pl.when(i == 0)
    def _():
        row = lax.broadcasted_iota(jnp.int32, (strip, LANES), 0)
        plane = jnp.zeros((strip, LANES), jnp.int32)
        for p in range(owner_ref.shape[0]):
            plane = jnp.where(row == p, owner_ref[p], plane)
        for k in range(count):
            out = outs[k]
            out[out.shape[0] - 1] = plane.astype(F32).astype(BF16)


def pack(me, destination, pieces, beam, count, groups):
    piece_count, channels, size, _ = pieces.shape
    strip = size // count
    step = 2
    parts = pieces.reshape(piece_count, channels, count, strip, LANES)
    beams = beam.reshape(piece_count, count, strip, LANES)
    planes = [piece_count * (channels // groups + (g == 0)) + (g == 0) for g in range(groups)]
    outs = [jax.ShapeDtypeStruct((planes[g], strip, LANES), BF16) for g in range(groups) for _ in range(count)]
    found = pl.pallas_call(
        functools.partial(pack_kernel, count, groups),
        grid=(piece_count // step,),
        in_specs=[
            SMEM,
            SMEM,
            pl.BlockSpec((step, channels, count, strip, LANES), lambda i: (i, 0, 0, 0, 0)),
            pl.BlockSpec((step, count, strip, LANES), lambda i: (i, 0, 0, 0)),
        ],
        out_specs=[pl.BlockSpec(out.shape, lambda i: (0, 0, 0)) for out in outs],
        out_shape=outs,
        compiler_params=params(56),
        cost_estimate=cost(pieces.size, 4 * pieces.size),
        name="pack_pieces",
    )(me, destination, parts, beams)
    return [found[g * count : (g + 1) * count] for g in range(groups)]


def write_strips(count, me, scale, total, outs):
    _, channels, strip, _ = total.shape
    first = me == 0
    last = me == count - 1
    for k, out in enumerate(outs):
        tile = me ^ k
        other = jnp.where(last, tile - 1, tile + 1)
        valid = jnp.logical_or(
            jnp.logical_and(last, tile > 0), jnp.logical_and(first, tile < count - 1)
        )
        other = jnp.clip(other, 0, count - 1)
        for column in range(COLB):
            lanes = slice(column * LANES, (column + 1) * LANES)
            block = tile * COLB + column
            factor = scale[block]
            for c in range(channels):
                out[c, :, lanes] = (total[block, c] * factor).astype(BF16)
            block = other * COLB + column
            rows = []
            for c in range(channels):
                high = total[block, c, strip - RIM :] * scale[block, strip - RIM :]
                low = total[block, c, :RIM] * scale[block, :RIM]
                rows.append(jnp.where(valid, jnp.where(last, high, low), 0.0))
            rims = jnp.concatenate(rows, axis=0)
            for e in range(channels * RIM // strip):
                out[channels + e, :, lanes] = rims[e * strip : (e + 1) * strip].astype(BF16)


def combine_first_kernel(count, piece_count, me_ref, *refs):
    parts, outs = refs[:count], refs[count : 2 * count]
    scale, owners, total, cover, rows, table, sem = refs[2 * count :]
    planes = (parts[0].shape[0] - 1) // piece_count
    channels = planes - 1
    me = me_ref[0]
    for k, part in enumerate(parts):
        plane = part[part.shape[0] - 1].astype(F32)[:piece_count]
        rows[k * piece_count : (k + 1) * piece_count] = plane.astype(jnp.int32)
    copy = pltpu.make_async_copy(rows, table, sem)
    copy.start()
    total[...] = jnp.zeros_like(total)
    cover[...] = jnp.full(cover.shape, REGULARIZER, F32)
    copy.wait()
    for k, part in enumerate(parts):

        def add(p, _, k=k, part=part):
            block = table[k * piece_count + p, 0]
            owners[k, p] = block
            beam = part[p * planes + channels].astype(F32)
            cover[block] += beam * beam
            total[block] += part[pl.ds(p * planes, channels)].astype(F32)
            return 0

        lax.fori_loop(0, piece_count, add, 0)
    scale[...] = 1.0 / cover[...]
    write_strips(count, me, scale, total, outs)


def combine_next_kernel(count, piece_count, me_ref, owners, scale, *refs):
    parts, outs, total = refs[:count], refs[count : 2 * count], refs[2 * count]
    channels = parts[0].shape[0] // piece_count
    total[...] = jnp.zeros_like(total)
    for k, part in enumerate(parts):

        def add(p, _, k=k, part=part):
            total[owners[k, p]] += part[pl.ds(p * channels, channels)].astype(F32)
            return 0

        lax.fori_loop(0, piece_count, add, 0)
    write_strips(count, me_ref[0], scale, total, outs)


def combine(me, known, parts, channels, piece_count, count):
    strip = parts[0].shape[1]
    out = jax.ShapeDtypeStruct((channels + channels * RIM // strip, strip, COLB * LANES), BF16)
    blocks = count * COLB
    total = pltpu.VMEM((blocks, channels, strip, LANES), F32)
    common = dict(
        compiler_params=params(24),
        cost_estimate=cost(4 * count * parts[0].size, 4 * count * parts[0].size),
    )
    if known is None:
        found = pl.pallas_call(
            functools.partial(combine_first_kernel, count, piece_count),
            in_specs=[SMEM] + [VMEM] * count,
            out_specs=[VMEM] * (count + 1) + [SMEM],
            out_shape=[out] * count
            + [
                jax.ShapeDtypeStruct((blocks, strip, LANES), F32),
                jax.ShapeDtypeStruct((count, piece_count), jnp.int32),
            ],
            scratch_shapes=[
                total,
                pltpu.VMEM((blocks, strip, LANES), F32),
                pltpu.VMEM((count * piece_count, LANES), jnp.int32),
                pltpu.SMEM((count * piece_count, LANES), jnp.int32),
                pltpu.SemaphoreType.DMA,
            ],
            name="combine_first",
            **common,
        )(me, *parts)
        return found[:count], found[count:]
    scale, owners = known
    found = pl.pallas_call(
        functools.partial(combine_next_kernel, count, piece_count),
        in_specs=[SMEM, SMEM, VMEM] + [VMEM] * count,
        out_specs=[VMEM] * count,
        out_shape=[out] * count,
        scratch_shapes=[total],
        name="combine_next",
        **common,
    )(me, owners, scale, *parts)
    return found, known


def assemble_kernel(count, ranges, me_ref, *refs):
    parts, outs = refs[:count], refs[count:]
    channels, tall, broad = outs[0].shape
    strip = parts[0].shape[1]
    me = me_ref[0]

    def place(c, value, start):
        size = value.shape[0]
        for out, (low, high) in zip(outs, ranges):
            if low <= c < high:
                out[c - low, start : start + size] = value

    rims = [part[channels:].astype(F32).reshape(channels, RIM, broad) for part in parts]
    for c in range(channels):
        above = jnp.zeros((RIM, broad), F32)
        below = jnp.zeros((RIM, broad), F32)
        for k, rim in enumerate(rims):
            source = me ^ k
            above = jnp.where(source == count - 1, rim[c], above)
            below = jnp.where(source == 0, rim[c], below)
        edges = jnp.concatenate([above, below], axis=0).astype(BF16)
        if strip % 16 == 0:
            for k, part in enumerate(parts):
                place(c, part[c], k * strip)
        else:
            body = jnp.concatenate([part[c].astype(F32) for part in parts], axis=0)
            place(c, body.astype(BF16), 0)
        place(c, edges, count * strip)


def assemble(me, parts, ranges, count):
    _, strip, broad = parts[0].shape
    tall = count * strip + 2 * RIM
    outs = [jax.ShapeDtypeStruct((high - low, tall, broad), BF16) for low, high in ranges]
    return pl.pallas_call(
        functools.partial(assemble_kernel, count, ranges),
        in_specs=[SMEM] + [VMEM] * count,
        out_specs=[VMEM] * len(outs),
        out_shape=outs,
        compiler_params=params(16),
        cost_estimate=cost(outs[0].size, 8 * outs[0].size),
        name="assemble_tile",
    )(me, *parts)


def smooth_planes(sources, down, across, middle, out):
    tall = down.shape[0] // KERNELS
    broad = sources[0].shape[2]
    half = broad // 2
    at = 0
    for source in sources:
        for c in range(source.shape[0]):
            found = jnp.dot(down[...], source[c], preferred_element_type=F32).astype(BF16)
            for k in range(KERNELS):
                middle[k, at * tall : (at + 1) * tall] = found[k * tall : (k + 1) * tall]
            at += 1
    chunks = -(-at // 4)
    sizes = [at // chunks + (i < at % chunks) for i in range(chunks)]
    for k in range(KERNELS):
        start = 0
        for size in sizes:
            rows = slice(start * tall, (start + size) * tall)
            quarter = half // 2
            left = jnp.dot(middle[k, rows, :half], across[k, 0], preferred_element_type=F32)
            right = jnp.dot(middle[k, rows, half:], across[k, 1], preferred_element_type=F32)
            seam = jnp.dot(
                middle[k, rows, quarter : quarter + half], across[k, 2], preferred_element_type=F32
            )
            parts = [
                left[:, :quarter],
                left[:, quarter:] + seam[:, :quarter],
                right[:, :quarter] + seam[:, quarter:],
                right[:, quarter:],
            ]
            for i, part in enumerate(parts):
                lanes = slice(i * quarter, (i + 1) * quarter)
                value = part.astype(BF16).reshape(size, tall, quarter)
                out[k, start : start + size, :, lanes] = value
            start += size


def smooth_kernel(inputs, me_ref, down, across, *refs):
    sources, (out, middle) = refs[:inputs], refs[inputs:]
    smooth_planes(sources, down.at[me_ref[0]], across, middle, out)


def smooth(me, sources, down, across, name):
    planes = sum(source.shape[0] for source in sources)
    broad = sources[0].shape[2]
    tall = down.shape[1] // KERNELS
    out = jax.ShapeDtypeStruct((KERNELS, planes, tall, broad), BF16)
    return pl.pallas_call(
        functools.partial(smooth_kernel, len(sources)),
        in_specs=[SMEM] + [VMEM] * (2 + len(sources)),
        out_specs=VMEM,
        out_shape=out,
        scratch_shapes=[pltpu.VMEM((KERNELS, planes * tall, broad), BF16)],
        compiler_params=params(20),
        cost_estimate=cost(2 * out.size * (broad + 256), 4 * out.size),
        name=name,
    )(me, down, across, *sources)


def boxcars(load, channels):
    x, two, four, eight, one, three = {}, {}, {}, {}, {}, {}
    for i in range(channels + 2 * EDGE):
        x[i] = load(i)
        if i >= 1:
            two[i - 1] = x[i - 1] + x[i]
        if i >= 3:
            four[i - 3] = two[i - 3] + two[i - 1]
        if i >= 7:
            eight[i - 7] = four[i - 7] + four[i - 3]
        if i >= 2:
            one[i - 1] = two[i - 2] + x[i]
        if i >= 6:
            three[i - 3] = four[i - 6] + one[i - 1]
        ready = [(0, i, x), (1, i - 1, one), (2, i - 3, three)]
        for w, center, table in ready:
            if EDGE <= center < EDGE + channels:
                yield w, center - EDGE, table[center]
        if i >= 2 * EDGE:
            yield 3, i - 2 * EDGE, eight[i - 14] + three[i - 3]


def layer_order(counts):
    own, halo = counts
    groups = len(own)
    order = []
    for g in range(groups):
        order += [(groups + g, c) for c in range(halo[g][0])]
    for g in range(groups):
        order += [(g, c) for c in range(own[g])]
    for g in range(groups):
        order += [(groups + g, halo[g][0] + c) for c in range(halo[g][1])]
    return order


def power_kernel(order, channels, inputs, me_ref, down, across, *refs):
    sources, ready = refs[:inputs], refs[inputs:-4]
    halo, power, middle, sums = refs[-4:]
    smooth_planes(sources, down.at[me_ref[0]], across, middle, halo)
    layers = list(ready) + [halo]
    tall, broad = halo.shape[2:]
    sums[...] = jnp.zeros_like(sums)
    lane_groups = broad // LANES

    def add(step, _):
        rows = pl.ds(pl.multiple_of(step // lane_groups * 16, 16), 16)
        lanes = pl.ds(pl.multiple_of(step % lane_groups * LANES, LANES), LANES)
        for k in range(KERNELS):

            def load(i, k=k):
                array, plane = order[i]
                return layers[array][k, plane, rows, lanes].astype(F32)

            for w, c, value in boxcars(load, channels):
                square = value * value
                sums[(k * WIDTHS + w) * channels + c] += square[:8] + square[8:]
        return 0

    lax.fori_loop(0, tall // 16 * lane_groups, add, 0)
    total = jnp.sum(jnp.sum(sums[...], axis=1), axis=1, keepdims=True)
    power[...] = jnp.broadcast_to(total, power.shape)


def smooth_power(me, sources, ready, order, channels, down, across):
    planes = sum(source.shape[0] for source in sources)
    _, _, tall, broad = ready[0].shape
    pairs = KERNELS * WIDTHS * channels
    halo = jax.ShapeDtypeStruct((KERNELS, planes, tall, broad), BF16)
    return pl.pallas_call(
        functools.partial(power_kernel, order, channels, len(sources)),
        in_specs=[SMEM] + [VMEM] * (2 + len(sources) + len(ready)),
        out_specs=[VMEM] * 2,
        out_shape=[halo, jax.ShapeDtypeStruct((pairs, LANES), F32)],
        scratch_shapes=[
            pltpu.VMEM((KERNELS, planes * tall, broad), BF16),
            pltpu.VMEM((pairs, 8, LANES), F32),
        ],
        compiler_params=params(32),
        cost_estimate=cost(2 * halo.size * (broad + 256), 8 * halo.size),
        name="smooth_power",
    )(me, down, across, *sources, *ready)


def score_kernel(order, count, cells, inputs, *refs):
    layers, clips, powers = refs[:inputs], refs[inputs], refs[inputs + 1 : inputs + 1 + count]
    out, factor = refs[-2:]
    channels, step_rows, broad = out.shape

    @pl.when(pl.program_id(0) == 0)
    def _():
        total = powers[0][...]
        for item in powers[1:]:
            total = total + item[...]
        scale = 10.0 / (clips[...] * jnp.sqrt(total / cells + EPSILON))
        factor[...] = jnp.broadcast_to(scale[:, None], factor.shape)

    lane_groups = broad // LANES
    base = pl.program_id(0) * step_rows

    def score(step, _):
        start = pl.multiple_of(step // lane_groups * 16, 16)
        rows = pl.ds(pl.multiple_of(base + start, 16), 16)
        lanes = pl.ds(pl.multiple_of(step % lane_groups * LANES, LANES), LANES)
        for half in range(2):
            best = [None] * channels
            for k in range(KERNELS):

                def load(i, k=k):
                    array, plane = order[i]
                    value = layers[array][k, plane, rows, lanes].astype(F32)
                    return value[half * 8 : half * 8 + 8]

                for w, c, value in boxcars(load, channels):
                    value = jnp.abs(value) * factor[(k * WIDTHS + w) * channels + c]
                    best[c] = value if best[c] is None else jnp.maximum(best[c], value)
            for c in range(channels):
                out[c, pl.ds(start + half * 8, 8), lanes] = best[c]
        return 0

    lax.fori_loop(0, step_rows // 16 * lane_groups, score, 0)


def score(layers, order, channels, clips, powers, cells):
    _, _, tall, broad = layers[0].shape
    pairs = KERNELS * WIDTHS * channels
    step = 32
    return pl.pallas_call(
        functools.partial(score_kernel, order, len(powers), cells, len(layers)),
        grid=(tall // step,),
        in_specs=[VMEM] * (len(layers) + 1 + len(powers)),
        out_specs=pl.BlockSpec((channels, step, broad), lambda i: (0, i, 0)),
        out_shape=jax.ShapeDtypeStruct((channels, tall, broad), F32),
        scratch_shapes=[pltpu.VMEM((pairs, 8, LANES), F32)],
        compiler_params=params(24),
        cost_estimate=cost(40 * KERNELS * channels * tall * broad, 8 * layers[0].size),
        name="score_cells",
    )(*layers, clips, *powers)


def shards(across_table, down_table, pieces, beam, destination, clip_tenths):
    count = lax.axis_size("sky")
    links = lax.axis_size("freq")
    piece_count, channels = pieces.shape[:2]
    groups = 2
    size = channels // groups
    me = lax.axis_index("sky").astype(jnp.int32).reshape(1)
    across = jnp.asarray(across_table)
    down = jnp.asarray(down_table)
    upward = [(i, i + 1) for i in range(links - 1)]
    downward = [(i + 1, i) for i in range(links - 1)]
    packed = pack(me, destination, pieces, beam, count, groups)
    arrived = [[part[0]] + [exchange(part[k], "sky", k) for k in range(1, count)] for part in packed]
    known = None
    own, halo = [], []
    for g in range(groups):
        strips, known = combine(me, known, arrived[g], size, piece_count, count)
        tiles = [strips[0]] + [exchange(strips[k], "sky", k) for k in range(1, count)]
        lower = (0, min(size, EDGE - g * size))
        upper = (max(0, channels - EDGE - g * size), size)
        cuts = [(0, size)] + [cut for cut in (lower, upper) if cut != (0, size)]
        parts = dict(zip(cuts, assemble(me, tiles, cuts, count)))
        low = lax.ppermute(parts[upper], "freq", upward)
        high = lax.ppermute(parts[lower], "freq", downward)
        own.append(parts[(0, size)])
        halo.append([low, high])
    order = layer_order(
        ([item.shape[0] for item in own], [[item.shape[0] for item in pair] for pair in halo])
    )
    ready = [smooth(me, [item], down, across, "smooth_own") for item in own]
    ready += [smooth(me, pair, down, across, "smooth_halo") for pair in halo[:-1]]
    last, power = smooth_power(me, halo[-1], ready, order, channels, down, across)
    powers = [power] + [exchange(power, "sky", k) for k in range(1, count)]
    clips = jnp.repeat(clip_tenths.astype(F32).reshape(-1), channels)
    clips = jnp.broadcast_to(clips[:, None], power.shape)
    cells = float(count * ROWB * LANES * COLB * LANES)
    return score(ready + [last], order, channels, clips, powers, cells)


def solution(mesh):
    count = mesh.shape["sky"]
    body = functools.partial(
        shards, across_matrices(COLB * LANES), down_matrices(count, ROWB * LANES // count)
    )
    return jax.shard_map(
        body,
        mesh=mesh,
        in_specs=(P("sky", "freq", None, None), P("sky", None, None), P("sky"), P()),
        out_specs=P("freq", "sky", None),
        check_vma=False,
    )
```

time: 109 us -> 101 us (0.927)
  blocking collectives: 25.3 us -> 0 us
  waiting for transfers between devices: 18 us -> 36.4 us
  starting transfers between devices: 17 us -> 30.5 us
  Pallas kernels: 35 us -> 25.2 us
  local copies, waits for them, and re-layouts: 12.7 us -> 8.36 us
    unnamed x1 -> x0, blocking collectives: 25.3 us -> none
    ppermute x9 -> x15, waiting for transfers between devices: 13.9 us -> 33.1 us  [exchange(): return lax.ppermute(block, axis, [(i, i ^ k) for i in range(count)])]
    pallas_call x6 -> x10, Pallas kernels: 35 us -> 25.2 us  [the longest x1 6.89 us: score(): pl.pallas_call(functools.partial(score_kernel, order, len(powers), cells,...]
    ppermute x2 -> x4, starting transfers between devices: 8.33 us -> 16.5 us  [the longest x2 8.96 us: shards(): high = lax.ppermute(parts[lower], 'freq', downward)]
    ppermute x9 -> x15, starting transfers between devices: 8.64 us -> 14 us  [exchange(): return lax.ppermute(block, axis, [(i, i ^ k) for i in range(count)])]
    unnamed x27 -> x22, local copies, waits for them, and re-layouts: 11.3 us -> 8.05 us
    ppermute x2 -> x4, waiting for transfers between devices: 4.08 us -> 3.31 us  [the longest x2 3.3 us: shards(): high = lax.ppermute(parts[lower], 'freq', downward)]
  transfers between devices with their start and end apart: 11 -> 19, of which waited for: 7 -> 11; matrix products, arithmetic and copies ran while one was open for 2% -> 0% of each run, Pallas kernels for 5% -> 6%
where the time goes in v2:
time: 101 us
  waiting for transfers between devices  36.4 us (36%)
  starting transfers between devices  30.5 us (30%)
  Pallas kernels  25.2 us (25%)
  local copies, waits for them, and re-layouts  8.36 us (8%)
    ppermute x15, waiting for transfers between devices, exchange(): return lax.ppermute(block, axis, [(i, i ^ k) for i in range(count)])  33.1 us
    ppermute x15, starting transfers between devices, exchange(): return lax.ppermute(block, axis, [(i, i ^ k) for i in range(count)])  14 us
    ppermute x2, starting transfers between devices, shards(): high = lax.ppermute(parts[lower], 'freq', downward)  8.96 us
    unnamed x22, local copies, waits for them, and re-layouts  8.05 us
    ppermute x2, starting transfers between devices, shards(): low = lax.ppermute(parts[upper], 'freq', upward)  7.54 us
    pallas_call x1, Pallas kernels, score(): pl.pallas_call(functools.partial(score_kernel, order, len(powers), cells,...  6.89 us
    pallas_call x1, Pallas kernels, smooth_power(): pl.pallas_call(functools.partial(power_kernel, order, channels, len(sourc...  6.78 us
    pallas_call x3, Pallas kernels, smooth(): pl.pallas_call(functools.partial(smooth_kernel, len(sources)), in_specs=[...  4.29 us
  transfers between devices with their start and end apart: 19, of which 11 were waited for; matrix products, arithmetic and copies ran while one was open for 0% of the time, Pallas kernels for 6%

profile of v2, /device:TPU:1, one launch (start us, length us, event | category | flops | bytes accessed | tf_op | source)
XLA Modules:
  0.0 100.7 jit_solution(9683117421252265454)
XLA Ops:
  0.0 4.0 %pack_pieces.1 = (bf16[41,32,128]{2,1,0:T(8,128)(2,1)}, bf16[41,32,128]{2,1,0:T(8,128)(2,1)}, bf16[41,32,128]{2,1,0:T(8,128)(2,1)}, bf16[41,32,128]{2,1,0:T(8,12...) custom-call(s32[1]{0:T(128)} %bitcast.me_ref, ...), custom_call_target="tpu_custom_call" | custom-call | flops 1048576 | bytes 4194304 | tf_op jit(solution)/shard_map/pack_pieces/pallas_call | solution.py:119
  4.0 2.1 %collective-permute-start = (bf16[41,32,128]{2,1,0:T(8,128)(2,1)}, bf16[41,32,128]{2,1,0:T(8,128)(2,1)S(1)}, u32[]{:S(2)}, u32[]{:S(2)}) collective-permute-start(bf16[41,32,128]{2,1,0:T(8,128)(2,1)} %get-tuple-element.30), channel_id=1, source_target_pairs={{0,8},{8,0},{16,24},{24,16},{1,9},{9,1},{17,25},{25,17},{2,10},{10... | collective-permute-start | bytes 1007624 | tf_op jit(solution)/shard_map/ppermute | solution.py:75
  6.1 1.2 %collective-permute-start.1 = (bf16[41,32,128]{2,1,0:T(8,128)(2,1)}, bf16[41,32,128]{2,1,0:T(8,128)(2,1)S(1)}, u32[]{:S(2)}, u32[]{:S(2)}) collective-permute-start(bf16[41,32,128]{2,1,0:T(8,128)(2,1)} %get-tuple-element.31), channel_id=1, source_target_pairs={{0,16},{8,24},{16,0},{24,8},{1,17},{9,25},{17,1},{25,9},{2,18},{10... | collective-permute-start | bytes 1007624 | tf_op jit(solution)/shard_map/ppermute | solution.py:75
  7.4 6.6 %collective-permute-done.refs_1_ = bf16[41,32,128]{2,1,0:T(8,128)(2,1)S(1)} collective-permute-done((bf16[41,32,128]{2,1,0:T(8,128)(2,1)}, bf16[41,32,128]{2,1,0:T(8,128)(2,1)S(1)}, u32[]{:S(2)}, u32[]{:S(2)}) %collective-permute-start) | collective-permute-done | bytes 335904 | tf_op jit(solution)/shard_map/ppermute | solution.py:75
  13.9 0.8 collective-permute-done.1.refs_2_
  14.7 7.3 %collective-permute-done.2.refs_3_ = bf16[41,32,128]{2,1,0:T(8,128)(2,1)S(1)} collective-permute-done((bf16[41,32,128]{2,1,0:T(8,128)(2,1)}, bf16[41,32,128]{2,1,0:T(8,128)(2,1)S(1)}, u32[]{:S(2)}, u32[]{:S(2)}) %collective-permute-start.2) | collective-permute-done | bytes 335904 | tf_op jit(solution)/shard_map/ppermute | solution.py:75
  22.0 1.0 copy-done.8
  23.0 1.9 %combine_first.1 = (bf16[5,32,512]{2,1,0:T(8,128)(2,1)S(1)}, bf16[5,32,512]{2,1,0:T(8,128)(2,1)S(1)}, bf16[5,32,512]{2,1,0:T(8,128)(2,1)S(1)}, bf16[5,32,512]{2,...) custom-call(s32[1]{0:T(128)} %bitcast.me_ref, bf16[41,32,128]{2,1,0:T(8,128)(2,1)S(1)} %copy-done.8, ...), custom_call_target="tpu_custom_call" | custom-call | flops 2686976 | bytes 2686976 | tf_op jit(solution)/shard_map/combine_first/pallas_call | solution.py:218
  25.0 1.2 %collective-permute-start.3 = (bf16[5,32,512]{2,1,0:T(8,128)(2,1)S(1)}, bf16[5,32,512]{2,1,0:T(8,128)(2,1)S(1)}, u32[]{:S(2)}, u32[]{:S(2)}) collective-permute-start(bf16[5,32,512]{2,1,0:T(8,128)(2,1)S(1)} %get-tuple-element.34), channel_id=1, source_target_pairs={{0,8},{8,0},{16,24},{24,16},{1,9},{9,1},{17,25},{25,17},{2,10},{10... | collective-permute-start | bytes 491528 | tf_op jit(solution)/shard_map/ppermute | solution.py:75
  26.2 0.3 collective-permute-start.6
  26.5 0.3 collective-permute-start.7
  26.8 2.1 %collective-permute-start.8 = (bf16[32,32,128]{2,1,0:T(8,128)(2,1)}, bf16[32,32,128]{2,1,0:T(8,128)(2,1)S(1)}, u32[]{:S(2)}, u32[]{:S(2)}) collective-permute-start(bf16[32,32,128]{2,1,0:T(8,128)(2,1)} %get-tuple-element.43), channel_id=1, source_target_pairs={{0,24},{8,16},{16,8},{24,0},{1,25},{9,17},{17,9},{25,1},{2,26},{10... | collective-permute-start | bytes 786440 | tf_op jit(solution)/shard_map/ppermute | solution.py:75
  28.8 0.3 collective-permute-start.4
  29.1 0.1 collective-permute-done.3.refs_1_
  29.2 1.2 %collective-permute-start.5 = (bf16[5,32,512]{2,1,0:T(8,128)(2,1)S(1)}, bf16[5,32,512]{2,1,0:T(8,128)(2,1)S(1)}, u32[]{:S(2)}, u32[]{:S(2)}) collective-permute-start(bf16[5,32,512]{2,1,0:T(8,128)(2,1)S(1)} %get-tuple-element.36), channel_id=1, source_target_pairs={{0,24},{8,16},{16,8},{24,0},{1,25},{9,17},{17,9},{25,1},{2,26},{10... | collective-permute-start | bytes 491528 | tf_op jit(solution)/shard_map/ppermute | solution.py:75
  30.4 7.4 %collective-permute-done.4.refs_2_ = bf16[5,32,512]{2,1,0:T(8,128)(2,1)S(1)} collective-permute-done((bf16[5,32,512]{2,1,0:T(8,128)(2,1)S(1)}, bf16[5,32,512]{2,1,0:T(8,128)(2,1)S(1)}, u32[]{:S(2)}, u32[]{:S(2)}) %collective-permute-start.4) | collective-permute-done | bytes 163872 | tf_op jit(solution)/shard_map/ppermute | solution.py:75
  37.7 5.2 %collective-permute-done.5.refs_3_ = bf16[5,32,512]{2,1,0:T(8,128)(2,1)S(1)} collective-permute-done((bf16[5,32,512]{2,1,0:T(8,128)(2,1)S(1)}, bf16[5,32,512]{2,1,0:T(8,128)(2,1)S(1)}, u32[]{:S(2)}, u32[]{:S(2)}) %collective-permute-start.5) | collective-permute-done | bytes 163872 | tf_op jit(solution)/shard_map/ppermute | solution.py:75
  42.9 0.1 assemble_tile.2
  43.0 7.0 %collective-permute-start.13 = (bf16[4,144,512]{2,1,0:T(8,128)(2,1)S(1)}, bf16[4,144,512]{2,1,0:T(8,128)(2,1)S(1)}, u32[]{:S(2)}, u32[]{:S(2)}) collective-permute-start(bf16[4,144,512]{2,1,0:T(8,128)(2,1)S(1)} %get-tuple-element.37.refs_0_), channel_id=1, source_target_pairs={{1,0},{2,1},{3,2},{4,3},{5,4},{6,5},{7,6},{9,8},{10,9},{11,10},{12... | collective-permute-start | bytes 1769480 | tf_op jit(solution)/shard_map/ppermute | solution.py:516
  50.1 0.9 copy-done.9
  51.0 1.2 %combine_next.1 = (bf16[5,32,512]{2,1,0:T(8,128)(2,1)S(1)}, bf16[5,32,512]{2,1,0:T(8,128)(2,1)S(1)}, bf16[5,32,512]{2,1,0:T(8,128)(2,1)S(1)}, bf16[5,32,512]{2,1,0:T(8,128)(2,1)S(1)}) custom-call(s32[1]{0:T(128)} %bitcast.me_ref, s32[4,8]{1,0:T(4,128)S(1)} %get-tuple-element.38.owners, f32[16,32,128]{2,1,0:T(8,128)S(1)} %get-tuple-element.39.scale, ...), custom_call_target="tpu_custom_call" | custom-call | flops 2097152 | bytes 2097152 | tf_op jit(solution)/shard_map/combine_next/pallas_call | solution.py:239
  52.2 1.2 %collective-permute-start.9 = (bf16[5,32,512]{2,1,0:T(8,128)(2,1)S(1)}, bf16[5,32,512]{2,1,0:T(8,128)(2,1)S(1)}, u32[]{:S(2)}, u32[]{:S(2)}) collective-permute-start(bf16[5,32,512]{2,1,0:T(8,128)(2,1)S(1)} %get-tuple-element.45), channel_id=1, source_target_pairs={{0,8},{8,0},{16,24},{24,16},{1,9},{9,1},{17,25},{25,17},{2,10},{10... | collective-permute-start | bytes 491528 | tf_op jit(solution)/shard_map/ppermute | solution.py:75
  53.4 0.3 collective-permute-start.10
  53.7 1.2 %collective-permute-start.11 = (bf16[5,32,512]{2,1,0:T(8,128)(2,1)S(1)}, bf16[5,32,512]{2,1,0:T(8,128)(2,1)S(1)}, u32[]{:S(2)}, u32[]{:S(2)}) collective-permute-start(bf16[5,32,512]{2,1,0:T(8,128)(2,1)S(1)} %get-tuple-element.47), channel_id=1, source_target_pairs={{0,24},{8,16},{16,8},{24,0},{1,25},{9,17},{17,9},{25,1},{2,26},{10... | collective-permute-start | bytes 491528 | tf_op jit(solution)/shard_map/ppermute | solution.py:75
  54.9 3.9 %collective-permute-start.12 = (bf16[3,144,512]{2,1,0:T(8,128)(2,1)S(1)}, bf16[3,144,512]{2,1,0:T(8,128)(2,1)S(1)}, u32[]{:S(2)}, u32[]{:S(2)}) collective-permute-start(bf16[3,144,512]{2,1,0:T(8,128)(2,1)S(1)} %get-tuple-element.49), channel_id=1, source_target_pairs={{0,1},{1,2},{2,3},{3,4},{4,5},{5,6},{6,7},{8,9},{9,10},{10,11},{11... | collective-permute-start | bytes 1327112 | tf_op jit(solution)/shard_map/ppermute | solution.py:515
  58.9 4.2 %collective-permute-done.10.refs_2_ = bf16[5,32,512]{2,1,0:T(8,128)(2,1)S(1)} collective-permute-done((bf16[5,32,512]{2,1,0:T(8,128)(2,1)S(1)}, bf16[5,32,512]{2,1,0:T(8,128)(2,1)S(1)}, u32[]{:S(2)}, u32[]{:S(2)}) %collective-permute-start.10) | collective-permute-done | bytes 163872 | tf_op jit(solution)/shard_map/ppermute | solution.py:75
  63.0 0.1 assemble_tile.3
  63.1 3.6 %collective-permute-start.14 = (bf16[4,144,512]{2,1,0:T(8,128)(2,1)S(1)}, bf16[4,144,512]{2,1,0:T(8,128)(2,1)S(1)}, u32[]{:S(2)}, u32[]{:S(2)}) collective-permute-start(bf16[4,144,512]{2,1,0:T(8,128)(2,1)S(1)} %get-tuple-element.48.refs_0_), channel_id=1, source_target_pairs={{0,1},{1,2},{2,3},{3,4},{4,5},{5,6},{6,7},{8,9},{9,10},{10,11},{11... | collective-permute-start | bytes 1769480 | tf_op jit(solution)/shard_map/ppermute | solution.py:515
  66.7 1.9 %collective-permute-start.15 = (bf16[3,144,512]{2,1,0:T(8,128)(2,1)S(1)}, bf16[3,144,512]{2,1,0:T(8,128)(2,1)S(1)}, u32[]{:S(2)}, u32[]{:S(2)}) collective-permute-start(bf16[3,144,512]{2,1,0:T(8,128)(2,1)S(1)} %get-tuple-element.50), channel_id=1, source_target_pairs={{1,0},{2,1},{3,2},{4,3},{5,4},{6,5},{7,6},{9,8},{10,9},{11,10},{12... | collective-permute-start | bytes 1327112 | tf_op jit(solution)/shard_map/ppermute | solution.py:516
  68.7 1.2 %smooth_own.2.refs_2_.refs_0_ = bf16[3,4,128,512]{3,2,1,0:T(8,128)(2,1)S(1)} custom-call(s32[1]{0:T(128)} %bitcast.me_ref, bf16[4,384,144]{2,1,0:T(8,128)(2,1)S(1)} %copy-done.7, bf16[3,3,256,256]{3,2,1,0:T(8,128)(2,1)S(1)} %copy-done.6, bf16[4,144,512]{2,1,0:T(8,128)(2,1)S(1)} %get-tuple-element.37.refs_0_), custom_call_target="tpu_custom_call" | custom-call | flops 1207959552 | bytes 3145728 | tf_op jit(solution)/shard_map/smooth_own/pallas_call | solution.py:342
  69.9 1.2 %smooth_own.3.refs_3_.refs_1_ = bf16[3,4,128,512]{3,2,1,0:T(8,128)(2,1)S(1)} custom-call(s32[1]{0:T(128)} %bitcast.me_ref, bf16[4,384,144]{2,1,0:T(8,128)(2,1)S(1)} %copy-done.7, bf16[3,3,256,256]{3,2,1,0:T(8,128)(2,1)S(1)} %copy-done.6, bf16[4,144,512]{2,1,0:T(8,128)(2,1)S(1)} %get-tuple-element.48.refs_0_), custom_call_target="tpu_custom_call" | custom-call | flops 1207959552 | bytes 3145728 | tf_op jit(solution)/shard_map/smooth_own/pallas_call | solution.py:342
  71.1 1.9 %smooth_halo.1.refs_4_.refs_2_ = bf16[3,7,128,512]{3,2,1,0:T(8,128)(2,1)S(1)} custom-call(s32[1]{0:T(128)} %bitcast.me_ref, bf16[4,384,144]{2,1,0:T(8,128)(2,1)S(1)} %copy-done.7, bf16[3,3,256,256]{3,2,1,0:T(8,128)(2,1)S(1)} %copy-done.6, bf16[3,144,512]{2,1,0:T(8,128)(2,1)S(1)} %collective-permute-done.12.refs_0_, ...), custom_call_target="tpu_custom_call" | custom-call | flops 2113929216 | bytes 5505024 | tf_op jit(solution)/shard_map/smooth_halo/pallas_call | solution.py:342
  73.1 3.3 %collective-permute-done.15.refs_1_ = bf16[3,144,512]{2,1,0:T(8,128)(2,1)S(1)} collective-permute-done((bf16[3,144,512]{2,1,0:T(8,128)(2,1)S(1)}, bf16[3,144,512]{2,1,0:T(8,128)(2,1)S(1)}, u32[]{:S(2)}, u32[]{:S(2)}) %collective-permute-start.15) | collective-permute-done | bytes 442400 | tf_op jit(solution)/shard_map/ppermute | solution.py:516
  76.4 6.8 %smooth_power.1 = (bf16[3,7,128,512]{3,2,1,0:T(8,128)(2,1)S(1)}, f32[96,128]{1,0:T(8,128)S(1)}) custom-call(s32[1]{0:T(128)} %bitcast.me_ref, bf16[4,384,144]{2,1,0:T(8,128)(2,1)S(1)} %copy-done.7, bf16[3,3,256,256]{3,2,1,0:T(8,128)(2,1)S(1)} %copy-done.6, bf16[4,144,512]{2,1,0:T(8,128)(2,1)S(1)} %collective-permute-done.14.refs_0_, ...), custom_call_target="tpu_custom_call" | custom-call | flops 2113929216 | bytes 11010048 | tf_op jit(solution)/shard_map/smooth_power/pallas_call | solution.py:422
  83.2 1.5 %copy-done.4 = bf16[3,7,128,512]{3,2,1,0:T(8,128)(2,1)} copy-done((bf16[3,7,128,512]{3,2,1,0:T(8,128)(2,1)}, bf16[3,7,128,512]{3,2,1,0:T(8,128)(2,1)S(1)}, u32[]{:S(2)}) %copy-start.4) | copy-done | bytes 2752536
  84.7 0.9 collective-permute-start.18
  85.6 0.6 collective-permute-start.17
  86.1 1.2 %collective-permute-start.16 = (f32[96,128]{1,0:T(8,128)S(1)}, f32[96,128]{1,0:T(8,128)S(1)}, u32[]{:S(2)}, u32[]{:S(2)}) collective-permute-start(f32[96,128]{1,0:T(8,128)S(1)} %get-tuple-element.52.refs_5_), channel_id=1, source_target_pairs={{0,8},{8,0},{16,24},{24,16},{1,9},{9,1},{17,25},{25,17},{2,10},{10... | collective-permute-start | bytes 147464 | tf_op jit(solution)/shard_map/ppermute | solution.py:75
  87.3 0.1 reshape.16
  87.4 0.1 broadcast_in_dim.10
  87.5 0.1 broadcast_in_dim.11
  87.6 1.0 %collective-permute-done.18.refs_8_ = f32[96,128]{1,0:T(8,128)S(1)} collective-permute-done((f32[96,128]{1,0:T(8,128)S(1)}, f32[96,128]{1,0:T(8,128)S(1)}, u32[]{:S(2)}, u32[]{:S(2)}) %collective-permute-start.18) | collective-permute-done | bytes 49184 | tf_op jit(solution)/shard_map/ppermute | solution.py:75
  88.6 0.4 collective-permute-done.17.refs_7_
  89.1 0.1 broadcast_in_dim.12.refs_4_
  89.2 1.4 %copy-done.1 = bf16[3,4,128,512]{3,2,1,0:T(8,128)(2,1)S(1)} copy-done((bf16[3,4,128,512]{3,2,1,0:T(8,128)(2,1)S(1)}, bf16[3,4,128,512]{3,2,1,0:T(8,128)(2,1)}, u32[]{:S(2)}) %copy-start.1) | copy-done | bytes 1572888
  90.6 1.4 %copy-done.3 = bf16[3,4,128,512]{3,2,1,0:T(8,128)(2,1)S(1)} copy-done((bf16[3,4,128,512]{3,2,1,0:T(8,128)(2,1)S(1)}, bf16[3,4,128,512]{3,2,1,0:T(8,128)(2,1)}, u32[]{:S(2)}) %copy-start.3) | copy-done | bytes 1572888
  92.0 1.8 %copy-done.5 = bf16[3,7,128,512]{3,2,1,0:T(8,128)(2,1)S(1)} copy-done((bf16[3,7,128,512]{3,2,1,0:T(8,128)(2,1)S(1)}, bf16[3,7,128,512]{3,2,1,0:T(8,128)(2,1)}, u32[]{:S(2)}) %copy-start.5) | copy-done | bytes 2752536
  93.8 6.9 %score_cells.1 = f32[8,128,512]{2,1,0:T(8,128)} custom-call(bf16[3,4,128,512]{3,2,1,0:T(8,128)(2,1)S(1)} %copy-done.1, bf16[3,4,128,512]{3,2,1,0:T(8,128)(2,1)S(1)} %copy-done.3, bf16[3,7,128,512]{3,2,1,0:T(8,128)(2,1)S(1)} %smooth_halo.1.refs_4_.refs_2_, bf16[3,7,128,512]{3,2,1,0:T(8,128)(2,1)S(1)} %copy-done.5, f32[96,128]{1,0:T(8,128)S(1)} %broadcast_in_dim.12.refs_4_, ...), custom_call_target="tpu_custom_call" | custom-call | flops 62914560 | bytes 6291456 | tf_op jit(solution)/shard_map/score_cells/pallas_call | solution.py:480
  (27 shorter events, 0.1 us)
Async XLA Ops:
  4.0 64.7 %copy-start.6 = (bf16[3,3,256,256]{3,2,1,0:T(8,128)(2,1)S(1)}, bf16[3,3,256,256]{3,2,1,0:T(8,128)(2,1)}, u32[]{:S(2)}) copy-start(bf16[3,3,256,256]{3,2,1,0:T(8,128)(2,1)} %constant.9.clone.across) | copy-start | bytes 3538948
  4.0 64.7 %copy-start.7 = (bf16[4,384,144]{2,1,0:T(8,128)(2,1)S(1)}, bf16[4,384,144]{2,1,0:T(8,128)(2,1)}, u32[]{:S(2)}) copy-start(bf16[4,384,144]{2,1,0:T(8,128)(2,1)} %constant.10.clone.down) | copy-start | bytes 1327108
  4.0 9.9 %collective-permute-start = (bf16[41,32,128]{2,1,0:T(8,128)(2,1)}, bf16[41,32,128]{2,1,0:T(8,128)(2,1)S(1)}, u32[]{:S(2)}, u32[]{:S(2)}) collective-permute-start(bf16[41,32,128]{2,1,0:T(8,128)(2,1)} %get-tuple-element.30), channel_id=1, source_target_pairs={{0,8},{8,0},{16,24},{24,16},{1,9},{9,1},{17,25},{25,17},{2,10},{10... | collective-permute-start | bytes 1007624 | tf_op jit(solution)/shard_map/ppermute | solution.py:75
  6.1 8.6 %collective-permute-start.1 = (bf16[41,32,128]{2,1,0:T(8,128)(2,1)}, bf16[41,32,128]{2,1,0:T(8,128)(2,1)S(1)}, u32[]{:S(2)}, u32[]{:S(2)}) collective-permute-start(bf16[41,32,128]{2,1,0:T(8,128)(2,1)} %get-tuple-element.31), channel_id=1, source_target_pairs={{0,16},{8,24},{16,0},{24,8},{1,17},{9,25},{17,1},{25,9},{2,18},{10... | collective-permute-start | bytes 1007624 | tf_op jit(solution)/shard_map/ppermute | solution.py:75
  7.3 14.7 %collective-permute-start.2 = (bf16[41,32,128]{2,1,0:T(8,128)(2,1)}, bf16[41,32,128]{2,1,0:T(8,128)(2,1)S(1)}, u32[]{:S(2)}, u32[]{:S(2)}) collective-permute-start(bf16[41,32,128]{2,1,0:T(8,128)(2,1)} %get-tuple-element.32), channel_id=1, source_target_pairs={{0,24},{8,16},{16,8},{24,0},{1,25},{9,17},{17,9},{25,1},{2,26},{10... | collective-permute-start | bytes 1007624 | tf_op jit(solution)/shard_map/ppermute | solution.py:75
  22.0 1.0 copy-start.8
  25.0 4.2 %collective-permute-start.3 = (bf16[5,32,512]{2,1,0:T(8,128)(2,1)S(1)}, bf16[5,32,512]{2,1,0:T(8,128)(2,1)S(1)}, u32[]{:S(2)}, u32[]{:S(2)}) collective-permute-start(bf16[5,32,512]{2,1,0:T(8,128)(2,1)S(1)} %get-tuple-element.34), channel_id=1, source_target_pairs={{0,8},{8,0},{16,24},{24,16},{1,9},{9,1},{17,25},{25,17},{2,10},{10... | collective-permute-start | bytes 491528 | tf_op jit(solution)/shard_map/ppermute | solution.py:75
  26.2 23.9 %collective-permute-start.6 = (bf16[32,32,128]{2,1,0:T(8,128)(2,1)}, bf16[32,32,128]{2,1,0:T(8,128)(2,1)S(1)}, u32[]{:S(2)}, u32[]{:S(2)}) collective-permute-start(bf16[32,32,128]{2,1,0:T(8,128)(2,1)} %get-tuple-element.41), channel_id=1, source_target_pairs={{0,8},{8,0},{16,24},{24,16},{1,9},{9,1},{17,25},{25,17},{2,10},{10... | collective-permute-start | bytes 786440 | tf_op jit(solution)/shard_map/ppermute | solution.py:75
  26.5 23.6 %collective-permute-start.7 = (bf16[32,32,128]{2,1,0:T(8,128)(2,1)}, bf16[32,32,128]{2,1,0:T(8,128)(2,1)S(1)}, u32[]{:S(2)}, u32[]{:S(2)}) collective-permute-start(bf16[32,32,128]{2,1,0:T(8,128)(2,1)} %get-tuple-element.42), channel_id=1, source_target_pairs={{0,16},{8,24},{16,0},{24,8},{1,17},{9,25},{17,1},{25,9},{2,18},{10... | collective-permute-start | bytes 786440 | tf_op jit(solution)/shard_map/ppermute | solution.py:75
  26.8 23.3 %collective-permute-start.8 = (bf16[32,32,128]{2,1,0:T(8,128)(2,1)}, bf16[32,32,128]{2,1,0:T(8,128)(2,1)S(1)}, u32[]{:S(2)}, u32[]{:S(2)}) collective-permute-start(bf16[32,32,128]{2,1,0:T(8,128)(2,1)} %get-tuple-element.43), channel_id=1, source_target_pairs={{0,24},{8,16},{16,8},{24,0},{1,25},{9,17},{17,9},{25,1},{2,26},{10... | collective-permute-start | bytes 786440 | tf_op jit(solution)/shard_map/ppermute | solution.py:75
  28.8 8.9 %collective-permute-start.4 = (bf16[5,32,512]{2,1,0:T(8,128)(2,1)S(1)}, bf16[5,32,512]{2,1,0:T(8,128)(2,1)S(1)}, u32[]{:S(2)}, u32[]{:S(2)}) collective-permute-start(bf16[5,32,512]{2,1,0:T(8,128)(2,1)S(1)} %get-tuple-element.35), channel_id=1, source_target_pairs={{0,16},{8,24},{16,0},{24,8},{1,17},{9,25},{17,1},{25,9},{2,18},{10... | collective-permute-start | bytes 491528 | tf_op jit(solution)/shard_map/ppermute | solution.py:75
  29.2 13.7 %collective-permute-start.5 = (bf16[5,32,512]{2,1,0:T(8,128)(2,1)S(1)}, bf16[5,32,512]{2,1,0:T(8,128)(2,1)S(1)}, u32[]{:S(2)}, u32[]{:S(2)}) collective-permute-start(bf16[5,32,512]{2,1,0:T(8,128)(2,1)S(1)} %get-tuple-element.36), channel_id=1, source_target_pairs={{0,24},{8,16},{16,8},{24,0},{1,25},{9,17},{17,9},{25,1},{2,26},{10... | collective-permute-start | bytes 491528 | tf_op jit(solution)/shard_map/ppermute | solution.py:75
  43.0 28.1 %collective-permute-start.13 = (bf16[4,144,512]{2,1,0:T(8,128)(2,1)S(1)}, bf16[4,144,512]{2,1,0:T(8,128)(2,1)S(1)}, u32[]{:S(2)}, u32[]{:S(2)}) collective-permute-start(bf16[4,144,512]{2,1,0:T(8,128)(2,1)S(1)} %get-tuple-element.37.refs_0_), channel_id=1, source_target_pairs={{1,0},{2,1},{3,2},{4,3},{5,4},{6,5},{7,6},{9,8},{10,9},{11,10},{12... | collective-permute-start | bytes 1769480 | tf_op jit(solution)/shard_map/ppermute | solution.py:516
  50.1 1.0 copy-start.9
  52.2 6.7 %collective-permute-start.9 = (bf16[5,32,512]{2,1,0:T(8,128)(2,1)S(1)}, bf16[5,32,512]{2,1,0:T(8,128)(2,1)S(1)}, u32[]{:S(2)}, u32[]{:S(2)}) collective-permute-start(bf16[5,32,512]{2,1,0:T(8,128)(2,1)S(1)} %get-tuple-element.45), channel_id=1, source_target_pairs={{0,8},{8,0},{16,24},{24,16},{1,9},{9,1},{17,25},{25,17},{2,10},{10... | collective-permute-start | bytes 491528 | tf_op jit(solution)/shard_map/ppermute | solution.py:75
  53.4 9.6 %collective-permute-start.10 = (bf16[5,32,512]{2,1,0:T(8,128)(2,1)S(1)}, bf16[5,32,512]{2,1,0:T(8,128)(2,1)S(1)}, u32[]{:S(2)}, u32[]{:S(2)}) collective-permute-start(bf16[5,32,512]{2,1,0:T(8,128)(2,1)S(1)} %get-tuple-element.46), channel_id=1, source_target_pairs={{0,16},{8,24},{16,0},{24,8},{1,17},{9,25},{17,1},{25,9},{2,18},{10... | collective-permute-start | bytes 491528 | tf_op jit(solution)/shard_map/ppermute | solution.py:75
  53.7 9.3 %collective-permute-start.11 = (bf16[5,32,512]{2,1,0:T(8,128)(2,1)S(1)}, bf16[5,32,512]{2,1,0:T(8,128)(2,1)S(1)}, u32[]{:S(2)}, u32[]{:S(2)}) collective-permute-start(bf16[5,32,512]{2,1,0:T(8,128)(2,1)S(1)} %get-tuple-element.47), channel_id=1, source_target_pairs={{0,24},{8,16},{16,8},{24,0},{1,25},{9,17},{17,9},{25,1},{2,26},{10... | collective-permute-start | bytes 491528 | tf_op jit(solution)/shard_map/ppermute | solution.py:75
  54.9 16.2 %collective-permute-start.12 = (bf16[3,144,512]{2,1,0:T(8,128)(2,1)S(1)}, bf16[3,144,512]{2,1,0:T(8,128)(2,1)S(1)}, u32[]{:S(2)}, u32[]{:S(2)}) collective-permute-start(bf16[3,144,512]{2,1,0:T(8,128)(2,1)S(1)} %get-tuple-element.49), channel_id=1, source_target_pairs={{0,1},{1,2},{2,3},{3,4},{4,5},{5,6},{6,7},{8,9},{9,10},{10,11},{11... | collective-permute-start | bytes 1327112 | tf_op jit(solution)/shard_map/ppermute | solution.py:515
  63.1 13.2 %collective-permute-start.14 = (bf16[4,144,512]{2,1,0:T(8,128)(2,1)S(1)}, bf16[4,144,512]{2,1,0:T(8,128)(2,1)S(1)}, u32[]{:S(2)}, u32[]{:S(2)}) collective-permute-start(bf16[4,144,512]{2,1,0:T(8,128)(2,1)S(1)} %get-tuple-element.48.refs_0_), channel_id=1, source_target_pairs={{0,1},{1,2},{2,3},{3,4},{4,5},{5,6},{6,7},{8,9},{9,10},{10,11},{11... | collective-permute-start | bytes 1769480 | tf_op jit(solution)/shard_map/ppermute | solution.py:515
  66.7 9.6 %collective-permute-start.15 = (bf16[3,144,512]{2,1,0:T(8,128)(2,1)S(1)}, bf16[3,144,512]{2,1,0:T(8,128)(2,1)S(1)}, u32[]{:S(2)}, u32[]{:S(2)}) collective-permute-start(bf16[3,144,512]{2,1,0:T(8,128)(2,1)S(1)} %get-tuple-element.50), channel_id=1, source_target_pairs={{1,0},{2,1},{3,2},{4,3},{5,4},{6,5},{7,6},{9,8},{10,9},{11,10},{12... | collective-permute-start | bytes 1327112 | tf_op jit(solution)/shard_map/ppermute | solution.py:516
  69.9 6.5 %copy-start = (bf16[3,4,128,512]{3,2,1,0:T(8,128)(2,1)}, bf16[3,4,128,512]{3,2,1,0:T(8,128)(2,1)S(1)}, u32[]{:S(2)}) copy-start(bf16[3,4,128,512]{3,2,1,0:T(8,128)(2,1)S(1)} %smooth_own.2.refs_2_.refs_0_) | copy-start | bytes 4718596
  71.1 5.3 %copy-start.2 = (bf16[3,4,128,512]{3,2,1,0:T(8,128)(2,1)}, bf16[3,4,128,512]{3,2,1,0:T(8,128)(2,1)S(1)}, u32[]{:S(2)}) copy-start(bf16[3,4,128,512]{3,2,1,0:T(8,128)(2,1)S(1)} %smooth_own.3.refs_3_.refs_1_) | copy-start | bytes 4718596
  73.1 14.3 %copy-start.10 = (s32[3,4]{1,0:T(4,128)S(1)}, s32[3,4]{1,0:T(4,128)}, u32[]{:S(2)}) copy-start(s32[3,4]{1,0:T(4,128)} %param.9) | copy-start | bytes 148
  83.2 1.5 %copy-start.4 = (bf16[3,7,128,512]{3,2,1,0:T(8,128)(2,1)}, bf16[3,7,128,512]{3,2,1,0:T(8,128)(2,1)S(1)}, u32[]{:S(2)}) copy-start(bf16[3,7,128,512]{3,2,1,0:T(8,128)(2,1)S(1)} %get-tuple-element.51.refs_3_) | copy-start | bytes 8257540
  84.7 3.9 %collective-permute-start.18 = (f32[96,128]{1,0:T(8,128)S(1)}, f32[96,128]{1,0:T(8,128)S(1)}, u32[]{:S(2)}, u32[]{:S(2)}) collective-permute-start(f32[96,128]{1,0:T(8,128)S(1)} %get-tuple-element.52.refs_5_), channel_id=1, source_target_pairs={{0,24},{8,16},{16,8},{24,0},{1,25},{9,17},{17,9},{25,1},{2,26},{10... | collective-permute-start | bytes 147464 | tf_op jit(solution)/shard_map/ppermute | solution.py:75
  85.6 3.5 %collective-permute-start.17 = (f32[96,128]{1,0:T(8,128)S(1)}, f32[96,128]{1,0:T(8,128)S(1)}, u32[]{:S(2)}, u32[]{:S(2)}) collective-permute-start(f32[96,128]{1,0:T(8,128)S(1)} %get-tuple-element.52.refs_5_), channel_id=1, source_target_pairs={{0,16},{8,24},{16,0},{24,8},{1,17},{9,25},{17,1},{25,9},{2,18},{10... | collective-permute-start | bytes 147464 | tf_op jit(solution)/shard_map/ppermute | solution.py:75
  86.1 2.9 %collective-permute-start.16 = (f32[96,128]{1,0:T(8,128)S(1)}, f32[96,128]{1,0:T(8,128)S(1)}, u32[]{:S(2)}, u32[]{:S(2)}) collective-permute-start(f32[96,128]{1,0:T(8,128)S(1)} %get-tuple-element.52.refs_5_), channel_id=1, source_target_pairs={{0,8},{8,0},{16,24},{24,16},{1,9},{9,1},{17,25},{25,17},{2,10},{10... | collective-permute-start | bytes 147464 | tf_op jit(solution)/shard_map/ppermute | solution.py:75
  89.2 1.4 %copy-start.1 = (bf16[3,4,128,512]{3,2,1,0:T(8,128)(2,1)S(1)}, bf16[3,4,128,512]{3,2,1,0:T(8,128)(2,1)}, u32[]{:S(2)}) copy-start(bf16[3,4,128,512]{3,2,1,0:T(8,128)(2,1)} %copy-done) | copy-start | bytes 4718596
  90.6 1.4 %copy-start.3 = (bf16[3,4,128,512]{3,2,1,0:T(8,128)(2,1)S(1)}, bf16[3,4,128,512]{3,2,1,0:T(8,128)(2,1)}, u32[]{:S(2)}) copy-start(bf16[3,4,128,512]{3,2,1,0:T(8,128)(2,1)} %copy-done.2) | copy-start | bytes 4718596
  92.0 1.8 %copy-start.5 = (bf16[3,7,128,512]{3,2,1,0:T(8,128)(2,1)S(1)}, bf16[3,7,128,512]{3,2,1,0:T(8,128)(2,1)}, u32[]{:S(2)}) copy-start(bf16[3,7,128,512]{3,2,1,0:T(8,128)(2,1)} %copy-done.4) | copy-start | bytes 8257540

commit v3 on v2

v3 whole, which is shorter than its diff:
```python
import functools

import jax
import jax.numpy as jnp
import ml_dtypes
import numpy as np
from jax import lax
from jax.experimental import pallas as pl
from jax.experimental.pallas import tpu as pltpu
from jax.sharding import PartitionSpec as P

ROWB = 1
COLB = 4
RIM = 8
EDGE = 7
KERNELS = 3
WIDTHS = 4

REGULARIZER = 0.05
EPSILON = 1e-06
KERNEL_FWHM = (3.0, 6.0, 9.0)
HALF_WIDTHS = (0, 1, 3, 7)

LANES = 128
MIB = 1 << 20
F32 = jnp.float32
BF16 = jnp.bfloat16
SMEM = pl.BlockSpec(memory_space=pltpu.SMEM)
VMEM = pl.BlockSpec(memory_space=pltpu.VMEM)


def params(mib):
    return pltpu.CompilerParams(vmem_limit_bytes=mib * MIB)


def cost(flops, moved):
    return pl.CostEstimate(flops=int(flops), bytes_accessed=int(moved), transcendentals=0)


def tap_table(distance):
    offsets = np.arange(-RIM, RIM + 1).astype(np.float32)
    near = np.abs(distance) <= RIM
    index = np.clip(distance + RIM, 0, 2 * RIM)
    found = []
    for fwhm in KERNEL_FWHM:
        sigma = np.float32(fwhm / 2.3548)
        taps = np.exp(-offsets * offsets / (np.float32(2.0) * sigma * sigma)).astype(ml_dtypes.bfloat16)
        found.append(np.where(near, taps[index], np.zeros((), ml_dtypes.bfloat16)))
    return np.stack(found)


def across_matrices(broad):
    half = broad // 2
    cells = np.arange(broad)
    table = tap_table(cells[:, None] - cells[None, :])
    middle = slice(half // 2, half // 2 + half)
    seam = (cells[middle, None] < half) != (cells[None, middle] < half)
    crossing = np.where(seam[None], table[:, middle, middle], np.zeros((), ml_dtypes.bfloat16))
    return np.stack([table[:, :half, :half], table[:, half:, half:], crossing], axis=1)


def down_matrices(count, strip):
    tall = count * strip
    found = []
    for me in range(count):
        rows = [(me ^ k) * strip + np.arange(strip) for k in range(count)]
        rows += [np.arange(-RIM, 0), np.arange(tall, tall + RIM)]
        rows = np.concatenate(rows)
        found.append(tap_table(rows[None, :] - np.arange(tall)[:, None]).reshape(KERNELS * tall, tall + 2 * RIM))
    return np.stack(found)


def exchange(block, axis, k):
    count = lax.axis_size(axis)
    return lax.ppermute(block, axis, [(i, i ^ k) for i in range(count)])


def fetch_strip(pieces_hbm, beam_hbm, pieces, beams, sems, target):
    return (
        pltpu.make_async_copy(beam_hbm.at[:, target], beams, sems.at[0]),
        pltpu.make_async_copy(pieces_hbm.at[:, :, target], pieces, sems.at[1]),
    )


def weigh(pieces, beams, p):
    wide = beams[p].astype(F32)
    return [(wide * pieces[p, c].astype(F32)).astype(BF16) for c in range(pieces.shape[1])]


def pack_kernel(count, me_ref, owner_ref, pieces_hbm, beam_hbm, *refs):
    outs, (pieces, beams, packed, in_sems, out_sems) = refs[: count - 1], refs[count - 1 :]
    _, piece_count, channels, strip, _ = pieces.shape
    planes = channels + 1
    me = me_ref[0]

    def fetch(k):
        here = (pieces.at[k - 1], beams.at[k - 1], in_sems.at[k - 1])
        return fetch_strip(pieces_hbm, beam_hbm, *here, me ^ k)

    order = range(count - 1, 0, -1)
    for k in order:
        for copy in fetch(k):
            copy.start()
    row = lax.broadcasted_iota(jnp.int32, (strip, LANES), 0)
    plane = jnp.zeros((strip, LANES), jnp.int32)
    for p in range(piece_count):
        plane = jnp.where(row == p, owner_ref[p], plane)
    plane = plane.astype(F32).astype(BF16)
    for k in order:
        for copy in fetch(k):
            copy.wait()
        for p in range(piece_count):
            for c, value in enumerate(weigh(pieces.at[k - 1], beams.at[k - 1], p)):
                packed[k - 1, p * planes + c] = value
            packed[k - 1, p * planes + channels] = beams[k - 1, p]
        packed[k - 1, piece_count * planes] = plane
        pltpu.make_async_copy(packed.at[k - 1], outs[k - 1], out_sems.at[k - 1]).start()
    for k in order:
        pltpu.make_async_copy(packed.at[k - 1], outs[k - 1], out_sems.at[k - 1]).wait()


def pack(me, destination, parts, beams):
    piece_count, channels, count, strip, _ = parts.shape
    out = jax.ShapeDtypeStruct((piece_count * (channels + 1) + 1, strip, LANES), BF16)
    far = pl.BlockSpec(memory_space=pl.ANY)
    return pl.pallas_call(
        functools.partial(pack_kernel, count),
        in_specs=[SMEM, SMEM, far, far],
        out_specs=[far] * (count - 1),
        out_shape=[out] * (count - 1),
        scratch_shapes=[
            pltpu.VMEM((count - 1, piece_count, channels, strip, LANES), BF16),
            pltpu.VMEM((count - 1, piece_count, strip, LANES), BF16),
            pltpu.VMEM((count - 1,) + out.shape, BF16),
            pltpu.SemaphoreType.DMA((count - 1, 2)),
            pltpu.SemaphoreType.DMA((count - 1,)),
        ],
        compiler_params=params(58),
        cost_estimate=cost(parts.size, 4 * parts.size),
        name="pack_pieces",
    )(me, destination, parts, beams)


def gather_kernel(me_ref, owner_ref, pieces_hbm, beam_hbm, total, cover, pieces, beams, sems):
    copies = fetch_strip(pieces_hbm, beam_hbm, pieces, beams, sems, me_ref[0])
    for copy in copies:
        copy.start()
    total[...] = jnp.zeros_like(total)
    cover[...] = jnp.full(cover.shape, REGULARIZER, F32)
    for copy in copies:
        copy.wait()
    for p in range(pieces.shape[0]):
        block = owner_ref[p]
        beam = beams[p].astype(F32)
        cover[block] += beam * beam
        for c, value in enumerate(weigh(pieces, beams, p)):
            total[block, c] += value.astype(F32)


def gather_own(me, destination, parts, beams):
    piece_count, channels, count, strip, _ = parts.shape
    blocks = count * COLB
    far = pl.BlockSpec(memory_space=pl.ANY)
    return pl.pallas_call(
        gather_kernel,
        in_specs=[SMEM, SMEM, far, far],
        out_specs=[VMEM] * 2,
        out_shape=[
            jax.ShapeDtypeStruct((blocks, channels, strip, LANES), F32),
            jax.ShapeDtypeStruct((blocks, strip, LANES), F32),
        ],
        scratch_shapes=[
            pltpu.VMEM((piece_count, channels, strip, LANES), BF16),
            pltpu.VMEM((piece_count, strip, LANES), BF16),
            pltpu.SemaphoreType.DMA((2,)),
        ],
        compiler_params=params(24),
        cost_estimate=cost(parts.size, 4 * parts.size),
        name="gather_own",
    )(me, destination, parts, beams)


def write_strips(count, me, scale, total, outs):
    _, channels, strip, _ = total.shape
    first = me == 0
    last = me == count - 1
    for k, out in enumerate(outs):
        tile = me ^ k
        other = jnp.where(last, tile - 1, tile + 1)
        valid = jnp.logical_or(
            jnp.logical_and(last, tile > 0), jnp.logical_and(first, tile < count - 1)
        )
        other = jnp.clip(other, 0, count - 1)
        for column in range(COLB):
            lanes = slice(column * LANES, (column + 1) * LANES)
            block = tile * COLB + column
            factor = scale[block]
            for c in range(channels):
                out[c, :, lanes] = (total[block, c] * factor).astype(BF16)
            if out.shape[0] == channels:
                continue
            block = other * COLB + column
            rows = []
            for c in range(channels):
                high = total[block, c, strip - RIM :] * scale[block, strip - RIM :]
                low = total[block, c, :RIM] * scale[block, :RIM]
                rows.append(jnp.where(valid, jnp.where(last, high, low), 0.0))
            rims = jnp.concatenate(rows, axis=0)
            for e in range(channels * RIM // strip):
                out[channels + e, :, lanes] = rims[e * strip : (e + 1) * strip].astype(BF16)


def combine_kernel(count, piece_count, me_ref, total_in, cover_in, *refs):
    parts, outs = refs[: count - 1], refs[count - 1 : 2 * count - 1]
    total, cover, rows, table, sem = refs[2 * count - 1 :]
    planes = (parts[0].shape[0] - 1) // piece_count
    channels = planes - 1
    for i, part in enumerate(parts):
        plane = part[part.shape[0] - 1].astype(F32)[:piece_count]
        rows[i * piece_count : (i + 1) * piece_count] = plane.astype(jnp.int32)
    copy = pltpu.make_async_copy(rows, table, sem)
    copy.start()
    total[...] = total_in[...]
    cover[...] = cover_in[...]
    copy.wait()
    for i, part in enumerate(parts):

        def add(p, _, i=i, part=part):
            block = table[i * piece_count + p, 0]
            beam = part[p * planes + channels].astype(F32)
            cover[block] += beam * beam
            total[block] += part[pl.ds(p * planes, channels)].astype(F32)
            return 0

        lax.fori_loop(0, piece_count, add, 0)
    cover[...] = 1.0 / cover[...]
    write_strips(count, me_ref[0], cover, total, outs)


def combine(me, total, cover, parts, piece_count):
    count = len(parts) + 1
    blocks, channels, strip, _ = total.shape
    rim_planes = channels * RIM // strip
    outs = [
        jax.ShapeDtypeStruct((channels + rim_planes * (k != count - 1), strip, COLB * LANES), BF16)
        for k in range(count)
    ]
    rows = len(parts) * piece_count
    return pl.pallas_call(
        functools.partial(combine_kernel, count, piece_count),
        in_specs=[SMEM] + [VMEM] * (2 + len(parts)),
        out_specs=[VMEM] * count,
        out_shape=outs,
        scratch_shapes=[
            pltpu.VMEM(total.shape, F32),
            pltpu.VMEM(cover.shape, F32),
            pltpu.VMEM((rows, LANES), jnp.int32),
            pltpu.SMEM((rows, LANES), jnp.int32),
            pltpu.SemaphoreType.DMA,
        ],
        compiler_params=params(20),
        cost_estimate=cost(1, 1),
        name="combine_strips",
    )(me, total, cover, *parts)


def tile_plane(me, strips, channels, c):
    count = len(strips)
    strip, broad = strips[0].shape[1:]
    above = jnp.zeros((RIM, broad), F32)
    below = jnp.zeros((RIM, broad), F32)
    plane, row = divmod(c * RIM, strip)
    for k, part in enumerate(strips[:-1]):
        rim = part[channels + plane].astype(F32)[row : row + RIM]
        source = me ^ k
        above = jnp.where(source == count - 1, rim, above)
        below = jnp.where(source == 0, rim, below)
    if strip % 16 == 0:
        edges = jnp.concatenate([above, below], axis=0).astype(BF16)
        return jnp.concatenate([part[c] for part in strips] + [edges], axis=0)
    wide = [part[c].astype(F32) for part in strips]
    return jnp.concatenate(wide + [above, below], axis=0).astype(BF16)


def smooth_planes(me, strips, chosen, down, across, middle, out, base):
    tall = down.shape[0] // KERNELS
    broad = strips[0].shape[2]
    channels = strips[-1].shape[0]
    half = broad // 2
    at = len(chosen)
    for i, c in enumerate(chosen):
        plane = tile_plane(me, strips, channels, c)
        found = jnp.dot(down[...], plane, preferred_element_type=F32).astype(BF16)
        for k in range(KERNELS):
            middle[k, i * tall : (i + 1) * tall] = found[k * tall : (k + 1) * tall]
    chunks = -(-at // 4)
    sizes = [at // chunks + (i < at % chunks) for i in range(chunks)]
    for k in range(KERNELS):
        start = 0
        for size in sizes:
            rows = slice(start * tall, (start + size) * tall)
            quarter = half // 2
            left = jnp.dot(middle[k, rows, :half], across[k, 0], preferred_element_type=F32)
            right = jnp.dot(middle[k, rows, half:], across[k, 1], preferred_element_type=F32)
            seam = jnp.dot(
                middle[k, rows, quarter : quarter + half], across[k, 2], preferred_element_type=F32
            )
            parts = [
                left[:, :quarter],
                left[:, quarter:] + seam[:, :quarter],
                right[:, :quarter] + seam[:, quarter:],
                right[:, quarter:],
            ]
            for i, part in enumerate(parts):
                lanes = slice(i * quarter, (i + 1) * quarter)
                value = part.astype(BF16).reshape(size, tall, quarter)
                out[k, base + start : base + start + size, :, lanes] = value
            start += size


def smooth_kernel(count, me_ref, down, across, *refs):
    strips, (out, middle) = refs[:count], refs[count:]
    me = me_ref[0]
    smooth_planes(me, strips, range(out.shape[1]), down.at[me], across, middle, out, 0)


def smooth(me, strips, down, across):
    channels = strips[-1].shape[0]
    broad = strips[0].shape[2]
    tall = down.shape[1] // KERNELS
    out = jax.ShapeDtypeStruct((KERNELS, channels, tall, broad), BF16)
    return pl.pallas_call(
        functools.partial(smooth_kernel, len(strips)),
        in_specs=[SMEM] + [VMEM] * (2 + len(strips)),
        out_specs=VMEM,
        out_shape=out,
        scratch_shapes=[pltpu.VMEM((KERNELS, channels * tall, broad), BF16)],
        compiler_params=params(16),
        cost_estimate=cost(2 * out.size * (broad + 256), 4 * out.size),
        name="smooth_own",
    )(me, down, across, *strips)


def boxcars(load, channels):
    x, two, four, eight, one, three = {}, {}, {}, {}, {}, {}
    for i in range(channels + 2 * EDGE):
        x[i] = load(i)
        if i >= 1:
            two[i - 1] = x[i - 1] + x[i]
        if i >= 3:
            four[i - 3] = two[i - 3] + two[i - 1]
        if i >= 7:
            eight[i - 7] = four[i - 7] + four[i - 3]
        if i >= 2:
            one[i - 1] = two[i - 2] + x[i]
        if i >= 6:
            three[i - 3] = four[i - 6] + one[i - 1]
        ready = [(0, i, x), (1, i - 1, one), (2, i - 3, three)]
        for w, center, table in ready:
            if EDGE <= center < EDGE + channels:
                yield w, center - EDGE, table[center]
        if i >= 2 * EDGE:
            yield 3, i - 2 * EDGE, eight[i - 14] + three[i - 3]


def layer_order(channels):
    order = [(1, c) for c in range(EDGE)]
    order += [(0, c) for c in range(channels)]
    order += [(1, c) for c in range(EDGE, 2 * EDGE)]
    return order


def power_kernel(count, me_ref, down, across, own, *refs):
    low, high = refs[:count], refs[count : 2 * count]
    halo, power, middle, sums = refs[2 * count :]
    channels, tall, broad = own.shape[1:]
    me = me_ref[0]
    smooth_planes(me, low, range(channels - EDGE, channels), down.at[me], across, middle, halo, 0)
    smooth_planes(me, high, range(EDGE), down.at[me], across, middle, halo, EDGE)
    layers = (own, halo)
    order = layer_order(channels)
    sums[...] = jnp.zeros_like(sums)
    lane_groups = broad // LANES

    def add(step, _):
        rows = pl.ds(pl.multiple_of(step // lane_groups * 16, 16), 16)
        lanes = pl.ds(pl.multiple_of(step % lane_groups * LANES, LANES), LANES)
        for k in range(KERNELS):

            def load(i, k=k):
                array, plane = order[i]
                return layers[array][k, plane, rows, lanes].astype(F32)

            for w, c, value in boxcars(load, channels):
                square = value * value
                sums[(k * WIDTHS + w) * channels + c] += square[:8] + square[8:]
        return 0

    lax.fori_loop(0, tall // 16 * lane_groups, add, 0)
    total = jnp.sum(jnp.sum(sums[...], axis=1), axis=1, keepdims=True)
    power[...] = jnp.broadcast_to(total, power.shape)


def smooth_power(me, own, low, high, down, across):
    _, channels, tall, broad = own.shape
    pairs = KERNELS * WIDTHS * channels
    halo = jax.ShapeDtypeStruct((KERNELS, 2 * EDGE, tall, broad), BF16)
    return pl.pallas_call(
        functools.partial(power_kernel, len(low)),
        in_specs=[SMEM] + [VMEM] * (3 + len(low) + len(high)),
        out_specs=[VMEM] * 2,
        out_shape=[halo, jax.ShapeDtypeStruct((pairs, LANES), F32)],
        scratch_shapes=[
            pltpu.VMEM((KERNELS, EDGE * tall, broad), BF16),
            pltpu.VMEM((pairs, 8, LANES), F32),
        ],
        compiler_params=params(24),
        cost_estimate=cost(2 * halo.size * (broad + 256), 8 * halo.size),
        name="smooth_power",
    )(me, down, across, own, *low, *high)


def score_kernel(count, cells, own, halo, clips, *refs):
    layers, powers = (own, halo), refs[:count]
    out, factor = refs[-2:]
    channels, step_rows, broad = out.shape
    order = layer_order(channels)

    @pl.when(pl.program_id(0) == 0)
    def _():
        total = powers[0][...]
        for item in powers[1:]:
            total = total + item[...]
        scale = 10.0 / (clips[...] * jnp.sqrt(total / cells + EPSILON))
        factor[...] = jnp.broadcast_to(scale[:, None], factor.shape)

    lane_groups = broad // LANES
    base = pl.program_id(0) * step_rows

    def score(step, _):
        start = pl.multiple_of(step // lane_groups * 16, 16)
        rows = pl.ds(pl.multiple_of(base + start, 16), 16)
        lanes = pl.ds(pl.multiple_of(step % lane_groups * LANES, LANES), LANES)
        for half in range(2):
            best = [None] * channels
            for k in range(KERNELS):

                def load(i, k=k):
                    array, plane = order[i]
                    value = layers[array][k, plane, rows, lanes].astype(F32)
                    return value[half * 8 : half * 8 + 8]

                for w, c, value in boxcars(load, channels):
                    value = jnp.abs(value) * factor[(k * WIDTHS + w) * channels + c]
                    best[c] = value if best[c] is None else jnp.maximum(best[c], value)
            for c in range(channels):
                out[c, pl.ds(start + half * 8, 8), lanes] = best[c]
        return 0

    lax.fori_loop(0, step_rows // 16 * lane_groups, score, 0)


def score(own, halo, clips, powers, cells):
    _, channels, tall, broad = own.shape
    pairs = KERNELS * WIDTHS * channels
    step = 32
    return pl.pallas_call(
        functools.partial(score_kernel, len(powers), cells),
        grid=(tall // step,),
        in_specs=[VMEM] * (3 + len(powers)),
        out_specs=pl.BlockSpec((channels, step, broad), lambda i: (0, i, 0)),
        out_shape=jax.ShapeDtypeStruct((channels, tall, broad), F32),
        scratch_shapes=[pltpu.VMEM((pairs, 8, LANES), F32)],
        compiler_params=params(14),
        cost_estimate=cost(40 * KERNELS * channels * tall * broad, 8 * own.size),
        name="score_cells",
    )(own, halo, clips, *powers)


def shards(across_table, down_table, pieces, beam, destination, clip_tenths):
    count = lax.axis_size("sky")
    links = lax.axis_size("freq")
    piece_count, channels = pieces.shape[:2]
    me = lax.axis_index("sky").astype(jnp.int32).reshape(1)
    across = jnp.asarray(across_table)
    down = jnp.asarray(down_table)

    def neighbours(block):
        low = lax.ppermute(block, "freq", [(i, i + 1) for i in range(links - 1)])
        high = lax.ppermute(block, "freq", [(i + 1, i) for i in range(links - 1)])
        return low, high

    strip = LANES // count
    parts = pieces.reshape(piece_count, channels, count, strip, LANES)
    beams = beam.reshape(piece_count, count, strip, LANES)
    packed = pack(me, destination, parts, beams)
    arrived = [exchange(block, "sky", k) for k, block in enumerate(packed, 1)]
    total, cover = gather_own(me, destination, parts, beams)
    strips = combine(me, total, cover, arrived, piece_count)
    last = count - 1
    halo = [neighbours(strips[0])]
    opposite, *halo[0] = lax.optimization_barrier((strips[last], *halo[0]))
    tiles = [strips[0]] + [exchange(strips[k], "sky", k) for k in range(1, last)]
    tiles.append(exchange(opposite, "sky", last))
    halo += [neighbours(tile) for tile in tiles[1:last]]
    flat = [block for pair in halo for block in pair]
    final, *flat = lax.optimization_barrier((tiles[last], *flat))
    halo = [flat[2 * k : 2 * k + 2] for k in range(last)] + [neighbours(final)]
    own = smooth(me, tiles, down, across)
    low, high = zip(*halo)
    sides, power = smooth_power(me, own, low, high, down, across)
    powers = [power] + [exchange(power, "sky", k) for k in range(1, count)]
    clips = jnp.repeat(clip_tenths.astype(F32).reshape(-1), channels)
    clips = jnp.broadcast_to(clips[:, None], power.shape)
    cells = float(count * ROWB * LANES * COLB * LANES)
    return score(own, sides, clips, powers, cells)


def solution(mesh):
    count = mesh.shape["sky"]
    body = functools.partial(
        shards, across_matrices(COLB * LANES), down_matrices(count, ROWB * LANES // count)
    )
    return jax.shard_map(
        body,
        mesh=mesh,
        in_specs=(P("sky", "freq", None, None), P("sky", None, None), P("sky"), P()),
        out_specs=P("freq", "sky", None),
        check_vma=False,
    )
```

time: 101 us -> 101 us (level)
  starting transfers between devices: 30.5 us -> 35 us
  local copies, waits for them, and re-layouts: 8.36 us -> 5.3 us
  Pallas kernels: 25.2 us -> 23.3 us
    ppermute x4 -> x8, starting transfers between devices: 16.5 us -> 26.3 us  [the longest x4 18.6 us: neighbours(): low = lax.ppermute(block, 'freq', [(i, i + 1) for i in range(links - 1)])]
    ppermute x15 -> x9, starting transfers between devices: 14 us -> 8.74 us  [exchange(): return lax.ppermute(block, axis, [(i, i ^ k) for i in range(count)])]
    unnamed x22 -> x16, local copies, waits for them, and re-layouts: 8.05 us -> 4.99 us
    pallas_call x10 -> x6, Pallas kernels: 25.2 us -> 23.3 us  [the longest x1 8.54 us: smooth_power(): pl.pallas_call(functools.partial(power_kernel, len(low)), in_specs=[SMEM]...]
    ppermute x15 -> x9, waiting for transfers between devices: 33.1 us -> 33.7 us  [exchange(): return lax.ppermute(block, axis, [(i, i ^ k) for i in range(count)])]
    ppermute x4 -> x8, waiting for transfers between devices: 3.31 us -> 3.53 us  [the longest x4 3.52 us: neighbours(): high = lax.ppermute(block, 'freq', [(i + 1, i) for i in range(links - 1)])]
  transfers between devices with their start and end apart: 19 -> 17, of which waited for: 11 -> 7; matrix products, arithmetic and copies ran while one was open for 0% -> 0% of each run, Pallas kernels for 6% -> 3%
where the time goes in v3:
time: 101 us
  waiting for transfers between devices  37.2 us (37%)
  starting transfers between devices  35 us (35%)
  Pallas kernels  23.3 us (23%)
  local copies, waits for them, and re-layouts  5.3 us (5%)
    ppermute x9, waiting for transfers between devices, exchange(): return lax.ppermute(block, axis, [(i, i ^ k) for i in range(count)])  33.7 us
    ppermute x4, starting transfers between devices, neighbours(): low = lax.ppermute(block, 'freq', [(i, i + 1) for i in range(links - 1)])  18.6 us
    ppermute x9, starting transfers between devices, exchange(): return lax.ppermute(block, axis, [(i, i ^ k) for i in range(count)])  8.74 us
    pallas_call x1, Pallas kernels, smooth_power(): pl.pallas_call(functools.partial(power_kernel, len(low)), in_specs=[SMEM]...  8.54 us
    ppermute x4, starting transfers between devices, neighbours(): high = lax.ppermute(block, 'freq', [(i + 1, i) for i in range(links - 1)])  7.68 us
    pallas_call x1, Pallas kernels, score(): pl.pallas_call(functools.partial(score_kernel, len(powers), cells), grid=...  6.88 us
    unnamed x16, local copies, waits for them, and re-layouts  4.99 us
    ppermute x4, waiting for transfers between devices, neighbours(): high = lax.ppermute(block, 'freq', [(i + 1, i) for i in range(links - 1)])  3.52 us
  transfers between devices with their start and end apart: 17, of which 7 were waited for; matrix products, arithmetic and copies ran while one was open for 0% of the time, Pallas kernels for 3%

profile of v3, /device:TPU:1, one launch (start us, length us, event | category | flops | bytes accessed | tf_op | source)
XLA Modules:
  0.0 101.1 jit_solution(7142351636338726551)
XLA Ops:
  0.0 3.3 %pack_pieces.1 = (bf16[73,32,128]{2,1,0:T(8,128)(2,1)}, bf16[73,32,128]{2,1,0:T(8,128)(2,1)}, bf16[73,32,128]{2,1,0:T(8,128)(2,1)}) custom-call(s32[1]{0:T(128)} %bitcast.me_ref, s32[8]{0:T(128)} %owner_ref.3, bf16[8,8,4,32,128]{4,3,2,1,0:T(8,128)(2,1)} %bitcast.3, bf16[8,4,32,128]{3,2,1,0:T(8,128)(2,1)} %bitcast.5), custom_call_target="tpu_custom_call" | custom-call | flops 1048576 | bytes 4194304 | tf_op jit(solution)/shard_map/pack_pieces/pallas_call | solution.py:126
  3.3 2.1 %collective-permute-start = (bf16[73,32,128]{2,1,0:T(8,128)(2,1)}, bf16[73,32,128]{2,1,0:T(8,128)(2,1)S(1)}, u32[]{:S(2)}, u32[]{:S(2)}) collective-permute-start(bf16[73,32,128]{2,1,0:T(8,128)(2,1)} %get-tuple-element.28), channel_id=1, source_target_pairs={{0,8},{8,0},{16,24},{24,16},{1,9},{9,1},{17,25},{25,17},{2,10},{10... | collective-permute-start | bytes 1794056 | tf_op jit(solution)/shard_map/ppermute | solution.py:75
  5.4 1.2 %collective-permute-start.1 = (bf16[73,32,128]{2,1,0:T(8,128)(2,1)}, bf16[73,32,128]{2,1,0:T(8,128)(2,1)S(1)}, u32[]{:S(2)}, u32[]{:S(2)}) collective-permute-start(bf16[73,32,128]{2,1,0:T(8,128)(2,1)} %get-tuple-element.29), channel_id=1, source_target_pairs={{0,16},{8,24},{16,0},{24,8},{1,17},{9,25},{17,1},{25,9},{2,18},{10... | collective-permute-start | bytes 1794056 | tf_op jit(solution)/shard_map/ppermute | solution.py:75
  6.6 0.0 collective-permute-start.2
  6.7 1.0 gather_own.1
  7.6 0.0 copy-start.5
  7.7 0.0 copy-start.6
  7.7 11.2 %collective-permute-done.refs_0_ = bf16[73,32,128]{2,1,0:T(8,128)(2,1)S(1)} collective-permute-done((bf16[73,32,128]{2,1,0:T(8,128)(2,1)}, bf16[73,32,128]{2,1,0:T(8,128)(2,1)S(1)}, u32[]{:S(2)}, u32[]{:S(2)}) %collective-permute-start) | collective-permute-done | bytes 598048 | tf_op jit(solution)/shard_map/ppermute | solution.py:75
  18.8 0.8 collective-permute-done.1.refs_1_
  19.7 12.9 %collective-permute-done.2.refs_2_ = bf16[73,32,128]{2,1,0:T(8,128)(2,1)S(1)} collective-permute-done((bf16[73,32,128]{2,1,0:T(8,128)(2,1)}, bf16[73,32,128]{2,1,0:T(8,128)(2,1)S(1)}, u32[]{:S(2)}, u32[]{:S(2)}) %collective-permute-start.2) | collective-permute-done | bytes 598048 | tf_op jit(solution)/shard_map/ppermute | solution.py:75
  32.6 1.4 %combine_strips.1 = (bf16[10,32,512]{2,1,0:T(8,128)(2,1)S(1)}, bf16[10,32,512]{2,1,0:T(8,128)(2,1)S(1)}, bf16[10,32,512]{2,1,0:T(8,128)(2,1)S(1)}, bf16[8,32,512]{2,1,0:T(8,128)(2,1)S(1)}) custom-call(s32[1]{0:T(128)} %bitcast.me_ref, f32[16,8,32,128]{3,2,1,0:T(8,128)S(1)} %get-tuple-element.26.total_in, f32[16,32,128]{2,1,0:T(8,128)S(1)} %get-tuple-element.27.cover_in, ...), custom_call_target="tpu_custom_call" | custom-call | flops 1 | bytes 1 | tf_op jit(solution)/shard_map/combine_strips/pallas_call | solution.py:249
  34.0 0.4 collective-permute-start.4
  34.4 1.1 %collective-permute-start.3 = (bf16[10,32,512]{2,1,0:T(8,128)(2,1)S(1)}, bf16[10,32,512]{2,1,0:T(8,128)(2,1)S(1)}, u32[]{:S(2)}, u32[]{:S(2)}) collective-permute-start(bf16[10,32,512]{2,1,0:T(8,128)(2,1)S(1)} %get-tuple-element.32), channel_id=1, source_target_pairs={{0,8},{8,0},{16,24},{24,16},{1,9},{9,1},{17,25},{25,17},{2,10},{10... | collective-permute-start | bytes 983048 | tf_op jit(solution)/shard_map/ppermute | solution.py:75
  35.5 5.5 %collective-permute-start.5 = (bf16[10,32,512]{2,1,0:T(8,128)(2,1)S(1)}, bf16[10,32,512]{2,1,0:T(8,128)(2,1)S(1)}, u32[]{:S(2)}, u32[]{:S(2)}) collective-permute-start(bf16[10,32,512]{2,1,0:T(8,128)(2,1)S(1)} %get-tuple-element.31.refs_0_), channel_id=1, source_target_pairs={{0,1},{1,2},{2,3},{3,4},{4,5},{5,6},{6,7},{8,9},{9,10},{10,11},{11... | collective-permute-start | bytes 983048 | tf_op jit(solution)/shard_map/ppermute | solution.py:489
  41.0 1.9 %collective-permute-start.6 = (bf16[10,32,512]{2,1,0:T(8,128)(2,1)S(1)}, bf16[10,32,512]{2,1,0:T(8,128)(2,1)S(1)}, u32[]{:S(2)}, u32[]{:S(2)}) collective-permute-start(bf16[10,32,512]{2,1,0:T(8,128)(2,1)S(1)} %get-tuple-element.31.refs_0_), channel_id=1, source_target_pairs={{1,0},{2,1},{3,2},{4,3},{5,4},{6,5},{7,6},{9,8},{10,9},{11,10},{12... | collective-permute-start | bytes 983048 | tf_op jit(solution)/shard_map/ppermute | solution.py:490
  42.9 0.0 collective-permute-done.4.refs_2_
  42.9 4.4 %collective-permute-start.10 = (bf16[10,32,512]{2,1,0:T(8,128)(2,1)S(1)}, bf16[10,32,512]{2,1,0:T(8,128)(2,1)S(1)}, u32[]{:S(2)}, u32[]{:S(2)}) collective-permute-start(bf16[10,32,512]{2,1,0:T(8,128)(2,1)S(1)} %collective-permute-done.4.refs_2_), channel_id=1, source_target_pairs={{0,1},{1,2},{2,3},{3,4},{4,5},{5,6},{6,7},{8,9},{9,10},{10,11},{11... | collective-permute-start | bytes 983048 | tf_op jit(solution)/shard_map/ppermute | solution.py:489
  47.3 1.9 %collective-permute-start.11 = (bf16[10,32,512]{2,1,0:T(8,128)(2,1)S(1)}, bf16[10,32,512]{2,1,0:T(8,128)(2,1)S(1)}, u32[]{:S(2)}, u32[]{:S(2)}) collective-permute-start(bf16[10,32,512]{2,1,0:T(8,128)(2,1)S(1)} %collective-permute-done.4.refs_2_), channel_id=1, source_target_pairs={{1,0},{2,1},{3,2},{4,3},{5,4},{6,5},{7,6},{9,8},{10,9},{11,10},{12... | collective-permute-start | bytes 983048 | tf_op jit(solution)/shard_map/ppermute | solution.py:490
  49.2 0.0 collective-permute-done.3.refs_1_
  49.2 3.6 %collective-permute-start.8 = (bf16[10,32,512]{2,1,0:T(8,128)(2,1)S(1)}, bf16[10,32,512]{2,1,0:T(8,128)(2,1)S(1)}, u32[]{:S(2)}, u32[]{:S(2)}) collective-permute-start(bf16[10,32,512]{2,1,0:T(8,128)(2,1)S(1)} %collective-permute-done.3.refs_1_), channel_id=1, source_target_pairs={{0,1},{1,2},{2,3},{3,4},{4,5},{5,6},{6,7},{8,9},{9,10},{10,11},{11... | collective-permute-start | bytes 983048 | tf_op jit(solution)/shard_map/ppermute | solution.py:489
  52.9 0.0 collective-permute-done.5.refs_0_
  52.9 1.9 %collective-permute-start.9 = (bf16[10,32,512]{2,1,0:T(8,128)(2,1)S(1)}, bf16[10,32,512]{2,1,0:T(8,128)(2,1)S(1)}, u32[]{:S(2)}, u32[]{:S(2)}) collective-permute-start(bf16[10,32,512]{2,1,0:T(8,128)(2,1)S(1)} %collective-permute-done.3.refs_1_), channel_id=1, source_target_pairs={{1,0},{2,1},{3,2},{4,3},{5,4},{6,5},{7,6},{9,8},{10,9},{11,10},{12... | collective-permute-start | bytes 983048 | tf_op jit(solution)/shard_map/ppermute | solution.py:490
  54.8 0.0 collective-permute-done.6.refs_4_
  54.8 1.2 %collective-permute-start.7 = (bf16[8,32,512]{2,1,0:T(8,128)(2,1)S(1)}, bf16[8,32,512]{2,1,0:T(8,128)(2,1)S(1)}, u32[]{:S(2)}, u32[]{:S(2)}) collective-permute-start(bf16[8,32,512]{2,1,0:T(8,128)(2,1)S(1)} %get-tuple-element.35), channel_id=1, source_target_pairs={{0,24},{8,16},{16,8},{24,0},{1,25},{9,17},{17,9},{25,1},{2,26},{10... | collective-permute-start | bytes 786440 | tf_op jit(solution)/shard_map/ppermute | solution.py:75
  56.1 6.4 %collective-permute-done.7.refs_3_ = bf16[8,32,512]{2,1,0:T(8,128)(2,1)S(1)} collective-permute-done((bf16[8,32,512]{2,1,0:T(8,128)(2,1)S(1)}, bf16[8,32,512]{2,1,0:T(8,128)(2,1)S(1)}, u32[]{:S(2)}, u32[]{:S(2)}) %collective-permute-start.7) | collective-permute-done | bytes 262176 | tf_op jit(solution)/shard_map/ppermute | solution.py:75
  62.5 0.0 collective-permute-done.10.refs_2_
  62.5 0.0 collective-permute-done.11.refs_6_
  62.5 0.0 collective-permute-done.8.refs_1_
  62.5 5.2 %collective-permute-start.12 = (bf16[8,32,512]{2,1,0:T(8,128)(2,1)S(1)}, bf16[8,32,512]{2,1,0:T(8,128)(2,1)S(1)}, u32[]{:S(2)}, u32[]{:S(2)}) collective-permute-start(bf16[8,32,512]{2,1,0:T(8,128)(2,1)S(1)} %collective-permute-done.7.refs_3_), channel_id=1, source_target_pairs={{0,1},{1,2},{2,3},{3,4},{4,5},{5,6},{6,7},{8,9},{9,10},{10,11},{11... | collective-permute-start | bytes 786440 | tf_op jit(solution)/shard_map/ppermute | solution.py:489
  67.6 1.9 %collective-permute-start.13 = (bf16[8,32,512]{2,1,0:T(8,128)(2,1)S(1)}, bf16[8,32,512]{2,1,0:T(8,128)(2,1)S(1)}, u32[]{:S(2)}, u32[]{:S(2)}) collective-permute-start(bf16[8,32,512]{2,1,0:T(8,128)(2,1)S(1)} %collective-permute-done.7.refs_3_), channel_id=1, source_target_pairs={{1,0},{2,1},{3,2},{4,3},{5,4},{6,5},{7,6},{9,8},{10,9},{11,10},{12... | collective-permute-start | bytes 786440 | tf_op jit(solution)/shard_map/ppermute | solution.py:490
  69.6 2.2 %smooth_own.1.own = bf16[3,8,128,512]{3,2,1,0:T(8,128)(2,1)S(1)} custom-call(s32[1]{0:T(128)} %bitcast.me_ref, bf16[4,384,144]{2,1,0:T(8,128)(2,1)S(1)} %copy-done.6, bf16[3,3,256,256]{3,2,1,0:T(8,128)(2,1)S(1)} %copy-done.5, bf16[10,32,512]{2,1,0:T(8,128)(2,1)S(1)} %get-tuple-element.31.refs_0_, bf16[10,32,512]{2,1,0:T(8,128)(2,1)S(1)} %collective-permute-done.3.refs_1_, ...), custom_call_target="tpu_custom_call" | custom-call | flops 2415919104 | bytes 6291456 | tf_op jit(solution)/shard_map/smooth_own/pallas_call | solution.py:332
  71.8 0.0 copy-start.7
  71.8 0.0 collective-permute-done.12.refs_3_
  71.8 3.5 %collective-permute-done.13.refs_7_ = bf16[8,32,512]{2,1,0:T(8,128)(2,1)S(1)} collective-permute-done((bf16[8,32,512]{2,1,0:T(8,128)(2,1)S(1)}, bf16[8,32,512]{2,1,0:T(8,128)(2,1)S(1)}, u32[]{:S(2)}, u32[]{:S(2)}) %collective-permute-start.13) | collective-permute-done | bytes 262176 | tf_op jit(solution)/shard_map/ppermute | solution.py:490
  75.3 8.5 %smooth_power.1 = (bf16[3,14,128,512]{3,2,1,0:T(8,128)(2,1)S(1)}, f32[96,128]{1,0:T(8,128)S(1)}) custom-call(s32[1]{0:T(128)} %bitcast.me_ref, bf16[4,384,144]{2,1,0:T(8,128)(2,1)S(1)} %copy-done.6, bf16[3,3,256,256]{3,2,1,0:T(8,128)(2,1)S(1)} %copy-done.5, bf16[3,8,128,512]{3,2,1,0:T(8,128)(2,1)S(1)} %smooth_own.1.own, ...), custom_call_target="tpu_custom_call" | custom-call | flops 4227858432 | bytes 22020096 | tf_op jit(solution)/shard_map/smooth_power/pallas_call | solution.py:408
  83.9 2.4 %copy-done.1 = bf16[3,14,128,512]{3,2,1,0:T(8,128)(2,1)} copy-done((bf16[3,14,128,512]{3,2,1,0:T(8,128)(2,1)}, bf16[3,14,128,512]{3,2,1,0:T(8,128)(2,1)S(1)}, u32[]{:S(2)}) %copy-start.1) | copy-done | bytes 5505048
  86.3 1.2 %collective-permute-start.14 = (f32[96,128]{1,0:T(8,128)S(1)}, f32[96,128]{1,0:T(8,128)S(1)}, u32[]{:S(2)}, u32[]{:S(2)}) collective-permute-start(f32[96,128]{1,0:T(8,128)S(1)} %get-tuple-element.46.refs_0_), channel_id=1, source_target_pairs={{0,8},{8,0},{16,24},{24,16},{1,9},{9,1},{17,25},{25,17},{2,10},{10... | collective-permute-start | bytes 147464 | tf_op jit(solution)/shard_map/ppermute | solution.py:75
  87.4 0.3 collective-permute-start.15
  87.7 1.2 %collective-permute-start.16 = (f32[96,128]{1,0:T(8,128)S(1)}, f32[96,128]{1,0:T(8,128)S(1)}, u32[]{:S(2)}, u32[]{:S(2)}) collective-permute-start(f32[96,128]{1,0:T(8,128)S(1)} %get-tuple-element.46.refs_0_), channel_id=1, source_target_pairs={{0,24},{8,16},{16,8},{24,0},{1,25},{9,17},{17,9},{25,1},{2,26},{10... | collective-permute-start | bytes 147464 | tf_op jit(solution)/shard_map/ppermute | solution.py:75
  88.9 0.1 reshape.16
  89.0 0.1 broadcast_in_dim.10
  89.1 0.1 broadcast_in_dim.11
  89.2 0.0 collective-permute-done.14.refs_1_
  89.2 1.2 %collective-permute-done.15.refs_2_ = f32[96,128]{1,0:T(8,128)S(1)} collective-permute-done((f32[96,128]{1,0:T(8,128)S(1)}, f32[96,128]{1,0:T(8,128)S(1)}, u32[]{:S(2)}, u32[]{:S(2)}) %collective-permute-start.15) | collective-permute-done | bytes 49184 | tf_op jit(solution)/shard_map/ppermute | solution.py:75
  90.4 1.2 %collective-permute-done.16.refs_3_ = f32[96,128]{1,0:T(8,128)S(1)} collective-permute-done((f32[96,128]{1,0:T(8,128)S(1)}, f32[96,128]{1,0:T(8,128)S(1)}, u32[]{:S(2)}, u32[]{:S(2)}) %collective-permute-start.16) | collective-permute-done | bytes 49184 | tf_op jit(solution)/shard_map/ppermute | solution.py:75
  91.5 0.1 broadcast_in_dim.12.clips
  91.6 2.6 %copy-done.2 = bf16[3,14,128,512]{3,2,1,0:T(8,128)(2,1)S(1)} copy-done((bf16[3,14,128,512]{3,2,1,0:T(8,128)(2,1)S(1)}, bf16[3,14,128,512]{3,2,1,0:T(8,128)(2,1)}, u32[]{:S(2)}) %copy-start.2) | copy-done | bytes 5505048
  94.2 6.9 %score_cells.1 = f32[8,128,512]{2,1,0:T(8,128)} custom-call(bf16[3,8,128,512]{3,2,1,0:T(8,128)(2,1)S(1)} %smooth_own.1.own, bf16[3,14,128,512]{3,2,1,0:T(8,128)(2,1)S(1)} %copy-done.2, f32[96,128]{1,0:T(8,128)S(1)} %broadcast_in_dim.12.clips, f32[96,128]{1,0:T(8,128)S(1)} %get-tuple-element.46.refs_0_, f32[96,128]{1,0:T(8,128)S(1)} %collective-permute-done.14.refs_1_, ...), custom_call_target="tpu_custom_call" | custom-call | flops 62914560 | bytes 12582912 | tf_op jit(solution)/shard_map/score_cells/pallas_call | solution.py:467
  (13 shorter events, 0.0 us)
Async XLA Ops:
  0.0 6.6 %copy-start = (bf16[8,8,128,128]{3,2,1,0:T(8,128)(2,1)S(1)}, bf16[8,8,128,128]{3,2,1,0:T(8,128)(2,1)}, u32[]{:S(2)}) copy-start(bf16[8,8,128,128]{3,2,1,0:T(8,128)(2,1)} %param.6) | copy-start | bytes 6291460
  0.0 6.7 %copy-start.3 = (bf16[8,128,128]{2,1,0:T(8,128)(2,1)S(1)}, bf16[8,128,128]{2,1,0:T(8,128)(2,1)}, u32[]{:S(2)}) copy-start(bf16[8,128,128]{2,1,0:T(8,128)(2,1)} %param.7) | copy-start | bytes 786436
  0.0 6.7 %copy-start.4 = (s32[8]{0:T(128)S(1)}, s32[8]{0:T(128)}, u32[]{:S(2)}) copy-start(s32[8]{0:T(128)} %owner_ref.3) | copy-start | bytes 100
  3.3 15.5 %collective-permute-start = (bf16[73,32,128]{2,1,0:T(8,128)(2,1)}, bf16[73,32,128]{2,1,0:T(8,128)(2,1)S(1)}, u32[]{:S(2)}, u32[]{:S(2)}) collective-permute-start(bf16[73,32,128]{2,1,0:T(8,128)(2,1)} %get-tuple-element.28), channel_id=1, source_target_pairs={{0,8},{8,0},{16,24},{24,16},{1,9},{9,1},{17,25},{25,17},{2,10},{10... | collective-permute-start | bytes 1794056 | tf_op jit(solution)/shard_map/ppermute | solution.py:75
  5.4 14.3 %collective-permute-start.1 = (bf16[73,32,128]{2,1,0:T(8,128)(2,1)}, bf16[73,32,128]{2,1,0:T(8,128)(2,1)S(1)}, u32[]{:S(2)}, u32[]{:S(2)}) collective-permute-start(bf16[73,32,128]{2,1,0:T(8,128)(2,1)} %get-tuple-element.29), channel_id=1, source_target_pairs={{0,16},{8,24},{16,0},{24,8},{1,17},{9,25},{17,1},{25,9},{2,18},{10... | collective-permute-start | bytes 1794056 | tf_op jit(solution)/shard_map/ppermute | solution.py:75
  6.6 25.9 %collective-permute-start.2 = (bf16[73,32,128]{2,1,0:T(8,128)(2,1)}, bf16[73,32,128]{2,1,0:T(8,128)(2,1)S(1)}, u32[]{:S(2)}, u32[]{:S(2)}) collective-permute-start(bf16[73,32,128]{2,1,0:T(8,128)(2,1)} %get-tuple-element.30), channel_id=1, source_target_pairs={{0,24},{8,16},{16,8},{24,0},{1,25},{9,17},{17,9},{25,1},{2,26},{10... | collective-permute-start | bytes 1794056 | tf_op jit(solution)/shard_map/ppermute | solution.py:75
  7.6 61.9 %copy-start.5 = (bf16[3,3,256,256]{3,2,1,0:T(8,128)(2,1)S(1)}, bf16[3,3,256,256]{3,2,1,0:T(8,128)(2,1)}, u32[]{:S(2)}) copy-start(bf16[3,3,256,256]{3,2,1,0:T(8,128)(2,1)} %constant.9.clone.across) | copy-start | bytes 3538948
  7.7 61.9 %copy-start.6 = (bf16[4,384,144]{2,1,0:T(8,128)(2,1)S(1)}, bf16[4,384,144]{2,1,0:T(8,128)(2,1)}, u32[]{:S(2)}) copy-start(bf16[4,384,144]{2,1,0:T(8,128)(2,1)} %constant.10.clone.down) | copy-start | bytes 1327108
  34.0 8.9 %collective-permute-start.4 = (bf16[10,32,512]{2,1,0:T(8,128)(2,1)S(1)}, bf16[10,32,512]{2,1,0:T(8,128)(2,1)S(1)}, u32[]{:S(2)}, u32[]{:S(2)}) collective-permute-start(bf16[10,32,512]{2,1,0:T(8,128)(2,1)S(1)} %get-tuple-element.33), channel_id=1, source_target_pairs={{0,16},{8,24},{16,0},{24,8},{1,17},{9,25},{17,1},{25,9},{2,18},{10... | collective-permute-start | bytes 983048 | tf_op jit(solution)/shard_map/ppermute | solution.py:75
  34.4 14.8 %collective-permute-start.3 = (bf16[10,32,512]{2,1,0:T(8,128)(2,1)S(1)}, bf16[10,32,512]{2,1,0:T(8,128)(2,1)S(1)}, u32[]{:S(2)}, u32[]{:S(2)}) collective-permute-start(bf16[10,32,512]{2,1,0:T(8,128)(2,1)S(1)} %get-tuple-element.32), channel_id=1, source_target_pairs={{0,8},{8,0},{16,24},{24,16},{1,9},{9,1},{17,25},{25,17},{2,10},{10... | collective-permute-start | bytes 983048 | tf_op jit(solution)/shard_map/ppermute | solution.py:75
  35.5 17.4 %collective-permute-start.5 = (bf16[10,32,512]{2,1,0:T(8,128)(2,1)S(1)}, bf16[10,32,512]{2,1,0:T(8,128)(2,1)S(1)}, u32[]{:S(2)}, u32[]{:S(2)}) collective-permute-start(bf16[10,32,512]{2,1,0:T(8,128)(2,1)S(1)} %get-tuple-element.31.refs_0_), channel_id=1, source_target_pairs={{0,1},{1,2},{2,3},{3,4},{4,5},{5,6},{6,7},{8,9},{9,10},{10,11},{11... | collective-permute-start | bytes 983048 | tf_op jit(solution)/shard_map/ppermute | solution.py:489
  41.0 13.8 %collective-permute-start.6 = (bf16[10,32,512]{2,1,0:T(8,128)(2,1)S(1)}, bf16[10,32,512]{2,1,0:T(8,128)(2,1)S(1)}, u32[]{:S(2)}, u32[]{:S(2)}) collective-permute-start(bf16[10,32,512]{2,1,0:T(8,128)(2,1)S(1)} %get-tuple-element.31.refs_0_), channel_id=1, source_target_pairs={{1,0},{2,1},{3,2},{4,3},{5,4},{6,5},{7,6},{9,8},{10,9},{11,10},{12... | collective-permute-start | bytes 983048 | tf_op jit(solution)/shard_map/ppermute | solution.py:490
  42.9 19.5 %collective-permute-start.10 = (bf16[10,32,512]{2,1,0:T(8,128)(2,1)S(1)}, bf16[10,32,512]{2,1,0:T(8,128)(2,1)S(1)}, u32[]{:S(2)}, u32[]{:S(2)}) collective-permute-start(bf16[10,32,512]{2,1,0:T(8,128)(2,1)S(1)} %collective-permute-done.4.refs_2_), channel_id=1, source_target_pairs={{0,1},{1,2},{2,3},{3,4},{4,5},{5,6},{6,7},{8,9},{9,10},{10,11},{11... | collective-permute-start | bytes 983048 | tf_op jit(solution)/shard_map/ppermute | solution.py:489
  47.3 15.2 %collective-permute-start.11 = (bf16[10,32,512]{2,1,0:T(8,128)(2,1)S(1)}, bf16[10,32,512]{2,1,0:T(8,128)(2,1)S(1)}, u32[]{:S(2)}, u32[]{:S(2)}) collective-permute-start(bf16[10,32,512]{2,1,0:T(8,128)(2,1)S(1)} %collective-permute-done.4.refs_2_), channel_id=1, source_target_pairs={{1,0},{2,1},{3,2},{4,3},{5,4},{6,5},{7,6},{9,8},{10,9},{11,10},{12... | collective-permute-start | bytes 983048 | tf_op jit(solution)/shard_map/ppermute | solution.py:490
  49.2 13.2 %collective-permute-start.8 = (bf16[10,32,512]{2,1,0:T(8,128)(2,1)S(1)}, bf16[10,32,512]{2,1,0:T(8,128)(2,1)S(1)}, u32[]{:S(2)}, u32[]{:S(2)}) collective-permute-start(bf16[10,32,512]{2,1,0:T(8,128)(2,1)S(1)} %collective-permute-done.3.refs_1_), channel_id=1, source_target_pairs={{0,1},{1,2},{2,3},{3,4},{4,5},{5,6},{6,7},{8,9},{9,10},{10,11},{11... | collective-permute-start | bytes 983048 | tf_op jit(solution)/shard_map/ppermute | solution.py:489
  52.9 9.6 %collective-permute-start.9 = (bf16[10,32,512]{2,1,0:T(8,128)(2,1)S(1)}, bf16[10,32,512]{2,1,0:T(8,128)(2,1)S(1)}, u32[]{:S(2)}, u32[]{:S(2)}) collective-permute-start(bf16[10,32,512]{2,1,0:T(8,128)(2,1)S(1)} %collective-permute-done.3.refs_1_), channel_id=1, source_target_pairs={{1,0},{2,1},{3,2},{4,3},{5,4},{6,5},{7,6},{9,8},{10,9},{11,10},{12... | collective-permute-start | bytes 983048 | tf_op jit(solution)/shard_map/ppermute | solution.py:490
  54.8 7.6 %collective-permute-start.7 = (bf16[8,32,512]{2,1,0:T(8,128)(2,1)S(1)}, bf16[8,32,512]{2,1,0:T(8,128)(2,1)S(1)}, u32[]{:S(2)}, u32[]{:S(2)}) collective-permute-start(bf16[8,32,512]{2,1,0:T(8,128)(2,1)S(1)} %get-tuple-element.35), channel_id=1, source_target_pairs={{0,24},{8,16},{16,8},{24,0},{1,25},{9,17},{17,9},{25,1},{2,26},{10... | collective-permute-start | bytes 786440 | tf_op jit(solution)/shard_map/ppermute | solution.py:75
  62.5 9.3 %collective-permute-start.12 = (bf16[8,32,512]{2,1,0:T(8,128)(2,1)S(1)}, bf16[8,32,512]{2,1,0:T(8,128)(2,1)S(1)}, u32[]{:S(2)}, u32[]{:S(2)}) collective-permute-start(bf16[8,32,512]{2,1,0:T(8,128)(2,1)S(1)} %collective-permute-done.7.refs_3_), channel_id=1, source_target_pairs={{0,1},{1,2},{2,3},{3,4},{4,5},{5,6},{6,7},{8,9},{9,10},{10,11},{11... | collective-permute-start | bytes 786440 | tf_op jit(solution)/shard_map/ppermute | solution.py:489
  67.6 7.7 %collective-permute-start.13 = (bf16[8,32,512]{2,1,0:T(8,128)(2,1)S(1)}, bf16[8,32,512]{2,1,0:T(8,128)(2,1)S(1)}, u32[]{:S(2)}, u32[]{:S(2)}) collective-permute-start(bf16[8,32,512]{2,1,0:T(8,128)(2,1)S(1)} %collective-permute-done.7.refs_3_), channel_id=1, source_target_pairs={{1,0},{2,1},{3,2},{4,3},{5,4},{6,5},{7,6},{9,8},{10,9},{11,10},{12... | collective-permute-start | bytes 786440 | tf_op jit(solution)/shard_map/ppermute | solution.py:490
  71.8 17.1 %copy-start.7 = (s32[3,4]{1,0:T(4,128)S(1)}, s32[3,4]{1,0:T(4,128)}, u32[]{:S(2)}) copy-start(s32[3,4]{1,0:T(4,128)} %param.9) | copy-start | bytes 148
  83.9 2.4 %copy-start.1 = (bf16[3,14,128,512]{3,2,1,0:T(8,128)(2,1)}, bf16[3,14,128,512]{3,2,1,0:T(8,128)(2,1)S(1)}, u32[]{:S(2)}) copy-start(bf16[3,14,128,512]{3,2,1,0:T(8,128)(2,1)S(1)} %get-tuple-element.45.halo) | copy-start | bytes 16515076
  86.3 2.9 %collective-permute-start.14 = (f32[96,128]{1,0:T(8,128)S(1)}, f32[96,128]{1,0:T(8,128)S(1)}, u32[]{:S(2)}, u32[]{:S(2)}) collective-permute-start(f32[96,128]{1,0:T(8,128)S(1)} %get-tuple-element.46.refs_0_), channel_id=1, source_target_pairs={{0,8},{8,0},{16,24},{24,16},{1,9},{9,1},{17,25},{25,17},{2,10},{10... | collective-permute-start | bytes 147464 | tf_op jit(solution)/shard_map/ppermute | solution.py:75
  87.4 2.9 %collective-permute-start.15 = (f32[96,128]{1,0:T(8,128)S(1)}, f32[96,128]{1,0:T(8,128)S(1)}, u32[]{:S(2)}, u32[]{:S(2)}) collective-permute-start(f32[96,128]{1,0:T(8,128)S(1)} %get-tuple-element.46.refs_0_), channel_id=1, source_target_pairs={{0,16},{8,24},{16,0},{24,8},{1,17},{9,25},{17,1},{25,9},{2,18},{10... | collective-permute-start | bytes 147464 | tf_op jit(solution)/shard_map/ppermute | solution.py:75
  87.7 3.8 %collective-permute-start.16 = (f32[96,128]{1,0:T(8,128)S(1)}, f32[96,128]{1,0:T(8,128)S(1)}, u32[]{:S(2)}, u32[]{:S(2)}) collective-permute-start(f32[96,128]{1,0:T(8,128)S(1)} %get-tuple-element.46.refs_0_), channel_id=1, source_target_pairs={{0,24},{8,16},{16,8},{24,0},{1,25},{9,17},{17,9},{25,1},{2,26},{10... | collective-permute-start | bytes 147464 | tf_op jit(solution)/shard_map/ppermute | solution.py:75
  91.6 2.6 %copy-start.2 = (bf16[3,14,128,512]{3,2,1,0:T(8,128)(2,1)S(1)}, bf16[3,14,128,512]{3,2,1,0:T(8,128)(2,1)}, u32[]{:S(2)}) copy-start(bf16[3,14,128,512]{3,2,1,0:T(8,128)(2,1)} %copy-done.1) | copy-start | bytes 16515076

commit v4 on v3

--- a/solution.py
+++ b/solution.py
@@ -264,33 +264,64 @@
     )(me, total, cover, *parts)
 
 
-def tile_plane(me, strips, channels, c):
-    count = len(strips)
+def edge_rows(me, strips, channels, c):
+    count = len(strips) + 1
     strip, broad = strips[0].shape[1:]
     above = jnp.zeros((RIM, broad), F32)
     below = jnp.zeros((RIM, broad), F32)
     plane, row = divmod(c * RIM, strip)
-    for k, part in enumerate(strips[:-1]):
+    for k, part in enumerate(strips):
         rim = part[channels + plane].astype(F32)[row : row + RIM]
         source = me ^ k
         above = jnp.where(source == count - 1, rim, above)
         below = jnp.where(source == 0, rim, below)
-    if strip % 16 == 0:
-        edges = jnp.concatenate([above, below], axis=0).astype(BF16)
-        return jnp.concatenate([part[c] for part in strips] + [edges], axis=0)
-    wide = [part[c].astype(F32) for part in strips]
-    return jnp.concatenate(wide + [above, below], axis=0).astype(BF16)
-
-
-def smooth_planes(me, strips, chosen, down, across, middle, out, base):
+    return [above, below]
+
+
+def stack_rows(parts):
+    if all(part.shape[0] % 16 == 0 for part in parts):
+        return jnp.concatenate(parts, axis=0)
+    return jnp.concatenate([part.astype(F32) for part in parts], axis=0).astype(BF16)
+
+
+def join_kernel(me_ref, *refs):
+    strips, (lower, upper) = refs[:-2], refs[-2:]
+    me = me_ref[0]
+    channels = strips[0].shape[0] - upper_rim_planes(strips[0].shape[1], strips[0].shape[0])
+    for c in range(channels):
+        edges = jnp.concatenate(edge_rows(me, strips, channels, c), axis=0).astype(BF16)
+        plane = stack_rows([part[c] for part in strips] + [edges])
+        if c < EDGE:
+            lower[c] = plane
+        if c >= channels - EDGE:
+            upper[c - (channels - EDGE)] = plane
+
+
+def upper_rim_planes(strip, planes):
+    return planes * RIM // (strip + RIM)
+
+
+def join(me, strips):
+    _, strip, broad = strips[0].shape
+    out = jax.ShapeDtypeStruct((EDGE, len(strips) * strip + 2 * RIM, broad), BF16)
+    return pl.pallas_call(
+        join_kernel,
+        in_specs=[SMEM] + [VMEM] * len(strips),
+        out_specs=[VMEM] * 2,
+        out_shape=[out] * 2,
+        compiler_params=params(16),
+        cost_estimate=cost(1, 1),
+        name="join_strips",
+    )(me, *strips)
+
+
+def smooth_planes(planes, down, across, middle, out, base):
     tall = down.shape[0] // KERNELS
-    broad = strips[0].shape[2]
-    channels = strips[-1].shape[0]
+    broad = across.shape[2] * 2
     half = broad // 2
-    at = len(chosen)
-    for i, c in enumerate(chosen):
-        plane = tile_plane(me, strips, channels, c)
-        found = jnp.dot(down[...], plane, preferred_element_type=F32).astype(BF16)
+    at = len(planes)
+    for i, plane in enumerate(planes):
+        found = jnp.dot(down[...], plane(), preferred_element_type=F32).astype(BF16)
         for k in range(KERNELS):
             middle[k, i * tall : (i + 1) * tall] = found[k * tall : (k + 1) * tall]
     chunks = -(-at // 4)
@@ -321,7 +352,14 @@
 def smooth_kernel(count, me_ref, down, across, *refs):
     strips, (out, middle) = refs[:count], refs[count:]
     me = me_ref[0]
-    smooth_planes(me, strips, range(out.shape[1]), down.at[me], across, middle, out, 0)
+    channels = out.shape[1]
+
+    def plane(c):
+        edges = jnp.concatenate(edge_rows(me, strips[:-1], channels, c), axis=0).astype(BF16)
+        return stack_rows([part[c] for part in strips] + [edges])
+
+    planes = [functools.partial(plane, c) for c in range(channels)]
+    smooth_planes(planes, down.at[me], across, middle, out, 0)
 
 
 def smooth(me, strips, down, across):
@@ -370,13 +408,25 @@
     return order
 
 
-def power_kernel(count, me_ref, down, across, own, *refs):
-    low, high = refs[:count], refs[count : 2 * count]
-    halo, power, middle, sums = refs[2 * count :]
+def power_kernel(me_ref, down, across, own, low, low_last, high, high_last, halo, power, middle, sums):
     channels, tall, broad = own.shape[1:]
     me = me_ref[0]
-    smooth_planes(me, low, range(channels - EDGE, channels), down.at[me], across, middle, halo, 0)
-    smooth_planes(me, high, range(EDGE), down.at[me], across, middle, halo, EDGE)
+    for joined, last, first, base in (
+        (low, low_last, channels - EDGE, 0),
+        (high, high_last, 0, EDGE),
+    ):
+
+        def plane(c, joined=joined, last=last, first=first):
+            rows = joined[c]
+            body = rows.shape[0] - 2 * RIM
+            if last.shape[1] % 16 == 0:
+                return jnp.concatenate([rows[:body], last[first + c], rows[body:]], axis=0)
+            rows = rows.astype(F32)
+            middle_rows = last[first + c].astype(F32)
+            return jnp.concatenate([rows[:body], middle_rows, rows[body:]], axis=0).astype(BF16)
+
+        planes = [functools.partial(plane, c) for c in range(EDGE)]
+        smooth_planes(planes, down.at[me], across, middle, halo, base)
     layers = (own, halo)
     order = layer_order(channels)
     sums[...] = jnp.zeros_like(sums)
@@ -401,13 +451,13 @@
     power[...] = jnp.broadcast_to(total, power.shape)
 
 
-def smooth_power(me, own, low, high, down, across):
+def smooth_power(me, own, sides, down, across):
     _, channels, tall, broad = own.shape
     pairs = KERNELS * WIDTHS * channels
     halo = jax.ShapeDtypeStruct((KERNELS, 2 * EDGE, tall, broad), BF16)
     return pl.pallas_call(
-        functools.partial(power_kernel, len(low)),
-        in_specs=[SMEM] + [VMEM] * (3 + len(low) + len(high)),
+        power_kernel,
+        in_specs=[SMEM] + [VMEM] * (3 + len(sides)),
         out_specs=[VMEM] * 2,
         out_shape=[halo, jax.ShapeDtypeStruct((pairs, LANES), F32)],
         scratch_shapes=[
@@ -417,7 +467,7 @@
         compiler_params=params(24),
         cost_estimate=cost(2 * halo.size * (broad + 256), 8 * halo.size),
         name="smooth_power",
-    )(me, down, across, own, *low, *high)
+    )(me, down, across, own, *sides)
 
 
 def score_kernel(count, cells, own, halo, clips, *refs):
@@ -431,8 +481,12 @@
         total = powers[0][...]
         for item in powers[1:]:
             total = total + item[...]
-        scale = 10.0 / (clips[...] * jnp.sqrt(total / cells + EPSILON))
-        factor[...] = jnp.broadcast_to(scale[:, None], factor.shape)
+        noise = jnp.sqrt(total / cells + EPSILON)
+        for k in range(KERNELS):
+            for w in range(WIDTHS):
+                rows = slice((k * WIDTHS + w) * channels, (k * WIDTHS + w + 1) * channels)
+                scale = 10.0 / (clips[k, w].astype(F32) * noise[rows])
+                factor[rows] = jnp.broadcast_to(scale[:, None], (channels,) + factor.shape[1:])
 
     lane_groups = broad // LANES
     base = pl.program_id(0) * step_rows
@@ -467,7 +521,7 @@
     return pl.pallas_call(
         functools.partial(score_kernel, len(powers), cells),
         grid=(tall // step,),
-        in_specs=[VMEM] * (3 + len(powers)),
+        in_specs=[VMEM, VMEM, SMEM] + [VMEM] * len(powers),
         out_specs=pl.BlockSpec((channels, step, broad), lambda i: (0, i, 0)),
         out_shape=jax.ShapeDtypeStruct((channels, tall, broad), F32),
         scratch_shapes=[pltpu.VMEM((pairs, 8, LANES), F32)],
@@ -485,11 +539,6 @@
     across = jnp.asarray(across_table)
     down = jnp.asarray(down_table)
 
-    def neighbours(block):
-        low = lax.ppermute(block, "freq", [(i, i + 1) for i in range(links - 1)])
-        high = lax.ppermute(block, "freq", [(i + 1, i) for i in range(links - 1)])
-        return low, high
-
     strip = LANES // count
     parts = pieces.reshape(piece_count, channels, count, strip, LANES)
     beams = beam.reshape(piece_count, count, strip, LANES)
@@ -497,23 +546,21 @@
     arrived = [exchange(block, "sky", k) for k, block in enumerate(packed, 1)]
     total, cover = gather_own(me, destination, parts, beams)
     strips = combine(me, total, cover, arrived, piece_count)
-    last = count - 1
-    halo = [neighbours(strips[0])]
-    opposite, *halo[0] = lax.optimization_barrier((strips[last], *halo[0]))
-    tiles = [strips[0]] + [exchange(strips[k], "sky", k) for k in range(1, last)]
-    tiles.append(exchange(opposite, "sky", last))
-    halo += [neighbours(tile) for tile in tiles[1:last]]
-    flat = [block for pair in halo for block in pair]
-    final, *flat = lax.optimization_barrier((tiles[last], *flat))
-    halo = [flat[2 * k : 2 * k + 2] for k in range(last)] + [neighbours(final)]
+    tiles = [strips[0]] + [exchange(strips[k], "sky", k) for k in range(1, count)]
+    upward = [(i, i + 1) for i in range(links - 1)]
+    downward = [(i + 1, i) for i in range(links - 1)]
+    lower, upper = join(me, tiles[:-1])
+    sides = [
+        lax.ppermute(upper, "freq", upward),
+        lax.ppermute(tiles[-1], "freq", upward),
+        lax.ppermute(lower, "freq", downward),
+        lax.ppermute(tiles[-1], "freq", downward),
+    ]
     own = smooth(me, tiles, down, across)
-    low, high = zip(*halo)
-    sides, power = smooth_power(me, own, low, high, down, across)
+    halo, power = smooth_power(me, own, sides, down, across)
     powers = [power] + [exchange(power, "sky", k) for k in range(1, count)]
-    clips = jnp.repeat(clip_tenths.astype(F32).reshape(-1), channels)
-    clips = jnp.broadcast_to(clips[:, None], power.shape)
     cells = float(count * ROWB * LANES * COLB * LANES)
-    return score(own, sides, clips, powers, cells)
+    return score(own, halo, clip_tenths, powers, cells)
 
 
 def solution(mesh):

time: 101 us -> 90.8 us (0.90); the launches traced: 101 us -> 89.1 us
  starting transfers between devices: 35 us -> 23.2 us
  local copies, waits for them, and re-layouts: 5.3 us -> 0.02 us
  waiting for transfers between devices: 37.2 us -> 41.6 us
    ppermute x8 -> x4, starting transfers between devices: 26.3 us -> 15.4 us  [the longest x1 5.84 us: shards(): lax.ppermute(upper, 'freq', upward)]
    ppermute x9, waiting for transfers between devices: 33.7 us -> 40.6 us  [exchange(): return lax.ppermute(block, axis, [(i, i ^ k) for i in range(count)])]
    unnamed x16 -> x12, local copies, waits for them, and re-layouts: 4.99 us -> 0.02 us
    ppermute x8 -> x4, waiting for transfers between devices: 3.53 us -> 1.05 us  [the longest x1 1.04 us: shards(): lax.ppermute(tiles[-1], 'freq', upward)]
    pallas_call x1 -> x2, Pallas kernels: 8.54 us -> 8.67 us  [the longest x1 8.56 us: smooth_power(): pl.pallas_call(power_kernel, in_specs=[SMEM] + [VMEM] * (3 + len(sides)),...]
  transfers between devices with their start and end apart: 17 -> 13, of which waited for: 7 -> 9; matrix products, arithmetic and copies ran while one was open for 0% -> 0% of each run, Pallas kernels for 3% -> 4%
where the time goes in v4:
time: 90.8 us; the launch traced here: 89.1 us
  waiting for transfers between devices  41.6 us (46%)
  Pallas kernels  24.1 us (27%)
  starting transfers between devices  23.2 us (26%)
    ppermute x9, waiting for transfers between devices, exchange(): return lax.ppermute(block, axis, [(i, i ^ k) for i in range(count)])  40.6 us
    pallas_call x1, Pallas kernels, smooth_power(): pl.pallas_call(power_kernel, in_specs=[SMEM] + [VMEM] * (3 + len(sides)),...  8.56 us
    ppermute x9, starting transfers between devices, exchange(): return lax.ppermute(block, axis, [(i, i ^ k) for i in range(count)])  7.84 us
    pallas_call x1, Pallas kernels, score(): pl.pallas_call(functools.partial(score_kernel, len(powers), cells), grid=...  7.56 us
    ppermute x1, starting transfers between devices, shards(): lax.ppermute(upper, 'freq', upward)  5.84 us
    ppermute x1, starting transfers between devices, shards(): lax.ppermute(tiles[-1], 'freq', upward)  5.7 us
    pallas_call x1, Pallas kernels, pack(): pl.pallas_call(functools.partial(pack_kernel, count), in_specs=[SMEM, SME...  3.26 us
    pallas_call x1, Pallas kernels, smooth(): pl.pallas_call(functools.partial(smooth_kernel, len(strips)), in_specs=[S...  2.2 us
  transfers between devices with their start and end apart: 13, of which 9 were waited for; matrix products, arithmetic and copies ran while one was open for 0% of the time, Pallas kernels for 4%

profile of v4, /device:TPU:1, one launch (start us, length us, event | category | flops | bytes accessed | tf_op | source)
XLA Modules:
  0.0 89.1 jit_solution(7781199229798456045)
XLA Ops:
  0.0 0.0 copy-start.3
  0.0 0.0 copy-start.1
  0.0 0.0 copy-start
  0.0 3.3 %pack_pieces.1 = (bf16[73,32,128]{2,1,0:T(8,128)(2,1)}, bf16[73,32,128]{2,1,0:T(8,128)(2,1)}, bf16[73,32,128]{2,1,0:T(8,128)(2,1)}) custom-call(s32[1]{0:T(128)} %bitcast.me_ref, s32[8]{0:T(128)} %owner_ref.3, bf16[8,8,4,32,128]{4,3,2,1,0:T(8,128)(2,1)} %bitcast.3, bf16[8,4,32,128]{3,2,1,0:T(8,128)(2,1)} %bitcast.5), custom_call_target="tpu_custom_call" | custom-call | flops 1048576 | bytes 4194304 | tf_op jit(solution)/shard_map/pack_pieces/pallas_call | solution.py:126
  3.3 2.1 %collective-permute-start = (bf16[73,32,128]{2,1,0:T(8,128)(2,1)}, bf16[73,32,128]{2,1,0:T(8,128)(2,1)S(1)}, u32[]{:S(2)}, u32[]{:S(2)}) collective-permute-start(bf16[73,32,128]{2,1,0:T(8,128)(2,1)} %get-tuple-element.20), channel_id=1, source_target_pairs={{0,8},{8,0},{16,24},{24,16},{1,9},{9,1},{17,25},{25,17},{2,10},{10... | collective-permute-start | bytes 1794056 | tf_op jit(solution)/shard_map/ppermute | solution.py:75
  5.4 1.2 %collective-permute-start.1 = (bf16[73,32,128]{2,1,0:T(8,128)(2,1)}, bf16[73,32,128]{2,1,0:T(8,128)(2,1)S(1)}, u32[]{:S(2)}, u32[]{:S(2)}) collective-permute-start(bf16[73,32,128]{2,1,0:T(8,128)(2,1)} %get-tuple-element.21), channel_id=1, source_target_pairs={{0,16},{8,24},{16,0},{24,8},{1,17},{9,25},{17,1},{25,9},{2,18},{10... | collective-permute-start | bytes 1794056 | tf_op jit(solution)/shard_map/ppermute | solution.py:75
  6.6 0.0 collective-permute-start.2
  6.6 0.0 copy-done.3
  6.7 0.0 copy-done.1
  6.7 0.0 copy-done
  6.7 1.0 %gather_own.1 = (f32[16,8,32,128]{3,2,1,0:T(8,128)S(1)}, f32[16,32,128]{2,1,0:T(8,128)S(1)}) custom-call(s32[1]{0:T(128)} %bitcast.me_ref, s32[8]{0:T(128)S(1)} %copy-done.3, bf16[8,8,4,32,128]{4,3,2,1,0:T(8,128)(2,1)S(1)} %bitcast.4, bf16[8,4,32,128]{3,2,1,0:T(8,128)(2,1)S(1)} %bitcast.6), custom_call_target="tpu_custom_call" | custom-call | flops 1048576 | bytes 4194304 | tf_op jit(solution)/shard_map/gather_own/pallas_call | solution.py:164
  7.6 11.2 %collective-permute-done.refs_0_ = bf16[73,32,128]{2,1,0:T(8,128)(2,1)S(1)} collective-permute-done((bf16[73,32,128]{2,1,0:T(8,128)(2,1)}, bf16[73,32,128]{2,1,0:T(8,128)(2,1)S(1)}, u32[]{:S(2)}, u32[]{:S(2)}) %collective-permute-start) | collective-permute-done | bytes 598048 | tf_op jit(solution)/shard_map/ppermute | solution.py:75
  18.8 0.8 collective-permute-done.1.refs_1_
  19.7 12.9 %collective-permute-done.2.refs_2_ = bf16[73,32,128]{2,1,0:T(8,128)(2,1)S(1)} collective-permute-done((bf16[73,32,128]{2,1,0:T(8,128)(2,1)}, bf16[73,32,128]{2,1,0:T(8,128)(2,1)S(1)}, u32[]{:S(2)}, u32[]{:S(2)}) %collective-permute-start.2) | collective-permute-done | bytes 598048 | tf_op jit(solution)/shard_map/ppermute | solution.py:75
  32.6 0.0 copy-start.4
  32.6 0.0 copy-start.5
  32.6 1.4 %combine_strips.1 = (bf16[10,32,512]{2,1,0:T(8,128)(2,1)S(1)}, bf16[10,32,512]{2,1,0:T(8,128)(2,1)S(1)}, bf16[10,32,512]{2,1,0:T(8,128)(2,1)S(1)}, bf16[8,32,512]{2,1,0:T(8,128)(2,1)S(1)}) custom-call(s32[1]{0:T(128)} %bitcast.me_ref, f32[16,8,32,128]{3,2,1,0:T(8,128)S(1)} %get-tuple-element.18.total_in, f32[16,32,128]{2,1,0:T(8,128)S(1)} %get-tuple-element.19.cover_in, ...), custom_call_target="tpu_custom_call" | custom-call | flops 1 | bytes 1 | tf_op jit(solution)/shard_map/combine_strips/pallas_call | solution.py:249
  34.0 1.2 %collective-permute-start.3 = (bf16[10,32,512]{2,1,0:T(8,128)(2,1)S(1)}, bf16[10,32,512]{2,1,0:T(8,128)(2,1)S(1)}, u32[]{:S(2)}, u32[]{:S(2)}) collective-permute-start(bf16[10,32,512]{2,1,0:T(8,128)(2,1)S(1)} %get-tuple-element.24), channel_id=1, source_target_pairs={{0,8},{8,0},{16,24},{24,16},{1,9},{9,1},{17,25},{25,17},{2,10},{10... | collective-permute-start | bytes 983048 | tf_op jit(solution)/shard_map/ppermute | solution.py:75
  35.2 0.3 collective-permute-start.4
  35.5 6.0 %collective-permute-done.3.refs_1_ = bf16[10,32,512]{2,1,0:T(8,128)(2,1)S(1)} collective-permute-done((bf16[10,32,512]{2,1,0:T(8,128)(2,1)S(1)}, bf16[10,32,512]{2,1,0:T(8,128)(2,1)S(1)}, u32[]{:S(2)}, u32[]{:S(2)}) %collective-permute-start.3) | collective-permute-done | bytes 327712 | tf_op jit(solution)/shard_map/ppermute | solution.py:75
  41.5 1.1 %collective-permute-done.4.refs_2_ = bf16[10,32,512]{2,1,0:T(8,128)(2,1)S(1)} collective-permute-done((bf16[10,32,512]{2,1,0:T(8,128)(2,1)S(1)}, bf16[10,32,512]{2,1,0:T(8,128)(2,1)S(1)}, u32[]{:S(2)}, u32[]{:S(2)}) %collective-permute-start.4) | collective-permute-done | bytes 327712 | tf_op jit(solution)/shard_map/ppermute | solution.py:75
  42.6 0.1 join_strips.1
  42.7 5.8 %collective-permute-start.6 = (bf16[7,112,512]{2,1,0:T(8,128)(2,1)S(1)}, bf16[7,112,512]{2,1,0:T(8,128)(2,1)S(1)}, u32[]{:S(2)}, u32[]{:S(2)}) collective-permute-start(bf16[7,112,512]{2,1,0:T(8,128)(2,1)S(1)} %get-tuple-element.27), channel_id=1, source_target_pairs={{0,1},{1,2},{2,3},{3,4},{4,5},{5,6},{6,7},{8,9},{9,10},{10,11},{11... | collective-permute-start | bytes 2408456 | tf_op jit(solution)/shard_map/ppermute | solution.py:554
  48.6 1.9 %collective-permute-start.8 = (bf16[7,112,512]{2,1,0:T(8,128)(2,1)S(1)}, bf16[7,112,512]{2,1,0:T(8,128)(2,1)S(1)}, u32[]{:S(2)}, u32[]{:S(2)}) collective-permute-start(bf16[7,112,512]{2,1,0:T(8,128)(2,1)S(1)} %get-tuple-element.28), channel_id=1, source_target_pairs={{1,0},{2,1},{3,2},{4,3},{5,4},{6,5},{7,6},{9,8},{10,9},{11,10},{12... | collective-permute-start | bytes 2408456 | tf_op jit(solution)/shard_map/ppermute | solution.py:556
  50.5 0.3 collective-permute-start.5
  50.8 6.8 %collective-permute-done.5.refs_3_ = bf16[8,32,512]{2,1,0:T(8,128)(2,1)S(1)} collective-permute-done((bf16[8,32,512]{2,1,0:T(8,128)(2,1)S(1)}, bf16[8,32,512]{2,1,0:T(8,128)(2,1)S(1)}, u32[]{:S(2)}, u32[]{:S(2)}) %collective-permute-start.5) | collective-permute-done | bytes 262176 | tf_op jit(solution)/shard_map/ppermute | solution.py:75
  57.6 1.9 %collective-permute-start.9 = (bf16[8,32,512]{2,1,0:T(8,128)(2,1)S(1)}, bf16[8,32,512]{2,1,0:T(8,128)(2,1)S(1)}, u32[]{:S(2)}, u32[]{:S(2)}) collective-permute-start(bf16[8,32,512]{2,1,0:T(8,128)(2,1)S(1)} %collective-permute-done.5.refs_3_), channel_id=1, source_target_pairs={{1,0},{2,1},{3,2},{4,3},{5,4},{6,5},{7,6},{9,8},{10,9},{11,10},{12... | collective-permute-start | bytes 786440 | tf_op jit(solution)/shard_map/ppermute | solution.py:557
  59.5 5.7 %collective-permute-start.7 = (bf16[8,32,512]{2,1,0:T(8,128)(2,1)S(1)}, bf16[8,32,512]{2,1,0:T(8,128)(2,1)S(1)}, u32[]{:S(2)}, u32[]{:S(2)}) collective-permute-start(bf16[8,32,512]{2,1,0:T(8,128)(2,1)S(1)} %collective-permute-done.5.refs_3_), channel_id=1, source_target_pairs={{0,1},{1,2},{2,3},{3,4},{4,5},{5,6},{6,7},{8,9},{9,10},{10,11},{11... | collective-permute-start | bytes 786440 | tf_op jit(solution)/shard_map/ppermute | solution.py:555
  65.2 0.0 copy-done.4
  65.2 0.0 copy-done.5
  65.2 2.2 %smooth_own.1.own = bf16[3,8,128,512]{3,2,1,0:T(8,128)(2,1)S(1)} custom-call(s32[1]{0:T(128)} %bitcast.me_ref, bf16[4,384,144]{2,1,0:T(8,128)(2,1)S(1)} %copy-done.5, bf16[3,3,256,256]{3,2,1,0:T(8,128)(2,1)S(1)} %copy-done.4, bf16[10,32,512]{2,1,0:T(8,128)(2,1)S(1)} %get-tuple-element.23.refs_0_, bf16[10,32,512]{2,1,0:T(8,128)(2,1)S(1)} %collective-permute-done.3.refs_1_, ...), custom_call_target="tpu_custom_call" | custom-call | flops 2415919104 | bytes 6291456 | tf_op jit(solution)/shard_map/smooth_own/pallas_call | solution.py:370
  67.4 0.0 copy-start.2
  67.5 0.0 collective-permute-done.9.high_last
  67.5 1.0 %collective-permute-done.7.low_last = bf16[8,32,512]{2,1,0:T(8,128)(2,1)S(1)} collective-permute-done((bf16[8,32,512]{2,1,0:T(8,128)(2,1)S(1)}, bf16[8,32,512]{2,1,0:T(8,128)(2,1)S(1)}, u32[]{:S(2)}, u32[]{:S(2)}) %collective-permute-start.7) | collective-permute-done | bytes 262176 | tf_op jit(solution)/shard_map/ppermute | solution.py:555
  68.5 0.0 collective-permute-done.6.low
  68.5 0.0 collective-permute-done.8.high
  68.5 8.6 %smooth_power.1 = (bf16[3,14,128,512]{3,2,1,0:T(8,128)(2,1)S(1)}, f32[96,128]{1,0:T(8,128)S(1)}) custom-call(s32[1]{0:T(128)} %bitcast.me_ref, bf16[4,384,144]{2,1,0:T(8,128)(2,1)S(1)} %copy-done.5, bf16[3,3,256,256]{3,2,1,0:T(8,128)(2,1)S(1)} %copy-done.4, bf16[3,8,128,512]{3,2,1,0:T(8,128)(2,1)S(1)} %smooth_own.1.own, ...), custom_call_target="tpu_custom_call" | custom-call | flops 4227858432 | bytes 22020096 | tf_op jit(solution)/shard_map/smooth_power/pallas_call | solution.py:458
  77.1 0.3 collective-permute-start.12
  77.3 1.2 %collective-permute-start.11 = (f32[96,128]{1,0:T(8,128)S(1)}, f32[96,128]{1,0:T(8,128)S(1)}, u32[]{:S(2)}, u32[]{:S(2)}) collective-permute-start(f32[96,128]{1,0:T(8,128)S(1)} %get-tuple-element.30.refs_0_), channel_id=1, source_target_pairs={{0,16},{8,24},{16,0},{24,8},{1,17},{9,25},{17,1},{25,9},{2,18},{10... | collective-permute-start | bytes 147464 | tf_op jit(solution)/shard_map/ppermute | solution.py:75
  78.6 1.2 %collective-permute-start.10 = (f32[96,128]{1,0:T(8,128)S(1)}, f32[96,128]{1,0:T(8,128)S(1)}, u32[]{:S(2)}, u32[]{:S(2)}) collective-permute-start(f32[96,128]{1,0:T(8,128)S(1)} %get-tuple-element.30.refs_0_), channel_id=1, source_target_pairs={{0,8},{8,0},{16,24},{24,16},{1,9},{9,1},{17,25},{25,17},{2,10},{10... | collective-permute-start | bytes 147464 | tf_op jit(solution)/shard_map/ppermute | solution.py:75
  79.7 1.2 %collective-permute-done.12.refs_3_ = f32[96,128]{1,0:T(8,128)S(1)} collective-permute-done((f32[96,128]{1,0:T(8,128)S(1)}, f32[96,128]{1,0:T(8,128)S(1)}, u32[]{:S(2)}, u32[]{:S(2)}) %collective-permute-start.12) | collective-permute-done | bytes 49184 | tf_op jit(solution)/shard_map/ppermute | solution.py:75
  80.9 0.0 collective-permute-done.11.refs_2_
  80.9 0.6 collective-permute-done.10.refs_1_
  81.5 0.0 copy-done.2
  81.5 7.6 %score_cells.1 = f32[8,128,512]{2,1,0:T(8,128)} custom-call(bf16[3,8,128,512]{3,2,1,0:T(8,128)(2,1)S(1)} %smooth_own.1.own, bf16[3,14,128,512]{3,2,1,0:T(8,128)(2,1)S(1)} %get-tuple-element.29.halo, s32[3,4]{1,0:T(4,128)S(1)} %copy-done.2, f32[96,128]{1,0:T(8,128)S(1)} %get-tuple-element.30.refs_0_, f32[96,128]{1,0:T(8,128)S(1)} %collective-permute-done.10.refs_1_, ...), custom_call_target="tpu_custom_call" | custom-call | flops 62914560 | bytes 12582912 | tf_op jit(solution)/shard_map/score_cells/pallas_call | solution.py:521
Async XLA Ops:
  0.0 6.6 %copy-start.3 = (s32[8]{0:T(128)S(1)}, s32[8]{0:T(128)}, u32[]{:S(2)}) copy-start(s32[8]{0:T(128)} %owner_ref.3) | copy-start | bytes 100
  0.0 6.7 %copy-start.1 = (bf16[8,128,128]{2,1,0:T(8,128)(2,1)S(1)}, bf16[8,128,128]{2,1,0:T(8,128)(2,1)}, u32[]{:S(2)}) copy-start(bf16[8,128,128]{2,1,0:T(8,128)(2,1)} %param.7) | copy-start | bytes 786436
  0.0 6.7 %copy-start = (bf16[8,8,128,128]{3,2,1,0:T(8,128)(2,1)S(1)}, bf16[8,8,128,128]{3,2,1,0:T(8,128)(2,1)}, u32[]{:S(2)}) copy-start(bf16[8,8,128,128]{3,2,1,0:T(8,128)(2,1)} %param.6) | copy-start | bytes 6291460
  3.3 15.5 %collective-permute-start = (bf16[73,32,128]{2,1,0:T(8,128)(2,1)}, bf16[73,32,128]{2,1,0:T(8,128)(2,1)S(1)}, u32[]{:S(2)}, u32[]{:S(2)}) collective-permute-start(bf16[73,32,128]{2,1,0:T(8,128)(2,1)} %get-tuple-element.20), channel_id=1, source_target_pairs={{0,8},{8,0},{16,24},{24,16},{1,9},{9,1},{17,25},{25,17},{2,10},{10... | collective-permute-start | bytes 1794056 | tf_op jit(solution)/shard_map/ppermute | solution.py:75
  5.4 14.3 %collective-permute-start.1 = (bf16[73,32,128]{2,1,0:T(8,128)(2,1)}, bf16[73,32,128]{2,1,0:T(8,128)(2,1)S(1)}, u32[]{:S(2)}, u32[]{:S(2)}) collective-permute-start(bf16[73,32,128]{2,1,0:T(8,128)(2,1)} %get-tuple-element.21), channel_id=1, source_target_pairs={{0,16},{8,24},{16,0},{24,8},{1,17},{9,25},{17,1},{25,9},{2,18},{10... | collective-permute-start | bytes 1794056 | tf_op jit(solution)/shard_map/ppermute | solution.py:75
  6.6 25.9 %collective-permute-start.2 = (bf16[73,32,128]{2,1,0:T(8,128)(2,1)}, bf16[73,32,128]{2,1,0:T(8,128)(2,1)S(1)}, u32[]{:S(2)}, u32[]{:S(2)}) collective-permute-start(bf16[73,32,128]{2,1,0:T(8,128)(2,1)} %get-tuple-element.22), channel_id=1, source_target_pairs={{0,24},{8,16},{16,8},{24,0},{1,25},{9,17},{17,9},{25,1},{2,26},{10... | collective-permute-start | bytes 1794056 | tf_op jit(solution)/shard_map/ppermute | solution.py:75
  32.6 32.6 %copy-start.4 = (bf16[3,3,256,256]{3,2,1,0:T(8,128)(2,1)S(1)}, bf16[3,3,256,256]{3,2,1,0:T(8,128)(2,1)}, u32[]{:S(2)}) copy-start(bf16[3,3,256,256]{3,2,1,0:T(8,128)(2,1)} %constant.9.clone.across) | copy-start | bytes 3538948
  32.6 32.6 %copy-start.5 = (bf16[4,384,144]{2,1,0:T(8,128)(2,1)S(1)}, bf16[4,384,144]{2,1,0:T(8,128)(2,1)}, u32[]{:S(2)}) copy-start(bf16[4,384,144]{2,1,0:T(8,128)(2,1)} %constant.10.clone.down) | copy-start | bytes 1327108
  34.0 7.5 %collective-permute-start.3 = (bf16[10,32,512]{2,1,0:T(8,128)(2,1)S(1)}, bf16[10,32,512]{2,1,0:T(8,128)(2,1)S(1)}, u32[]{:S(2)}, u32[]{:S(2)}) collective-permute-start(bf16[10,32,512]{2,1,0:T(8,128)(2,1)S(1)} %get-tuple-element.24), channel_id=1, source_target_pairs={{0,8},{8,0},{16,24},{24,16},{1,9},{9,1},{17,25},{25,17},{2,10},{10... | collective-permute-start | bytes 983048 | tf_op jit(solution)/shard_map/ppermute | solution.py:75
  35.2 7.4 %collective-permute-start.4 = (bf16[10,32,512]{2,1,0:T(8,128)(2,1)S(1)}, bf16[10,32,512]{2,1,0:T(8,128)(2,1)S(1)}, u32[]{:S(2)}, u32[]{:S(2)}) collective-permute-start(bf16[10,32,512]{2,1,0:T(8,128)(2,1)S(1)} %get-tuple-element.25), channel_id=1, source_target_pairs={{0,16},{8,24},{16,0},{24,8},{1,17},{9,25},{17,1},{25,9},{2,18},{10... | collective-permute-start | bytes 983048 | tf_op jit(solution)/shard_map/ppermute | solution.py:75
  42.7 25.8 %collective-permute-start.6 = (bf16[7,112,512]{2,1,0:T(8,128)(2,1)S(1)}, bf16[7,112,512]{2,1,0:T(8,128)(2,1)S(1)}, u32[]{:S(2)}, u32[]{:S(2)}) collective-permute-start(bf16[7,112,512]{2,1,0:T(8,128)(2,1)S(1)} %get-tuple-element.27), channel_id=1, source_target_pairs={{0,1},{1,2},{2,3},{3,4},{4,5},{5,6},{6,7},{8,9},{9,10},{10,11},{11... | collective-permute-start | bytes 2408456 | tf_op jit(solution)/shard_map/ppermute | solution.py:554
  48.6 19.9 %collective-permute-start.8 = (bf16[7,112,512]{2,1,0:T(8,128)(2,1)S(1)}, bf16[7,112,512]{2,1,0:T(8,128)(2,1)S(1)}, u32[]{:S(2)}, u32[]{:S(2)}) collective-permute-start(bf16[7,112,512]{2,1,0:T(8,128)(2,1)S(1)} %get-tuple-element.28), channel_id=1, source_target_pairs={{1,0},{2,1},{3,2},{4,3},{5,4},{6,5},{7,6},{9,8},{10,9},{11,10},{12... | collective-permute-start | bytes 2408456 | tf_op jit(solution)/shard_map/ppermute | solution.py:556
  50.5 7.1 %collective-permute-start.5 = (bf16[8,32,512]{2,1,0:T(8,128)(2,1)S(1)}, bf16[8,32,512]{2,1,0:T(8,128)(2,1)S(1)}, u32[]{:S(2)}, u32[]{:S(2)}) collective-permute-start(bf16[8,32,512]{2,1,0:T(8,128)(2,1)S(1)} %get-tuple-element.26), channel_id=1, source_target_pairs={{0,24},{8,16},{16,8},{24,0},{1,25},{9,17},{17,9},{25,1},{2,26},{10... | collective-permute-start | bytes 786440 | tf_op jit(solution)/shard_map/ppermute | solution.py:75
  57.6 9.9 %collective-permute-start.9 = (bf16[8,32,512]{2,1,0:T(8,128)(2,1)S(1)}, bf16[8,32,512]{2,1,0:T(8,128)(2,1)S(1)}, u32[]{:S(2)}, u32[]{:S(2)}) collective-permute-start(bf16[8,32,512]{2,1,0:T(8,128)(2,1)S(1)} %collective-permute-done.5.refs_3_), channel_id=1, source_target_pairs={{1,0},{2,1},{3,2},{4,3},{5,4},{6,5},{7,6},{9,8},{10,9},{11,10},{12... | collective-permute-start | bytes 786440 | tf_op jit(solution)/shard_map/ppermute | solution.py:557
  59.5 9.0 %collective-permute-start.7 = (bf16[8,32,512]{2,1,0:T(8,128)(2,1)S(1)}, bf16[8,32,512]{2,1,0:T(8,128)(2,1)S(1)}, u32[]{:S(2)}, u32[]{:S(2)}) collective-permute-start(bf16[8,32,512]{2,1,0:T(8,128)(2,1)S(1)} %collective-permute-done.5.refs_3_), channel_id=1, source_target_pairs={{0,1},{1,2},{2,3},{3,4},{4,5},{5,6},{6,7},{8,9},{9,10},{10,11},{11... | collective-permute-start | bytes 786440 | tf_op jit(solution)/shard_map/ppermute | solution.py:555
  67.4 14.1 %copy-start.2 = (s32[3,4]{1,0:T(4,128)S(1)}, s32[3,4]{1,0:T(4,128)}, u32[]{:S(2)}) copy-start(s32[3,4]{1,0:T(4,128)} %clips.1) | copy-start | bytes 148
  77.1 3.9 %collective-permute-start.12 = (f32[96,128]{1,0:T(8,128)S(1)}, f32[96,128]{1,0:T(8,128)S(1)}, u32[]{:S(2)}, u32[]{:S(2)}) collective-permute-start(f32[96,128]{1,0:T(8,128)S(1)} %get-tuple-element.30.refs_0_), channel_id=1, source_target_pairs={{0,24},{8,16},{16,8},{24,0},{1,25},{9,17},{17,9},{25,1},{2,26},{10... | collective-permute-start | bytes 147464 | tf_op jit(solution)/shard_map/ppermute | solution.py:75
  77.3 3.6 %collective-permute-start.11 = (f32[96,128]{1,0:T(8,128)S(1)}, f32[96,128]{1,0:T(8,128)S(1)}, u32[]{:S(2)}, u32[]{:S(2)}) collective-permute-start(f32[96,128]{1,0:T(8,128)S(1)} %get-tuple-element.30.refs_0_), channel_id=1, source_target_pairs={{0,16},{8,24},{16,0},{24,8},{1,17},{9,25},{17,1},{25,9},{2,18},{10... | collective-permute-start | bytes 147464 | tf_op jit(solution)/shard_map/ppermute | solution.py:75
  78.6 2.9 %collective-permute-start.10 = (f32[96,128]{1,0:T(8,128)S(1)}, f32[96,128]{1,0:T(8,128)S(1)}, u32[]{:S(2)}, u32[]{:S(2)}) collective-permute-start(f32[96,128]{1,0:T(8,128)S(1)} %get-tuple-element.30.refs_0_), channel_id=1, source_target_pairs={{0,8},{8,0},{16,24},{24,16},{1,9},{9,1},{17,25},{25,17},{2,10},{10... | collective-permute-start | bytes 147464 | tf_op jit(solution)/shard_map/ppermute | solution.py:75

commit v5 on v4

--- a/solution.py
+++ b/solution.py
@@ -284,21 +284,20 @@
     return jnp.concatenate([part.astype(F32) for part in parts], axis=0).astype(BF16)
 
 
+def tile_plane(me, strips, channels, c):
+    edges = jnp.concatenate(edge_rows(me, strips[:-1], channels, c), axis=0).astype(BF16)
+    return stack_rows([part[c] for part in strips] + [edges])
+
+
 def join_kernel(me_ref, *refs):
     strips, (lower, upper) = refs[:-2], refs[-2:]
-    me = me_ref[0]
-    channels = strips[0].shape[0] - upper_rim_planes(strips[0].shape[1], strips[0].shape[0])
+    channels = strips[-1].shape[0]
     for c in range(channels):
-        edges = jnp.concatenate(edge_rows(me, strips, channels, c), axis=0).astype(BF16)
-        plane = stack_rows([part[c] for part in strips] + [edges])
+        plane = tile_plane(me_ref[0], strips, channels, c)
         if c < EDGE:
             lower[c] = plane
         if c >= channels - EDGE:
             upper[c - (channels - EDGE)] = plane
-
-
-def upper_rim_planes(strip, planes):
-    return planes * RIM // (strip + RIM)
 
 
 def join(me, strips):
@@ -354,11 +353,7 @@
     me = me_ref[0]
     channels = out.shape[1]
 
-    def plane(c):
-        edges = jnp.concatenate(edge_rows(me, strips[:-1], channels, c), axis=0).astype(BF16)
-        return stack_rows([part[c] for part in strips] + [edges])
-
-    planes = [functools.partial(plane, c) for c in range(channels)]
+    planes = [functools.partial(tile_plane, me, strips, channels, c) for c in range(channels)]
     smooth_planes(planes, down.at[me], across, middle, out, 0)
 
 
@@ -408,25 +403,11 @@
     return order
 
 
-def power_kernel(me_ref, down, across, own, low, low_last, high, high_last, halo, power, middle, sums):
+def power_kernel(me_ref, down, across, own, low, high, halo, power, middle, sums):
     channels, tall, broad = own.shape[1:]
-    me = me_ref[0]
-    for joined, last, first, base in (
-        (low, low_last, channels - EDGE, 0),
-        (high, high_last, 0, EDGE),
-    ):
-
-        def plane(c, joined=joined, last=last, first=first):
-            rows = joined[c]
-            body = rows.shape[0] - 2 * RIM
-            if last.shape[1] % 16 == 0:
-                return jnp.concatenate([rows[:body], last[first + c], rows[body:]], axis=0)
-            rows = rows.astype(F32)
-            middle_rows = last[first + c].astype(F32)
-            return jnp.concatenate([rows[:body], middle_rows, rows[body:]], axis=0).astype(BF16)
-
-        planes = [functools.partial(plane, c) for c in range(EDGE)]
-        smooth_planes(planes, down.at[me], across, middle, halo, base)
+    for side, base in ((low, 0), (high, EDGE)):
+        planes = [functools.partial(side.__getitem__, c) for c in range(EDGE)]
+        smooth_planes(planes, down.at[me_ref[0]], across, middle, halo, base)
     layers = (own, halo)
     order = layer_order(channels)
     sums[...] = jnp.zeros_like(sums)
@@ -495,20 +476,18 @@
         start = pl.multiple_of(step // lane_groups * 16, 16)
         rows = pl.ds(pl.multiple_of(base + start, 16), 16)
         lanes = pl.ds(pl.multiple_of(step % lane_groups * LANES, LANES), LANES)
-        for half in range(2):
-            best = [None] * channels
-            for k in range(KERNELS):
-
-                def load(i, k=k):
-                    array, plane = order[i]
-                    value = layers[array][k, plane, rows, lanes].astype(F32)
-                    return value[half * 8 : half * 8 + 8]
-
-                for w, c, value in boxcars(load, channels):
-                    value = jnp.abs(value) * factor[(k * WIDTHS + w) * channels + c]
-                    best[c] = value if best[c] is None else jnp.maximum(best[c], value)
-            for c in range(channels):
-                out[c, pl.ds(start + half * 8, 8), lanes] = best[c]
+        best = [None] * channels
+        for k in range(KERNELS):
+
+            def load(i, k=k):
+                array, plane = order[i]
+                return layers[array][k, plane, rows, lanes].astype(F32).reshape(2, 8, LANES)
+
+            for w, c, value in boxcars(load, channels):
+                value = jnp.abs(value) * factor[(k * WIDTHS + w) * channels + c]
+                best[c] = value if best[c] is None else jnp.maximum(best[c], value)
+        for c in range(channels):
+            out[c, pl.ds(start, 16), lanes] = best[c].reshape(16, LANES)
         return 0
 
     lax.fori_loop(0, step_rows // 16 * lane_groups, score, 0)
@@ -547,14 +526,10 @@
     total, cover = gather_own(me, destination, parts, beams)
     strips = combine(me, total, cover, arrived, piece_count)
     tiles = [strips[0]] + [exchange(strips[k], "sky", k) for k in range(1, count)]
-    upward = [(i, i + 1) for i in range(links - 1)]
-    downward = [(i + 1, i) for i in range(links - 1)]
-    lower, upper = join(me, tiles[:-1])
+    lower, upper = join(me, tiles)
     sides = [
-        lax.ppermute(upper, "freq", upward),
-        lax.ppermute(tiles[-1], "freq", upward),
-        lax.ppermute(lower, "freq", downward),
-        lax.ppermute(tiles[-1], "freq", downward),
+        lax.ppermute(upper, "freq", [(i, i + 1) for i in range(links - 1)]),
+        lax.ppermute(lower, "freq", [(i + 1, i) for i in range(links - 1)]),
     ]
     own = smooth(me, tiles, down, across)
     halo, power = smooth_power(me, own, sides, down, across)

time: 90.8 us -> 91 us (level); the launches traced: 89.1 us -> 90.9 us
  waiting for transfers between devices: 41.6 us -> 48.1 us
  starting transfers between devices: 23.2 us -> 18.4 us
    ppermute x4 -> x2, waiting for transfers between devices: 1.05 us -> 11.8 us  [the longest x1 7.38 us: shards(): lax.ppermute(upper, 'freq', [(i, i + 1) for i in range(links - 1)])]
    ppermute x4 -> x2, starting transfers between devices: 15.4 us -> 9.67 us  [the longest x1 7.75 us: shards(): lax.ppermute(upper, 'freq', [(i, i + 1) for i in range(links - 1)])]
    ppermute x9, waiting for transfers between devices: 40.6 us -> 36.3 us  [exchange(): return lax.ppermute(block, axis, [(i, i ^ k) for i in range(count)])]
  transfers between devices with their start and end apart: 13 -> 11, of which waited for: 9 -> 9; matrix products, arithmetic and copies ran while one was open for 0% -> 0% of each run, Pallas kernels for 4% -> 3%
where the time goes in v5:
time: 91 us; the launch traced here: 90.9 us
  waiting for transfers between devices  48.1 us (53%)
  Pallas kernels  24.2 us (27%)
  starting transfers between devices  18.4 us (20%)
    ppermute x9, waiting for transfers between devices, exchange(): return lax.ppermute(block, axis, [(i, i ^ k) for i in range(count)])  36.3 us
    ppermute x9, starting transfers between devices, exchange(): return lax.ppermute(block, axis, [(i, i ^ k) for i in range(count)])  8.74 us
    pallas_call x1, Pallas kernels, smooth_power(): pl.pallas_call(power_kernel, in_specs=[SMEM] + [VMEM] * (3 + len(sides)),...  8.56 us
    ppermute x1, starting transfers between devices, shards(): lax.ppermute(upper, 'freq', [(i, i + 1) for i in range(links - 1)])  7.75 us
    pallas_call x1, Pallas kernels, score(): pl.pallas_call(functools.partial(score_kernel, len(powers), cells), grid=...  7.68 us
    ppermute x1, waiting for transfers between devices, shards(): lax.ppermute(upper, 'freq', [(i, i + 1) for i in range(links - 1)])  7.38 us
    ppermute x1, waiting for transfers between devices, shards(): lax.ppermute(lower, 'freq', [(i + 1, i) for i in range(links - 1)])  4.4 us
    pallas_call x1, Pallas kernels, pack(): pl.pallas_call(functools.partial(pack_kernel, count), in_specs=[SMEM, SME...  3.26 us
  transfers between devices with their start and end apart: 11, of which 9 were waited for; matrix products, arithmetic and copies ran while one was open for 0% of the time, Pallas kernels for 3%

profile of v5, /device:TPU:1, one launch (start us, length us, event | category | flops | bytes accessed | tf_op | source)
XLA Modules:
  0.0 90.9 jit_solution(12352741631665142989)
XLA Ops:
  0.0 0.0 copy-start.3
  0.0 0.0 copy-start.1
  0.0 0.0 copy-start
  0.0 3.3 %pack_pieces.1 = (bf16[73,32,128]{2,1,0:T(8,128)(2,1)}, bf16[73,32,128]{2,1,0:T(8,128)(2,1)}, bf16[73,32,128]{2,1,0:T(8,128)(2,1)}) custom-call(s32[1]{0:T(128)} %bitcast.me_ref, s32[8]{0:T(128)} %owner_ref.3, bf16[8,8,4,32,128]{4,3,2,1,0:T(8,128)(2,1)} %bitcast.3, bf16[8,4,32,128]{3,2,1,0:T(8,128)(2,1)} %bitcast.5), custom_call_target="tpu_custom_call" | custom-call | flops 1048576 | bytes 4194304 | tf_op jit(solution)/shard_map/pack_pieces/pallas_call | solution.py:126
  3.3 2.1 %collective-permute-start = (bf16[73,32,128]{2,1,0:T(8,128)(2,1)}, bf16[73,32,128]{2,1,0:T(8,128)(2,1)S(1)}, u32[]{:S(2)}, u32[]{:S(2)}) collective-permute-start(bf16[73,32,128]{2,1,0:T(8,128)(2,1)} %get-tuple-element.20), channel_id=1, source_target_pairs={{0,8},{8,0},{16,24},{24,16},{1,9},{9,1},{17,25},{25,17},{2,10},{10... | collective-permute-start | bytes 1794056 | tf_op jit(solution)/shard_map/ppermute | solution.py:75
  5.4 1.2 %collective-permute-start.1 = (bf16[73,32,128]{2,1,0:T(8,128)(2,1)}, bf16[73,32,128]{2,1,0:T(8,128)(2,1)S(1)}, u32[]{:S(2)}, u32[]{:S(2)}) collective-permute-start(bf16[73,32,128]{2,1,0:T(8,128)(2,1)} %get-tuple-element.21), channel_id=1, source_target_pairs={{0,16},{8,24},{16,0},{24,8},{1,17},{9,25},{17,1},{25,9},{2,18},{10... | collective-permute-start | bytes 1794056 | tf_op jit(solution)/shard_map/ppermute | solution.py:75
  6.6 0.0 collective-permute-start.2
  6.6 0.0 copy-done.3
  6.7 0.0 copy-done.1
  6.7 0.0 copy-done
  6.7 1.0 %gather_own.1 = (f32[16,8,32,128]{3,2,1,0:T(8,128)S(1)}, f32[16,32,128]{2,1,0:T(8,128)S(1)}) custom-call(s32[1]{0:T(128)} %bitcast.me_ref, s32[8]{0:T(128)S(1)} %copy-done.3, bf16[8,8,4,32,128]{4,3,2,1,0:T(8,128)(2,1)S(1)} %bitcast.4, bf16[8,4,32,128]{3,2,1,0:T(8,128)(2,1)S(1)} %bitcast.6), custom_call_target="tpu_custom_call" | custom-call | flops 1048576 | bytes 4194304 | tf_op jit(solution)/shard_map/gather_own/pallas_call | solution.py:164
  7.6 11.2 %collective-permute-done.refs_0_ = bf16[73,32,128]{2,1,0:T(8,128)(2,1)S(1)} collective-permute-done((bf16[73,32,128]{2,1,0:T(8,128)(2,1)}, bf16[73,32,128]{2,1,0:T(8,128)(2,1)S(1)}, u32[]{:S(2)}, u32[]{:S(2)}) %collective-permute-start) | collective-permute-done | bytes 598048 | tf_op jit(solution)/shard_map/ppermute | solution.py:75
  18.8 0.8 collective-permute-done.1.refs_1_
  19.7 12.9 %collective-permute-done.2.refs_2_ = bf16[73,32,128]{2,1,0:T(8,128)(2,1)S(1)} collective-permute-done((bf16[73,32,128]{2,1,0:T(8,128)(2,1)}, bf16[73,32,128]{2,1,0:T(8,128)(2,1)S(1)}, u32[]{:S(2)}, u32[]{:S(2)}) %collective-permute-start.2) | collective-permute-done | bytes 598048 | tf_op jit(solution)/shard_map/ppermute | solution.py:75
  32.6 0.0 copy-start.4
  32.6 0.0 copy-start.5
  32.6 1.4 %combine_strips.1 = (bf16[10,32,512]{2,1,0:T(8,128)(2,1)S(1)}, bf16[10,32,512]{2,1,0:T(8,128)(2,1)S(1)}, bf16[10,32,512]{2,1,0:T(8,128)(2,1)S(1)}, bf16[8,32,512]{2,1,0:T(8,128)(2,1)S(1)}) custom-call(s32[1]{0:T(128)} %bitcast.me_ref, f32[16,8,32,128]{3,2,1,0:T(8,128)S(1)} %get-tuple-element.18.total_in, f32[16,32,128]{2,1,0:T(8,128)S(1)} %get-tuple-element.19.cover_in, ...), custom_call_target="tpu_custom_call" | custom-call | flops 1 | bytes 1 | tf_op jit(solution)/shard_map/combine_strips/pallas_call | solution.py:249
  34.0 1.2 %collective-permute-start.3 = (bf16[10,32,512]{2,1,0:T(8,128)(2,1)S(1)}, bf16[10,32,512]{2,1,0:T(8,128)(2,1)S(1)}, u32[]{:S(2)}, u32[]{:S(2)}) collective-permute-start(bf16[10,32,512]{2,1,0:T(8,128)(2,1)S(1)} %get-tuple-element.24), channel_id=1, source_target_pairs={{0,8},{8,0},{16,24},{24,16},{1,9},{9,1},{17,25},{25,17},{2,10},{10... | collective-permute-start | bytes 983048 | tf_op jit(solution)/shard_map/ppermute | solution.py:75
  35.2 0.3 collective-permute-start.4
  35.5 1.2 %collective-permute-start.5 = (bf16[8,32,512]{2,1,0:T(8,128)(2,1)S(1)}, bf16[8,32,512]{2,1,0:T(8,128)(2,1)S(1)}, u32[]{:S(2)}, u32[]{:S(2)}) collective-permute-start(bf16[8,32,512]{2,1,0:T(8,128)(2,1)S(1)} %get-tuple-element.26), channel_id=1, source_target_pairs={{0,24},{8,16},{16,8},{24,0},{1,25},{9,17},{17,9},{25,1},{2,26},{10... | collective-permute-start | bytes 786440 | tf_op jit(solution)/shard_map/ppermute | solution.py:75
  36.7 9.6 %collective-permute-done.5.refs_3_ = bf16[8,32,512]{2,1,0:T(8,128)(2,1)S(1)} collective-permute-done((bf16[8,32,512]{2,1,0:T(8,128)(2,1)S(1)}, bf16[8,32,512]{2,1,0:T(8,128)(2,1)S(1)}, u32[]{:S(2)}, u32[]{:S(2)}) %collective-permute-start.5) | collective-permute-done | bytes 262176 | tf_op jit(solution)/shard_map/ppermute | solution.py:75
  46.3 0.0 collective-permute-done.3.refs_1_
  46.3 0.0 collective-permute-done.4.refs_2_
  46.3 0.1 join_strips.1
  46.5 7.8 %collective-permute-start.6 = (bf16[7,144,512]{2,1,0:T(8,128)(2,1)S(1)}, bf16[7,144,512]{2,1,0:T(8,128)(2,1)S(1)}, u32[]{:S(2)}, u32[]{:S(2)}) collective-permute-start(bf16[7,144,512]{2,1,0:T(8,128)(2,1)S(1)} %get-tuple-element.27), channel_id=1, source_target_pairs={{0,1},{1,2},{2,3},{3,4},{4,5},{5,6},{6,7},{8,9},{9,10},{10,11},{11... | collective-permute-start | bytes 3096584 | tf_op jit(solution)/shard_map/ppermute | solution.py:531
  54.2 1.9 %collective-permute-start.7 = (bf16[7,144,512]{2,1,0:T(8,128)(2,1)S(1)}, bf16[7,144,512]{2,1,0:T(8,128)(2,1)S(1)}, u32[]{:S(2)}, u32[]{:S(2)}) collective-permute-start(bf16[7,144,512]{2,1,0:T(8,128)(2,1)S(1)} %get-tuple-element.28), channel_id=1, source_target_pairs={{1,0},{2,1},{3,2},{4,3},{5,4},{6,5},{7,6},{9,8},{10,9},{11,10},{12... | collective-permute-start | bytes 3096584 | tf_op jit(solution)/shard_map/ppermute | solution.py:532
  56.2 0.0 copy-done.4
  56.2 0.0 copy-done.5
  56.2 2.2 %smooth_own.1.own = bf16[3,8,128,512]{3,2,1,0:T(8,128)(2,1)S(1)} custom-call(s32[1]{0:T(128)} %bitcast.me_ref, bf16[4,384,144]{2,1,0:T(8,128)(2,1)S(1)} %copy-done.5, bf16[3,3,256,256]{3,2,1,0:T(8,128)(2,1)S(1)} %copy-done.4, bf16[10,32,512]{2,1,0:T(8,128)(2,1)S(1)} %get-tuple-element.23.refs_0_, bf16[10,32,512]{2,1,0:T(8,128)(2,1)S(1)} %collective-permute-done.3.refs_1_, ...), custom_call_target="tpu_custom_call" | custom-call | flops 2415919104 | bytes 6291456 | tf_op jit(solution)/shard_map/smooth_own/pallas_call | solution.py:365
  58.4 0.0 copy-start.2
  58.4 7.4 %collective-permute-done.6.low = bf16[7,144,512]{2,1,0:T(8,128)(2,1)S(1)} collective-permute-done((bf16[7,144,512]{2,1,0:T(8,128)(2,1)S(1)}, bf16[7,144,512]{2,1,0:T(8,128)(2,1)S(1)}, u32[]{:S(2)}, u32[]{:S(2)}) %collective-permute-start.6) | collective-permute-done | bytes 1032224 | tf_op jit(solution)/shard_map/ppermute | solution.py:531
  65.8 4.4 %collective-permute-done.7.high = bf16[7,144,512]{2,1,0:T(8,128)(2,1)S(1)} collective-permute-done((bf16[7,144,512]{2,1,0:T(8,128)(2,1)S(1)}, bf16[7,144,512]{2,1,0:T(8,128)(2,1)S(1)}, u32[]{:S(2)}, u32[]{:S(2)}) %collective-permute-start.7) | collective-permute-done | bytes 1032224 | tf_op jit(solution)/shard_map/ppermute | solution.py:532
  70.2 8.6 %smooth_power.1 = (bf16[3,14,128,512]{3,2,1,0:T(8,128)(2,1)S(1)}, f32[96,128]{1,0:T(8,128)S(1)}) custom-call(s32[1]{0:T(128)} %bitcast.me_ref, bf16[4,384,144]{2,1,0:T(8,128)(2,1)S(1)} %copy-done.5, bf16[3,3,256,256]{3,2,1,0:T(8,128)(2,1)S(1)} %copy-done.4, bf16[3,8,128,512]{3,2,1,0:T(8,128)(2,1)S(1)} %smooth_own.1.own, ...), custom_call_target="tpu_custom_call" | custom-call | flops 4227858432 | bytes 22020096 | tf_op jit(solution)/shard_map/smooth_power/pallas_call | solution.py:439
  78.7 0.9 %collective-permute-start.10 = (f32[96,128]{1,0:T(8,128)S(1)}, f32[96,128]{1,0:T(8,128)S(1)}, u32[]{:S(2)}, u32[]{:S(2)}) collective-permute-start(f32[96,128]{1,0:T(8,128)S(1)} %get-tuple-element.30.refs_0_), channel_id=1, source_target_pairs={{0,24},{8,16},{16,8},{24,0},{1,25},{9,17},{17,9},{25,1},{2,26},{10... | collective-permute-start | bytes 147464 | tf_op jit(solution)/shard_map/ppermute | solution.py:75
  79.7 0.6 collective-permute-start.9
  80.2 1.2 %collective-permute-start.8 = (f32[96,128]{1,0:T(8,128)S(1)}, f32[96,128]{1,0:T(8,128)S(1)}, u32[]{:S(2)}, u32[]{:S(2)}) collective-permute-start(f32[96,128]{1,0:T(8,128)S(1)} %get-tuple-element.30.refs_0_), channel_id=1, source_target_pairs={{0,8},{8,0},{16,24},{24,16},{1,9},{9,1},{17,25},{25,17},{2,10},{10... | collective-permute-start | bytes 147464 | tf_op jit(solution)/shard_map/ppermute | solution.py:75
  81.4 1.2 %collective-permute-done.10.refs_3_ = f32[96,128]{1,0:T(8,128)S(1)} collective-permute-done((f32[96,128]{1,0:T(8,128)S(1)}, f32[96,128]{1,0:T(8,128)S(1)}, u32[]{:S(2)}, u32[]{:S(2)}) %collective-permute-start.10) | collective-permute-done | bytes 49184 | tf_op jit(solution)/shard_map/ppermute | solution.py:75
  82.6 0.5 collective-permute-done.9.refs_2_
  83.1 0.1 collective-permute-done.8.refs_1_
  83.2 0.0 copy-done.2
  83.2 7.7 %score_cells.1 = f32[8,128,512]{2,1,0:T(8,128)} custom-call(bf16[3,8,128,512]{3,2,1,0:T(8,128)(2,1)S(1)} %smooth_own.1.own, bf16[3,14,128,512]{3,2,1,0:T(8,128)(2,1)S(1)} %get-tuple-element.29.halo, s32[3,4]{1,0:T(4,128)S(1)} %copy-done.2, f32[96,128]{1,0:T(8,128)S(1)} %get-tuple-element.30.refs_0_, f32[96,128]{1,0:T(8,128)S(1)} %collective-permute-done.8.refs_1_, ...), custom_call_target="tpu_custom_call" | custom-call | flops 62914560 | bytes 12582912 | tf_op jit(solution)/shard_map/score_cells/pallas_call | solution.py:500
Async XLA Ops:
  0.0 6.6 %copy-start.3 = (s32[8]{0:T(128)S(1)}, s32[8]{0:T(128)}, u32[]{:S(2)}) copy-start(s32[8]{0:T(128)} %owner_ref.3) | copy-start | bytes 100
  0.0 6.7 %copy-start.1 = (bf16[8,128,128]{2,1,0:T(8,128)(2,1)S(1)}, bf16[8,128,128]{2,1,0:T(8,128)(2,1)}, u32[]{:S(2)}) copy-start(bf16[8,128,128]{2,1,0:T(8,128)(2,1)} %param.7) | copy-start | bytes 786436
  0.0 6.7 %copy-start = (bf16[8,8,128,128]{3,2,1,0:T(8,128)(2,1)S(1)}, bf16[8,8,128,128]{3,2,1,0:T(8,128)(2,1)}, u32[]{:S(2)}) copy-start(bf16[8,8,128,128]{3,2,1,0:T(8,128)(2,1)} %param.6) | copy-start | bytes 6291460
  3.3 15.5 %collective-permute-start = (bf16[73,32,128]{2,1,0:T(8,128)(2,1)}, bf16[73,32,128]{2,1,0:T(8,128)(2,1)S(1)}, u32[]{:S(2)}, u32[]{:S(2)}) collective-permute-start(bf16[73,32,128]{2,1,0:T(8,128)(2,1)} %get-tuple-element.20), channel_id=1, source_target_pairs={{0,8},{8,0},{16,24},{24,16},{1,9},{9,1},{17,25},{25,17},{2,10},{10... | collective-permute-start | bytes 1794056 | tf_op jit(solution)/shard_map/ppermute | solution.py:75
  5.4 14.3 %collective-permute-start.1 = (bf16[73,32,128]{2,1,0:T(8,128)(2,1)}, bf16[73,32,128]{2,1,0:T(8,128)(2,1)S(1)}, u32[]{:S(2)}, u32[]{:S(2)}) collective-permute-start(bf16[73,32,128]{2,1,0:T(8,128)(2,1)} %get-tuple-element.21), channel_id=1, source_target_pairs={{0,16},{8,24},{16,0},{24,8},{1,17},{9,25},{17,1},{25,9},{2,18},{10... | collective-permute-start | bytes 1794056 | tf_op jit(solution)/shard_map/ppermute | solution.py:75
  6.6 25.9 %collective-permute-start.2 = (bf16[73,32,128]{2,1,0:T(8,128)(2,1)}, bf16[73,32,128]{2,1,0:T(8,128)(2,1)S(1)}, u32[]{:S(2)}, u32[]{:S(2)}) collective-permute-start(bf16[73,32,128]{2,1,0:T(8,128)(2,1)} %get-tuple-element.22), channel_id=1, source_target_pairs={{0,24},{8,16},{16,8},{24,0},{1,25},{9,17},{17,9},{25,1},{2,26},{10... | collective-permute-start | bytes 1794056 | tf_op jit(solution)/shard_map/ppermute | solution.py:75
  32.6 23.6 %copy-start.4 = (bf16[3,3,256,256]{3,2,1,0:T(8,128)(2,1)S(1)}, bf16[3,3,256,256]{3,2,1,0:T(8,128)(2,1)}, u32[]{:S(2)}) copy-start(bf16[3,3,256,256]{3,2,1,0:T(8,128)(2,1)} %constant.9.clone.across) | copy-start | bytes 3538948
  32.6 23.6 %copy-start.5 = (bf16[4,384,144]{2,1,0:T(8,128)(2,1)S(1)}, bf16[4,384,144]{2,1,0:T(8,128)(2,1)}, u32[]{:S(2)}) copy-start(bf16[4,384,144]{2,1,0:T(8,128)(2,1)} %constant.10.clone.down) | copy-start | bytes 1327108
  34.0 12.3 %collective-permute-start.3 = (bf16[10,32,512]{2,1,0:T(8,128)(2,1)S(1)}, bf16[10,32,512]{2,1,0:T(8,128)(2,1)S(1)}, u32[]{:S(2)}, u32[]{:S(2)}) collective-permute-start(bf16[10,32,512]{2,1,0:T(8,128)(2,1)S(1)} %get-tuple-element.24), channel_id=1, source_target_pairs={{0,8},{8,0},{16,24},{24,16},{1,9},{9,1},{17,25},{25,17},{2,10},{10... | collective-permute-start | bytes 983048 | tf_op jit(solution)/shard_map/ppermute | solution.py:75
  35.2 11.1 %collective-permute-start.4 = (bf16[10,32,512]{2,1,0:T(8,128)(2,1)S(1)}, bf16[10,32,512]{2,1,0:T(8,128)(2,1)S(1)}, u32[]{:S(2)}, u32[]{:S(2)}) collective-permute-start(bf16[10,32,512]{2,1,0:T(8,128)(2,1)S(1)} %get-tuple-element.25), channel_id=1, source_target_pairs={{0,16},{8,24},{16,0},{24,8},{1,17},{9,25},{17,1},{25,9},{2,18},{10... | collective-permute-start | bytes 983048 | tf_op jit(solution)/shard_map/ppermute | solution.py:75
  35.5 10.8 %collective-permute-start.5 = (bf16[8,32,512]{2,1,0:T(8,128)(2,1)S(1)}, bf16[8,32,512]{2,1,0:T(8,128)(2,1)S(1)}, u32[]{:S(2)}, u32[]{:S(2)}) collective-permute-start(bf16[8,32,512]{2,1,0:T(8,128)(2,1)S(1)} %get-tuple-element.26), channel_id=1, source_target_pairs={{0,24},{8,16},{16,8},{24,0},{1,25},{9,17},{17,9},{25,1},{2,26},{10... | collective-permute-start | bytes 786440 | tf_op jit(solution)/shard_map/ppermute | solution.py:75
  46.5 19.3 %collective-permute-start.6 = (bf16[7,144,512]{2,1,0:T(8,128)(2,1)S(1)}, bf16[7,144,512]{2,1,0:T(8,128)(2,1)S(1)}, u32[]{:S(2)}, u32[]{:S(2)}) collective-permute-start(bf16[7,144,512]{2,1,0:T(8,128)(2,1)S(1)} %get-tuple-element.27), channel_id=1, source_target_pairs={{0,1},{1,2},{2,3},{3,4},{4,5},{5,6},{6,7},{8,9},{9,10},{10,11},{11... | collective-permute-start | bytes 3096584 | tf_op jit(solution)/shard_map/ppermute | solution.py:531
  54.2 15.9 %collective-permute-start.7 = (bf16[7,144,512]{2,1,0:T(8,128)(2,1)S(1)}, bf16[7,144,512]{2,1,0:T(8,128)(2,1)S(1)}, u32[]{:S(2)}, u32[]{:S(2)}) collective-permute-start(bf16[7,144,512]{2,1,0:T(8,128)(2,1)S(1)} %get-tuple-element.28), channel_id=1, source_target_pairs={{1,0},{2,1},{3,2},{4,3},{5,4},{6,5},{7,6},{9,8},{10,9},{11,10},{12... | collective-permute-start | bytes 3096584 | tf_op jit(solution)/shard_map/ppermute | solution.py:532
  58.4 24.8 %copy-start.2 = (s32[3,4]{1,0:T(4,128)S(1)}, s32[3,4]{1,0:T(4,128)}, u32[]{:S(2)}) copy-start(s32[3,4]{1,0:T(4,128)} %clips.1) | copy-start | bytes 148
  78.7 3.9 %collective-permute-start.10 = (f32[96,128]{1,0:T(8,128)S(1)}, f32[96,128]{1,0:T(8,128)S(1)}, u32[]{:S(2)}, u32[]{:S(2)}) collective-permute-start(f32[96,128]{1,0:T(8,128)S(1)} %get-tuple-element.30.refs_0_), channel_id=1, source_target_pairs={{0,24},{8,16},{16,8},{24,0},{1,25},{9,17},{17,9},{25,1},{2,26},{10... | collective-permute-start | bytes 147464 | tf_op jit(solution)/shard_map/ppermute | solution.py:75
  79.7 3.5 %collective-permute-start.9 = (f32[96,128]{1,0:T(8,128)S(1)}, f32[96,128]{1,0:T(8,128)S(1)}, u32[]{:S(2)}, u32[]{:S(2)}) collective-permute-start(f32[96,128]{1,0:T(8,128)S(1)} %get-tuple-element.30.refs_0_), channel_id=1, source_target_pairs={{0,16},{8,24},{16,0},{24,8},{1,17},{9,25},{17,1},{25,9},{2,18},{10... | collective-permute-start | bytes 147464 | tf_op jit(solution)/shard_map/ppermute | solution.py:75
  80.2 2.9 %collective-permute-start.8 = (f32[96,128]{1,0:T(8,128)S(1)}, f32[96,128]{1,0:T(8,128)S(1)}, u32[]{:S(2)}, u32[]{:S(2)}) collective-permute-start(f32[96,128]{1,0:T(8,128)S(1)} %get-tuple-element.30.refs_0_), channel_id=1, source_target_pairs={{0,8},{8,0},{16,24},{24,16},{1,9},{9,1},{17,25},{25,17},{2,10},{10... | collective-permute-start | bytes 147464 | tf_op jit(solution)/shard_map/ppermute | solution.py:75

commit v6 on v5

--- a/solution.py
+++ b/solution.py
@@ -289,29 +289,34 @@
     return stack_rows([part[c] for part in strips] + [edges])
 
 
-def join_kernel(me_ref, *refs):
-    strips, (lower, upper) = refs[:-2], refs[-2:]
+def join_kernel(me_ref, odd_ref, *refs):
+    strips, (outer, inner) = refs[:-2], refs[-2:]
     channels = strips[-1].shape[0]
+    odd = odd_ref[0]
+    last = channels - EDGE
+    starts = ((outer, odd * last), (inner, (1 - odd) * last))
     for c in range(channels):
         plane = tile_plane(me_ref[0], strips, channels, c)
-        if c < EDGE:
-            lower[c] = plane
-        if c >= channels - EDGE:
-            upper[c - (channels - EDGE)] = plane
-
-
-def join(me, strips):
+        for out, start in starts:
+            at = c - start
+
+            @pl.when(jnp.logical_and(at >= 0, at < EDGE))
+            def _(out=out, at=at, plane=plane):
+                out[at] = plane
+
+
+def join(me, odd, strips):
     _, strip, broad = strips[0].shape
     out = jax.ShapeDtypeStruct((EDGE, len(strips) * strip + 2 * RIM, broad), BF16)
     return pl.pallas_call(
         join_kernel,
-        in_specs=[SMEM] + [VMEM] * len(strips),
+        in_specs=[SMEM, SMEM] + [VMEM] * len(strips),
         out_specs=[VMEM] * 2,
         out_shape=[out] * 2,
         compiler_params=params(16),
         cost_estimate=cost(1, 1),
         name="join_strips",
-    )(me, *strips)
+    )(me, odd, *strips)
 
 
 def smooth_planes(planes, down, across, middle, out, base):
@@ -344,7 +349,7 @@
             for i, part in enumerate(parts):
                 lanes = slice(i * quarter, (i + 1) * quarter)
                 value = part.astype(BF16).reshape(size, tall, quarter)
-                out[k, base + start : base + start + size, :, lanes] = value
+                out[k, pl.ds(base + start, size), :, lanes] = value
             start += size
 
 
@@ -403,9 +408,10 @@
     return order
 
 
-def power_kernel(me_ref, down, across, own, low, high, halo, power, middle, sums):
+def power_kernel(me_ref, odd_ref, down, across, own, outer, inner, halo, power, middle, sums):
     channels, tall, broad = own.shape[1:]
-    for side, base in ((low, 0), (high, EDGE)):
+    odd = odd_ref[0]
+    for side, base in ((inner, (1 - odd) * EDGE), (outer, odd * EDGE)):
         planes = [functools.partial(side.__getitem__, c) for c in range(EDGE)]
         smooth_planes(planes, down.at[me_ref[0]], across, middle, halo, base)
     layers = (own, halo)
@@ -432,13 +438,13 @@
     power[...] = jnp.broadcast_to(total, power.shape)
 
 
-def smooth_power(me, own, sides, down, across):
+def smooth_power(me, odd, own, sides, down, across):
     _, channels, tall, broad = own.shape
     pairs = KERNELS * WIDTHS * channels
     halo = jax.ShapeDtypeStruct((KERNELS, 2 * EDGE, tall, broad), BF16)
     return pl.pallas_call(
         power_kernel,
-        in_specs=[SMEM] + [VMEM] * (3 + len(sides)),
+        in_specs=[SMEM, SMEM] + [VMEM] * (3 + len(sides)),
         out_specs=[VMEM] * 2,
         out_shape=[halo, jax.ShapeDtypeStruct((pairs, LANES), F32)],
         scratch_shapes=[
@@ -448,7 +454,7 @@
         compiler_params=params(24),
         cost_estimate=cost(2 * halo.size * (broad + 256), 8 * halo.size),
         name="smooth_power",
-    )(me, down, across, own, *sides)
+    )(me, odd, down, across, own, *sides)
 
 
 def score_kernel(count, cells, own, halo, clips, *refs):
@@ -526,13 +532,16 @@
     total, cover = gather_own(me, destination, parts, beams)
     strips = combine(me, total, cover, arrived, piece_count)
     tiles = [strips[0]] + [exchange(strips[k], "sky", k) for k in range(1, count)]
-    lower, upper = join(me, tiles)
+    odd = lax.rem(lax.axis_index("freq").astype(jnp.int32), 2).reshape(1)
+    outer, inner = join(me, odd, tiles)
+    outer_pairs = [(i, i + 1) for i in range(1, links - 1, 2)]
+    inner_pairs = [(i, i + 1) for i in range(0, links - 1, 2)]
     sides = [
-        lax.ppermute(upper, "freq", [(i, i + 1) for i in range(links - 1)]),
-        lax.ppermute(lower, "freq", [(i + 1, i) for i in range(links - 1)]),
+        lax.ppermute(block, "freq", pairs + [(target, source) for source, target in pairs])
+        for block, pairs in ((outer, outer_pairs), (inner, inner_pairs))
     ]
     own = smooth(me, tiles, down, across)
-    halo, power = smooth_power(me, own, sides, down, across)
+    halo, power = smooth_power(me, odd, own, sides, down, across)
     powers = [power] + [exchange(power, "sky", k) for k in range(1, count)]
     cells = float(count * ROWB * LANES * COLB * LANES)
     return score(own, halo, clip_tenths, powers, cells)

time: 91 us -> 88.2 us (0.969)
  waiting for transfers between devices: 48.1 us -> 45.2 us
  starting transfers between devices: 18.4 us -> 16.6 us
  local copies, waits for them, and re-layouts: 0.02 us -> 1.15 us
    ppermute x2, waiting for transfers between devices: 11.8 us -> 8.85 us  [shards(): lax.ppermute(block, 'freq', pairs + [(target, source) for source, target...]
    ppermute x2, starting transfers between devices: 9.67 us -> 7.82 us  [shards(): lax.ppermute(block, 'freq', pairs + [(target, source) for source, target...]
    unnamed x12, local copies, waits for them, and re-layouts: 0.02 us -> 1.15 us
  transfers between devices with their start and end apart: 11 -> 11, of which waited for: 9 -> 8; matrix products, arithmetic and copies ran while one was open for 0% -> 0% of each run, Pallas kernels for 3% -> 4%
where the time goes in v6:
time: 88.2 us; the launch traced here: 87.3 us
  waiting for transfers between devices  45.2 us (51%)
  Pallas kernels  24.3 us (28%)
  starting transfers between devices  16.6 us (19%)
  local copies, waits for them, and re-layouts  1.15 us (1%)
    ppermute x9, waiting for transfers between devices, exchange(): return lax.ppermute(block, axis, [(i, i ^ k) for i in range(count)])  36.3 us
    ppermute x2, waiting for transfers between devices, shards(): lax.ppermute(block, 'freq', pairs + [(target, source) for source, target...  8.85 us
    ppermute x9, starting transfers between devices, exchange(): return lax.ppermute(block, axis, [(i, i ^ k) for i in range(count)])  8.74 us
    pallas_call x1, Pallas kernels, smooth_power(): pl.pallas_call(power_kernel, in_specs=[SMEM, SMEM] + [VMEM] * (3 + len(si...  8.53 us
    ppermute x2, starting transfers between devices, shards(): lax.ppermute(block, 'freq', pairs + [(target, source) for source, target...  7.82 us
    pallas_call x1, Pallas kernels, score(): pl.pallas_call(functools.partial(score_kernel, len(powers), cells), grid=...  7.68 us
    pallas_call x1, Pallas kernels, pack(): pl.pallas_call(functools.partial(pack_kernel, count), in_specs=[SMEM, SME...  3.26 us
    pallas_call x1, Pallas kernels, smooth(): pl.pallas_call(functools.partial(smooth_kernel, len(strips)), in_specs=[S...  2.19 us
  transfers between devices with their start and end apart: 11, of which 8 were waited for; matrix products, arithmetic and copies ran while one was open for 0% of the time, Pallas kernels for 4%

profile of v6, /device:TPU:1, one launch (start us, length us, event | category | flops | bytes accessed | tf_op | source)
XLA Modules:
  0.0 87.3 jit_solution(251173312552269709)
XLA Ops:
  0.0 0.0 copy-start.3
  0.0 0.0 copy-start.1
  0.0 0.0 copy-start
  0.0 3.3 %pack_pieces.1 = (bf16[73,32,128]{2,1,0:T(8,128)(2,1)}, bf16[73,32,128]{2,1,0:T(8,128)(2,1)}, bf16[73,32,128]{2,1,0:T(8,128)(2,1)}) custom-call(s32[1]{0:T(128)} %bitcast.me_ref, s32[8]{0:T(128)} %owner_ref.3, bf16[8,8,4,32,128]{4,3,2,1,0:T(8,128)(2,1)} %bitcast.4, bf16[8,4,32,128]{3,2,1,0:T(8,128)(2,1)} %bitcast.6), custom_call_target="tpu_custom_call" | custom-call | flops 1048576 | bytes 4194304 | tf_op jit(solution)/shard_map/pack_pieces/pallas_call | solution.py:126
  3.3 2.1 %collective-permute-start = (bf16[73,32,128]{2,1,0:T(8,128)(2,1)}, bf16[73,32,128]{2,1,0:T(8,128)(2,1)S(1)}, u32[]{:S(2)}, u32[]{:S(2)}) collective-permute-start(bf16[73,32,128]{2,1,0:T(8,128)(2,1)} %get-tuple-element.20), channel_id=1, source_target_pairs={{0,8},{8,0},{16,24},{24,16},{1,9},{9,1},{17,25},{25,17},{2,10},{10... | collective-permute-start | bytes 1794056 | tf_op jit(solution)/shard_map/ppermute | solution.py:75
  5.4 1.2 %collective-permute-start.1 = (bf16[73,32,128]{2,1,0:T(8,128)(2,1)}, bf16[73,32,128]{2,1,0:T(8,128)(2,1)S(1)}, u32[]{:S(2)}, u32[]{:S(2)}) collective-permute-start(bf16[73,32,128]{2,1,0:T(8,128)(2,1)} %get-tuple-element.21), channel_id=1, source_target_pairs={{0,16},{8,24},{16,0},{24,8},{1,17},{9,25},{17,1},{25,9},{2,18},{10... | collective-permute-start | bytes 1794056 | tf_op jit(solution)/shard_map/ppermute | solution.py:75
  6.6 0.0 collective-permute-start.2
  6.6 0.0 copy-done.3
  6.7 0.0 copy-done.1
  6.7 0.0 copy-done
  6.7 1.0 %gather_own.1 = (f32[16,8,32,128]{3,2,1,0:T(8,128)S(1)}, f32[16,32,128]{2,1,0:T(8,128)S(1)}) custom-call(s32[1]{0:T(128)} %bitcast.me_ref, s32[8]{0:T(128)S(1)} %copy-done.3, bf16[8,8,4,32,128]{4,3,2,1,0:T(8,128)(2,1)S(1)} %bitcast.5, bf16[8,4,32,128]{3,2,1,0:T(8,128)(2,1)S(1)} %bitcast.7), custom_call_target="tpu_custom_call" | custom-call | flops 1048576 | bytes 4194304 | tf_op jit(solution)/shard_map/gather_own/pallas_call | solution.py:164
  7.6 11.2 %collective-permute-done.refs_0_ = bf16[73,32,128]{2,1,0:T(8,128)(2,1)S(1)} collective-permute-done((bf16[73,32,128]{2,1,0:T(8,128)(2,1)}, bf16[73,32,128]{2,1,0:T(8,128)(2,1)S(1)}, u32[]{:S(2)}, u32[]{:S(2)}) %collective-permute-start) | collective-permute-done | bytes 598048 | tf_op jit(solution)/shard_map/ppermute | solution.py:75
  18.8 0.8 collective-permute-done.1.refs_1_
  19.7 12.9 %collective-permute-done.2.refs_2_ = bf16[73,32,128]{2,1,0:T(8,128)(2,1)S(1)} collective-permute-done((bf16[73,32,128]{2,1,0:T(8,128)(2,1)}, bf16[73,32,128]{2,1,0:T(8,128)(2,1)S(1)}, u32[]{:S(2)}, u32[]{:S(2)}) %collective-permute-start.2) | collective-permute-done | bytes 598048 | tf_op jit(solution)/shard_map/ppermute | solution.py:75
  32.6 0.0 copy-start.4
  32.6 1.4 %combine_strips.1 = (bf16[10,32,512]{2,1,0:T(8,128)(2,1)S(1)}, bf16[10,32,512]{2,1,0:T(8,128)(2,1)S(1)}, bf16[10,32,512]{2,1,0:T(8,128)(2,1)S(1)}, bf16[8,32,512]{2,1,0:T(8,128)(2,1)S(1)}) custom-call(s32[1]{0:T(128)} %bitcast.me_ref, f32[16,8,32,128]{3,2,1,0:T(8,128)S(1)} %get-tuple-element.18.total_in, f32[16,32,128]{2,1,0:T(8,128)S(1)} %get-tuple-element.19.cover_in, ...), custom_call_target="tpu_custom_call" | custom-call | flops 1 | bytes 1 | tf_op jit(solution)/shard_map/combine_strips/pallas_call | solution.py:249
  34.0 1.2 %collective-permute-start.3 = (bf16[10,32,512]{2,1,0:T(8,128)(2,1)S(1)}, bf16[10,32,512]{2,1,0:T(8,128)(2,1)S(1)}, u32[]{:S(2)}, u32[]{:S(2)}) collective-permute-start(bf16[10,32,512]{2,1,0:T(8,128)(2,1)S(1)} %get-tuple-element.24), channel_id=1, source_target_pairs={{0,8},{8,0},{16,24},{24,16},{1,9},{9,1},{17,25},{25,17},{2,10},{10... | collective-permute-start | bytes 983048 | tf_op jit(solution)/shard_map/ppermute | solution.py:75
  35.2 0.3 collective-permute-start.4
  35.5 1.2 %collective-permute-start.5 = (bf16[8,32,512]{2,1,0:T(8,128)(2,1)S(1)}, bf16[8,32,512]{2,1,0:T(8,128)(2,1)S(1)}, u32[]{:S(2)}, u32[]{:S(2)}) collective-permute-start(bf16[8,32,512]{2,1,0:T(8,128)(2,1)S(1)} %get-tuple-element.26), channel_id=1, source_target_pairs={{0,24},{8,16},{16,8},{24,0},{1,25},{9,17},{17,9},{25,1},{2,26},{10... | collective-permute-start | bytes 786440 | tf_op jit(solution)/shard_map/ppermute | solution.py:75
  36.7 9.6 %collective-permute-done.5.refs_3_ = bf16[8,32,512]{2,1,0:T(8,128)(2,1)S(1)} collective-permute-done((bf16[8,32,512]{2,1,0:T(8,128)(2,1)S(1)}, bf16[8,32,512]{2,1,0:T(8,128)(2,1)S(1)}, u32[]{:S(2)}, u32[]{:S(2)}) %collective-permute-start.5) | collective-permute-done | bytes 262176 | tf_op jit(solution)/shard_map/ppermute | solution.py:75
  46.3 0.0 collective-permute-done.3.refs_1_
  46.3 0.0 collective-permute-done.4.refs_2_
  46.3 0.3 join_strips.1
  46.6 7.8 %collective-permute-start.6 = (bf16[7,144,512]{2,1,0:T(8,128)(2,1)S(1)}, bf16[7,144,512]{2,1,0:T(8,128)(2,1)S(1)}, u32[]{:S(2)}, u32[]{:S(2)}) collective-permute-start(bf16[7,144,512]{2,1,0:T(8,128)(2,1)S(1)} %get-tuple-element.27), channel_id=1, source_target_pairs={{1,2},{3,4},{5,6},{2,1},{4,3},{6,5},{9,10},{11,12},{13,14},{10,9},... | collective-permute-start | bytes 3096584 | tf_op jit(solution)/shard_map/ppermute | solution.py:540
  54.3 0.1 collective-permute-start.7
  54.4 0.0 copy-done.4
  54.4 0.0 copy-start.5
  54.4 1.1 %copy-done.5 = bf16[4,384,144]{2,1,0:T(8,128)(2,1)S(1)} copy-done((bf16[4,384,144]{2,1,0:T(8,128)(2,1)S(1)}, bf16[4,384,144]{2,1,0:T(8,128)(2,1)}, u32[]{:S(2)}) %copy-start.5) | copy-done | bytes 442392
  55.6 2.2 %smooth_own.1.own = bf16[3,8,128,512]{3,2,1,0:T(8,128)(2,1)S(1)} custom-call(s32[1]{0:T(128)} %bitcast.me_ref, bf16[4,384,144]{2,1,0:T(8,128)(2,1)S(1)} %copy-done.5, bf16[3,3,256,256]{3,2,1,0:T(8,128)(2,1)S(1)} %copy-done.4, bf16[10,32,512]{2,1,0:T(8,128)(2,1)S(1)} %get-tuple-element.23.refs_0_, bf16[10,32,512]{2,1,0:T(8,128)(2,1)S(1)} %collective-permute-done.3.refs_1_, ...), custom_call_target="tpu_custom_call" | custom-call | flops 2415919104 | bytes 6291456 | tf_op jit(solution)/shard_map/smooth_own/pallas_call | solution.py:370
  57.8 0.0 copy-start.2
  57.8 8.9 %collective-permute-done.6.outer = bf16[7,144,512]{2,1,0:T(8,128)(2,1)S(1)} collective-permute-done((bf16[7,144,512]{2,1,0:T(8,128)(2,1)S(1)}, bf16[7,144,512]{2,1,0:T(8,128)(2,1)S(1)}, u32[]{:S(2)}, u32[]{:S(2)}) %collective-permute-start.6) | collective-permute-done | bytes 1032224 | tf_op jit(solution)/shard_map/ppermute | solution.py:540
  66.6 0.0 collective-permute-done.7.inner
  66.6 8.5 %smooth_power.1 = (bf16[3,14,128,512]{3,2,1,0:T(8,128)(2,1)S(1)}, f32[96,128]{1,0:T(8,128)S(1)}) custom-call(s32[1]{0:T(128)} %bitcast.me_ref, s32[1]{0:T(128)} %bitcast.3.odd_ref, bf16[4,384,144]{2,1,0:T(8,128)(2,1)S(1)} %copy-done.5, bf16[3,3,256,256]{3,2,1,0:T(8,128)(2,1)S(1)} %copy-done.4, bf16[3,8,128,512]{3,2,1,0:T(8,128)(2,1)S(1)} %smooth_own.1.own, ...), custom_call_target="tpu_custom_call" | custom-call | flops 4227858432 | bytes 22020096 | tf_op jit(solution)/shard_map/smooth_power/pallas_call | solution.py:445
  75.2 0.9 %collective-permute-start.10 = (f32[96,128]{1,0:T(8,128)S(1)}, f32[96,128]{1,0:T(8,128)S(1)}, u32[]{:S(2)}, u32[]{:S(2)}) collective-permute-start(f32[96,128]{1,0:T(8,128)S(1)} %get-tuple-element.30.refs_0_), channel_id=1, source_target_pairs={{0,24},{8,16},{16,8},{24,0},{1,25},{9,17},{17,9},{25,1},{2,26},{10... | collective-permute-start | bytes 147464 | tf_op jit(solution)/shard_map/ppermute | solution.py:75
  76.1 0.6 collective-permute-start.9
  76.7 1.2 %collective-permute-start.8 = (f32[96,128]{1,0:T(8,128)S(1)}, f32[96,128]{1,0:T(8,128)S(1)}, u32[]{:S(2)}, u32[]{:S(2)}) collective-permute-start(f32[96,128]{1,0:T(8,128)S(1)} %get-tuple-element.30.refs_0_), channel_id=1, source_target_pairs={{0,8},{8,0},{16,24},{24,16},{1,9},{9,1},{17,25},{25,17},{2,10},{10... | collective-permute-start | bytes 147464 | tf_op jit(solution)/shard_map/ppermute | solution.py:75
  77.8 1.2 %collective-permute-done.10.refs_3_ = f32[96,128]{1,0:T(8,128)S(1)} collective-permute-done((f32[96,128]{1,0:T(8,128)S(1)}, f32[96,128]{1,0:T(8,128)S(1)}, u32[]{:S(2)}, u32[]{:S(2)}) %collective-permute-start.10) | collective-permute-done | bytes 49184 | tf_op jit(solution)/shard_map/ppermute | solution.py:75
  79.1 0.5 collective-permute-done.9.refs_2_
  79.6 0.1 collective-permute-done.8.refs_1_
  79.6 0.0 copy-done.2
  79.6 7.7 %score_cells.1 = f32[8,128,512]{2,1,0:T(8,128)} custom-call(bf16[3,8,128,512]{3,2,1,0:T(8,128)(2,1)S(1)} %smooth_own.1.own, bf16[3,14,128,512]{3,2,1,0:T(8,128)(2,1)S(1)} %get-tuple-element.29.halo, s32[3,4]{1,0:T(4,128)S(1)} %copy-done.2, f32[96,128]{1,0:T(8,128)S(1)} %get-tuple-element.30.refs_0_, f32[96,128]{1,0:T(8,128)S(1)} %collective-permute-done.8.refs_1_, ...), custom_call_target="tpu_custom_call" | custom-call | flops 62914560 | bytes 12582912 | tf_op jit(solution)/shard_map/score_cells/pallas_call | solution.py:506
Async XLA Ops:
  0.0 6.7 %copy-start.3 = (s32[8]{0:T(128)S(1)}, s32[8]{0:T(128)}, u32[]{:S(2)}) copy-start(s32[8]{0:T(128)} %owner_ref.3) | copy-start | bytes 100
  0.0 6.7 %copy-start.1 = (bf16[8,128,128]{2,1,0:T(8,128)(2,1)S(1)}, bf16[8,128,128]{2,1,0:T(8,128)(2,1)}, u32[]{:S(2)}) copy-start(bf16[8,128,128]{2,1,0:T(8,128)(2,1)} %param.7) | copy-start | bytes 786436
  0.0 6.7 %copy-start = (bf16[8,8,128,128]{3,2,1,0:T(8,128)(2,1)S(1)}, bf16[8,8,128,128]{3,2,1,0:T(8,128)(2,1)}, u32[]{:S(2)}) copy-start(bf16[8,8,128,128]{3,2,1,0:T(8,128)(2,1)} %param.6) | copy-start | bytes 6291460
  3.3 15.5 %collective-permute-start = (bf16[73,32,128]{2,1,0:T(8,128)(2,1)}, bf16[73,32,128]{2,1,0:T(8,128)(2,1)S(1)}, u32[]{:S(2)}, u32[]{:S(2)}) collective-permute-start(bf16[73,32,128]{2,1,0:T(8,128)(2,1)} %get-tuple-element.20), channel_id=1, source_target_pairs={{0,8},{8,0},{16,24},{24,16},{1,9},{9,1},{17,25},{25,17},{2,10},{10... | collective-permute-start | bytes 1794056 | tf_op jit(solution)/shard_map/ppermute | solution.py:75
  5.4 14.3 %collective-permute-start.1 = (bf16[73,32,128]{2,1,0:T(8,128)(2,1)}, bf16[73,32,128]{2,1,0:T(8,128)(2,1)S(1)}, u32[]{:S(2)}, u32[]{:S(2)}) collective-permute-start(bf16[73,32,128]{2,1,0:T(8,128)(2,1)} %get-tuple-element.21), channel_id=1, source_target_pairs={{0,16},{8,24},{16,0},{24,8},{1,17},{9,25},{17,1},{25,9},{2,18},{10... | collective-permute-start | bytes 1794056 | tf_op jit(solution)/shard_map/ppermute | solution.py:75
  6.6 25.9 %collective-permute-start.2 = (bf16[73,32,128]{2,1,0:T(8,128)(2,1)}, bf16[73,32,128]{2,1,0:T(8,128)(2,1)S(1)}, u32[]{:S(2)}, u32[]{:S(2)}) collective-permute-start(bf16[73,32,128]{2,1,0:T(8,128)(2,1)} %get-tuple-element.22), channel_id=1, source_target_pairs={{0,24},{8,16},{16,8},{24,0},{1,25},{9,17},{17,9},{25,1},{2,26},{10... | collective-permute-start | bytes 1794056 | tf_op jit(solution)/shard_map/ppermute | solution.py:75
  32.6 21.9 %copy-start.4 = (bf16[3,3,256,256]{3,2,1,0:T(8,128)(2,1)S(1)}, bf16[3,3,256,256]{3,2,1,0:T(8,128)(2,1)}, u32[]{:S(2)}) copy-start(bf16[3,3,256,256]{3,2,1,0:T(8,128)(2,1)} %constant.17.clone.across) | copy-start | bytes 3538948
  34.0 12.3 %collective-permute-start.3 = (bf16[10,32,512]{2,1,0:T(8,128)(2,1)S(1)}, bf16[10,32,512]{2,1,0:T(8,128)(2,1)S(1)}, u32[]{:S(2)}, u32[]{:S(2)}) collective-permute-start(bf16[10,32,512]{2,1,0:T(8,128)(2,1)S(1)} %get-tuple-element.24), channel_id=1, source_target_pairs={{0,8},{8,0},{16,24},{24,16},{1,9},{9,1},{17,25},{25,17},{2,10},{10... | collective-permute-start | bytes 983048 | tf_op jit(solution)/shard_map/ppermute | solution.py:75
  35.2 11.1 %collective-permute-start.4 = (bf16[10,32,512]{2,1,0:T(8,128)(2,1)S(1)}, bf16[10,32,512]{2,1,0:T(8,128)(2,1)S(1)}, u32[]{:S(2)}, u32[]{:S(2)}) collective-permute-start(bf16[10,32,512]{2,1,0:T(8,128)(2,1)S(1)} %get-tuple-element.25), channel_id=1, source_target_pairs={{0,16},{8,24},{16,0},{24,8},{1,17},{9,25},{17,1},{25,9},{2,18},{10... | collective-permute-start | bytes 983048 | tf_op jit(solution)/shard_map/ppermute | solution.py:75
  35.5 10.8 %collective-permute-start.5 = (bf16[8,32,512]{2,1,0:T(8,128)(2,1)S(1)}, bf16[8,32,512]{2,1,0:T(8,128)(2,1)S(1)}, u32[]{:S(2)}, u32[]{:S(2)}) collective-permute-start(bf16[8,32,512]{2,1,0:T(8,128)(2,1)S(1)} %get-tuple-element.26), channel_id=1, source_target_pairs={{0,24},{8,16},{16,8},{24,0},{1,25},{9,17},{17,9},{25,1},{2,26},{10... | collective-permute-start | bytes 786440 | tf_op jit(solution)/shard_map/ppermute | solution.py:75
  46.6 20.1 %collective-permute-start.6 = (bf16[7,144,512]{2,1,0:T(8,128)(2,1)S(1)}, bf16[7,144,512]{2,1,0:T(8,128)(2,1)S(1)}, u32[]{:S(2)}, u32[]{:S(2)}) collective-permute-start(bf16[7,144,512]{2,1,0:T(8,128)(2,1)S(1)} %get-tuple-element.27), channel_id=1, source_target_pairs={{1,2},{3,4},{5,6},{2,1},{4,3},{6,5},{9,10},{11,12},{13,14},{10,9},... | collective-permute-start | bytes 3096584 | tf_op jit(solution)/shard_map/ppermute | solution.py:540
  54.3 12.3 %collective-permute-start.7 = (bf16[7,144,512]{2,1,0:T(8,128)(2,1)S(1)}, bf16[7,144,512]{2,1,0:T(8,128)(2,1)S(1)}, u32[]{:S(2)}, u32[]{:S(2)}) collective-permute-start(bf16[7,144,512]{2,1,0:T(8,128)(2,1)S(1)} %get-tuple-element.28), channel_id=1, source_target_pairs={{0,1},{2,3},{4,5},{6,7},{1,0},{3,2},{5,4},{7,6},{8,9},{10,11},{12,... | collective-permute-start | bytes 3096584 | tf_op jit(solution)/shard_map/ppermute | solution.py:540
  54.4 1.1 %copy-start.5 = (bf16[4,384,144]{2,1,0:T(8,128)(2,1)S(1)}, bf16[4,384,144]{2,1,0:T(8,128)(2,1)}, u32[]{:S(2)}) copy-start(bf16[4,384,144]{2,1,0:T(8,128)(2,1)} %constant.18.clone.down) | copy-start | bytes 1327108
  57.8 21.8 %copy-start.2 = (s32[3,4]{1,0:T(4,128)S(1)}, s32[3,4]{1,0:T(4,128)}, u32[]{:S(2)}) copy-start(s32[3,4]{1,0:T(4,128)} %clips.1) | copy-start | bytes 148
  75.2 3.9 %collective-permute-start.10 = (f32[96,128]{1,0:T(8,128)S(1)}, f32[96,128]{1,0:T(8,128)S(1)}, u32[]{:S(2)}, u32[]{:S(2)}) collective-permute-start(f32[96,128]{1,0:T(8,128)S(1)} %get-tuple-element.30.refs_0_), channel_id=1, source_target_pairs={{0,24},{8,16},{16,8},{24,0},{1,25},{9,17},{17,9},{25,1},{2,26},{10... | collective-permute-start | bytes 147464 | tf_op jit(solution)/shard_map/ppermute | solution.py:75
  76.1 3.5 %collective-permute-start.9 = (f32[96,128]{1,0:T(8,128)S(1)}, f32[96,128]{1,0:T(8,128)S(1)}, u32[]{:S(2)}, u32[]{:S(2)}) collective-permute-start(f32[96,128]{1,0:T(8,128)S(1)} %get-tuple-element.30.refs_0_), channel_id=1, source_target_pairs={{0,16},{8,24},{16,0},{24,8},{1,17},{9,25},{17,1},{25,9},{2,18},{10... | collective-permute-start | bytes 147464 | tf_op jit(solution)/shard_map/ppermute | solution.py:75
  76.7 2.9 %collective-permute-start.8 = (f32[96,128]{1,0:T(8,128)S(1)}, f32[96,128]{1,0:T(8,128)S(1)}, u32[]{:S(2)}, u32[]{:S(2)}) collective-permute-start(f32[96,128]{1,0:T(8,128)S(1)} %get-tuple-element.30.refs_0_), channel_id=1, source_target_pairs={{0,8},{8,0},{16,24},{24,16},{1,9},{9,1},{17,25},{25,17},{2,10},{10... | collective-permute-start | bytes 147464 | tf_op jit(solution)/shard_map/ppermute | solution.py:75

commit v7 on v6

--- a/solution.py
+++ b/solution.py
@@ -87,17 +87,18 @@
     return [(wide * pieces[p, c].astype(F32)).astype(BF16) for c in range(pieces.shape[1])]
 
 
-def pack_kernel(count, me_ref, owner_ref, pieces_hbm, beam_hbm, *refs):
-    outs, (pieces, beams, packed, in_sems, out_sems) = refs[: count - 1], refs[count - 1 :]
+def pack_kernel(offsets, me_ref, owner_ref, pieces_hbm, beam_hbm, *refs):
+    parts = len(offsets)
+    outs, (pieces, beams, packed, in_sems, out_sems) = refs[:parts], refs[parts:]
     _, piece_count, channels, strip, _ = pieces.shape
     planes = channels + 1
     me = me_ref[0]
 
     def fetch(k):
         here = (pieces.at[k - 1], beams.at[k - 1], in_sems.at[k - 1])
-        return fetch_strip(pieces_hbm, beam_hbm, *here, me ^ k)
-
-    order = range(count - 1, 0, -1)
+        return fetch_strip(pieces_hbm, beam_hbm, *here, me ^ offsets[k - 1])
+
+    order = range(parts, 0, -1)
     for k in order:
         for copy in fetch(k):
             copy.start()
@@ -119,12 +120,13 @@
         pltpu.make_async_copy(packed.at[k - 1], outs[k - 1], out_sems.at[k - 1]).wait()
 
 
-def pack(me, destination, parts, beams):
-    piece_count, channels, count, strip, _ = parts.shape
+def pack(me, destination, parts, beams, offsets):
+    piece_count, channels, _, strip, _ = parts.shape
+    count = len(offsets) + 1
     out = jax.ShapeDtypeStruct((piece_count * (channels + 1) + 1, strip, LANES), BF16)
     far = pl.BlockSpec(memory_space=pl.ANY)
     return pl.pallas_call(
-        functools.partial(pack_kernel, count),
+        functools.partial(pack_kernel, offsets),
         in_specs=[SMEM, SMEM, far, far],
         out_specs=[far] * (count - 1),
         out_shape=[out] * (count - 1),
@@ -527,7 +529,8 @@
     strip = LANES // count
     parts = pieces.reshape(piece_count, channels, count, strip, LANES)
     beams = beam.reshape(piece_count, count, strip, LANES)
-    packed = pack(me, destination, parts, beams)
+    packed = pack(me, destination, parts, beams, (1,))
+    packed += pack(me, destination, parts, beams, tuple(range(2, count)))
     arrived = [exchange(block, "sky", k) for k, block in enumerate(packed, 1)]
     total, cover = gather_own(me, destination, parts, beams)
     strips = combine(me, total, cover, arrived, piece_count)

time: 88.2 us -> 90.7 us (1.028)
  Pallas kernels: 24.3 us -> 26.8 us
  starting transfers between devices: 16.6 us -> 14.8 us
  waiting for transfers between devices: 45.2 us -> 46.9 us
    pallas_call x1 -> x2, Pallas kernels: 3.26 us -> 5.73 us  [pack(): pl.pallas_call(functools.partial(pack_kernel, offsets), in_specs=[SMEM, S...]
    ppermute x2, starting transfers between devices: 7.82 us -> 5.95 us  [shards(): lax.ppermute(block, 'freq', pairs + [(target, source) for source, target...]
    ppermute x9, waiting for transfers between devices: 36.3 us -> 38 us  [exchange(): return lax.ppermute(block, axis, [(i, i ^ k) for i in range(count)])]
  transfers between devices with their start and end apart: 11 -> 11, of which waited for: 8 -> 7; matrix products, arithmetic and copies ran while one was open for 0% -> 0% of each run, Pallas kernels for 4% -> 7%
where the time goes in v7:
time: 90.7 us; the launch traced here: 89.7 us
  waiting for transfers between devices  46.9 us (52%)
  Pallas kernels  26.8 us (30%)
  starting transfers between devices  14.8 us (16%)
  local copies, waits for them, and re-layouts  1.15 us (1%)
    ppermute x9, waiting for transfers between devices, exchange(): return lax.ppermute(block, axis, [(i, i ^ k) for i in range(count)])  38 us
    ppermute x2, waiting for transfers between devices, shards(): lax.ppermute(block, 'freq', pairs + [(target, source) for source, target...  8.85 us
    ppermute x9, starting transfers between devices, exchange(): return lax.ppermute(block, axis, [(i, i ^ k) for i in range(count)])  8.84 us
    pallas_call x1, Pallas kernels, smooth_power(): pl.pallas_call(power_kernel, in_specs=[SMEM, SMEM] + [VMEM] * (3 + len(si...  8.54 us
    pallas_call x1, Pallas kernels, score(): pl.pallas_call(functools.partial(score_kernel, len(powers), cells), grid=...  7.68 us
    ppermute x2, starting transfers between devices, shards(): lax.ppermute(block, 'freq', pairs + [(target, source) for source, target...  5.95 us
    pallas_call x2, Pallas kernels, pack(): pl.pallas_call(functools.partial(pack_kernel, offsets), in_specs=[SMEM, S...  5.73 us
    pallas_call x1, Pallas kernels, smooth(): pl.pallas_call(functools.partial(smooth_kernel, len(strips)), in_specs=[S...  2.19 us
  transfers between devices with their start and end apart: 11, of which 7 were waited for; matrix products, arithmetic and copies ran while one was open for 0% of the time, Pallas kernels for 7%

profile of v7, /device:TPU:1, one launch (start us, length us, event | category | flops | bytes accessed | tf_op | source)
XLA Modules:
  0.0 89.7 jit_solution(6930408027898566762)
XLA Ops:
  0.0 0.0 copy-start
  0.0 0.0 copy-start.1
  0.0 0.0 copy-start.2
  0.0 2.8 %pack_pieces.2 = bf16[73,32,128]{2,1,0:T(8,128)(2,1)} custom-call(s32[1]{0:T(128)} %bitcast.me_ref, s32[8]{0:T(128)} %owner_ref.5, bf16[8,8,4,32,128]{4,3,2,1,0:T(8,128)(2,1)} %bitcast.4, bf16[8,4,32,128]{3,2,1,0:T(8,128)(2,1)} %bitcast.7), custom_call_target="tpu_custom_call" | custom-call | flops 1048576 | bytes 4194304 | tf_op jit(solution)/shard_map/pack_pieces/pallas_call | solution.py:128
  2.8 2.1 %collective-permute-start = (bf16[73,32,128]{2,1,0:T(8,128)(2,1)}, bf16[73,32,128]{2,1,0:T(8,128)(2,1)S(1)}, u32[]{:S(2)}, u32[]{:S(2)}) collective-permute-start(bf16[73,32,128]{2,1,0:T(8,128)(2,1)} %pack_pieces.2), channel_id=1, source_target_pairs={{0,8},{8,0},{16,24},{24,16},{1,9},{9,1},{17,25},{25,17},{2,10},{10... | collective-permute-start | bytes 1794056 | tf_op jit(solution)/shard_map/ppermute | solution.py:75
  4.9 2.9 %pack_pieces.3 = (bf16[73,32,128]{2,1,0:T(8,128)(2,1)}, bf16[73,32,128]{2,1,0:T(8,128)(2,1)}) custom-call(s32[1]{0:T(128)} %bitcast.me_ref, s32[8]{0:T(128)} %owner_ref.5, bf16[8,8,4,32,128]{4,3,2,1,0:T(8,128)(2,1)} %bitcast.5, bf16[8,4,32,128]{3,2,1,0:T(8,128)(2,1)} %bitcast.8), custom_call_target="tpu_custom_call" | custom-call | flops 1048576 | bytes 4194304 | tf_op jit(solution)/shard_map/pack_pieces/pallas_call | solution.py:128
  7.9 1.3 %collective-permute-start.1 = (bf16[73,32,128]{2,1,0:T(8,128)(2,1)}, bf16[73,32,128]{2,1,0:T(8,128)(2,1)S(1)}, u32[]{:S(2)}, u32[]{:S(2)}) collective-permute-start(bf16[73,32,128]{2,1,0:T(8,128)(2,1)} %get-tuple-element.19), channel_id=1, source_target_pairs={{0,16},{8,24},{16,0},{24,8},{1,17},{9,25},{17,1},{25,9},{2,18},{10... | collective-permute-start | bytes 1794056 | tf_op jit(solution)/shard_map/ppermute | solution.py:75
  9.2 0.0 collective-permute-start.2
  9.2 0.0 copy-done
  9.2 0.0 copy-done.1
  9.2 0.0 copy-done.2
  9.2 1.0 %gather_own.1 = (f32[16,8,32,128]{3,2,1,0:T(8,128)S(1)}, f32[16,32,128]{2,1,0:T(8,128)S(1)}) custom-call(s32[1]{0:T(128)} %bitcast.me_ref, s32[8]{0:T(128)S(1)} %copy-done.2, bf16[8,8,4,32,128]{4,3,2,1,0:T(8,128)(2,1)S(1)} %bitcast.6, bf16[8,4,32,128]{3,2,1,0:T(8,128)(2,1)S(1)} %bitcast.9), custom_call_target="tpu_custom_call" | custom-call | flops 1048576 | bytes 4194304 | tf_op jit(solution)/shard_map/gather_own/pallas_call | solution.py:166
  10.2 8.2 %collective-permute-done.refs_0_ = bf16[73,32,128]{2,1,0:T(8,128)(2,1)S(1)} collective-permute-done((bf16[73,32,128]{2,1,0:T(8,128)(2,1)}, bf16[73,32,128]{2,1,0:T(8,128)(2,1)S(1)}, u32[]{:S(2)}, u32[]{:S(2)}) %collective-permute-start) | collective-permute-done | bytes 598048 | tf_op jit(solution)/shard_map/ppermute | solution.py:75
  18.4 16.6 %collective-permute-done.1.refs_1_ = bf16[73,32,128]{2,1,0:T(8,128)(2,1)S(1)} collective-permute-done((bf16[73,32,128]{2,1,0:T(8,128)(2,1)}, bf16[73,32,128]{2,1,0:T(8,128)(2,1)S(1)}, u32[]{:S(2)}, u32[]{:S(2)}) %collective-permute-start.1) | collective-permute-done | bytes 598048 | tf_op jit(solution)/shard_map/ppermute | solution.py:75
  35.0 0.0 collective-permute-done.2.refs_2_
  35.0 0.0 copy-start.4
  35.0 1.4 %combine_strips.1 = (bf16[10,32,512]{2,1,0:T(8,128)(2,1)S(1)}, bf16[10,32,512]{2,1,0:T(8,128)(2,1)S(1)}, bf16[10,32,512]{2,1,0:T(8,128)(2,1)S(1)}, bf16[8,32,512]{2,1,0:T(8,128)(2,1)S(1)}) custom-call(s32[1]{0:T(128)} %bitcast.me_ref, f32[16,8,32,128]{3,2,1,0:T(8,128)S(1)} %get-tuple-element.17.total_in, f32[16,32,128]{2,1,0:T(8,128)S(1)} %get-tuple-element.18.cover_in, ...), custom_call_target="tpu_custom_call" | custom-call | flops 1 | bytes 1 | tf_op jit(solution)/shard_map/combine_strips/pallas_call | solution.py:251
  36.5 0.4 collective-permute-start.3
  36.9 1.1 %collective-permute-start.4 = (bf16[10,32,512]{2,1,0:T(8,128)(2,1)S(1)}, bf16[10,32,512]{2,1,0:T(8,128)(2,1)S(1)}, u32[]{:S(2)}, u32[]{:S(2)}) collective-permute-start(bf16[10,32,512]{2,1,0:T(8,128)(2,1)S(1)} %get-tuple-element.23), channel_id=1, source_target_pairs={{0,16},{8,24},{16,0},{24,8},{1,17},{9,25},{17,1},{25,9},{2,18},{10... | collective-permute-start | bytes 983048 | tf_op jit(solution)/shard_map/ppermute | solution.py:75
  38.0 1.2 %collective-permute-start.5 = (bf16[8,32,512]{2,1,0:T(8,128)(2,1)S(1)}, bf16[8,32,512]{2,1,0:T(8,128)(2,1)S(1)}, u32[]{:S(2)}, u32[]{:S(2)}) collective-permute-start(bf16[8,32,512]{2,1,0:T(8,128)(2,1)S(1)} %get-tuple-element.24), channel_id=1, source_target_pairs={{0,24},{8,16},{16,8},{24,0},{1,25},{9,17},{17,9},{25,1},{2,26},{10... | collective-permute-start | bytes 786440 | tf_op jit(solution)/shard_map/ppermute | solution.py:75
  39.2 11.3 %collective-permute-done.5.refs_3_ = bf16[8,32,512]{2,1,0:T(8,128)(2,1)S(1)} collective-permute-done((bf16[8,32,512]{2,1,0:T(8,128)(2,1)S(1)}, bf16[8,32,512]{2,1,0:T(8,128)(2,1)S(1)}, u32[]{:S(2)}, u32[]{:S(2)}) %collective-permute-start.5) | collective-permute-done | bytes 262176 | tf_op jit(solution)/shard_map/ppermute | solution.py:75
  50.4 0.0 collective-permute-done.3.refs_1_
  50.4 0.0 collective-permute-done.4.refs_2_
  50.4 0.3 join_strips.1
  50.7 5.9 %collective-permute-start.6 = (bf16[7,144,512]{2,1,0:T(8,128)(2,1)S(1)}, bf16[7,144,512]{2,1,0:T(8,128)(2,1)S(1)}, u32[]{:S(2)}, u32[]{:S(2)}) collective-permute-start(bf16[7,144,512]{2,1,0:T(8,128)(2,1)S(1)} %get-tuple-element.25), channel_id=1, source_target_pairs={{1,2},{3,4},{5,6},{2,1},{4,3},{6,5},{9,10},{11,12},{13,14},{10,9},... | collective-permute-start | bytes 3096584 | tf_op jit(solution)/shard_map/ppermute | solution.py:543
  56.6 0.1 collective-permute-start.7
  56.7 0.0 copy-done.4
  56.7 0.0 copy-start.5
  56.7 1.1 %copy-done.5 = bf16[4,384,144]{2,1,0:T(8,128)(2,1)S(1)} copy-done((bf16[4,384,144]{2,1,0:T(8,128)(2,1)S(1)}, bf16[4,384,144]{2,1,0:T(8,128)(2,1)}, u32[]{:S(2)}) %copy-start.5) | copy-done | bytes 442392
  57.8 2.2 %smooth_own.1.own = bf16[3,8,128,512]{3,2,1,0:T(8,128)(2,1)S(1)} custom-call(s32[1]{0:T(128)} %bitcast.me_ref, bf16[4,384,144]{2,1,0:T(8,128)(2,1)S(1)} %copy-done.5, bf16[3,3,256,256]{3,2,1,0:T(8,128)(2,1)S(1)} %copy-done.4, bf16[10,32,512]{2,1,0:T(8,128)(2,1)S(1)} %get-tuple-element.21.refs_0_, bf16[10,32,512]{2,1,0:T(8,128)(2,1)S(1)} %collective-permute-done.3.refs_1_, ...), custom_call_target="tpu_custom_call" | custom-call | flops 2415919104 | bytes 6291456 | tf_op jit(solution)/shard_map/smooth_own/pallas_call | solution.py:372
  60.0 0.0 copy-start.3
  60.0 8.9 %collective-permute-done.6.outer = bf16[7,144,512]{2,1,0:T(8,128)(2,1)S(1)} collective-permute-done((bf16[7,144,512]{2,1,0:T(8,128)(2,1)S(1)}, bf16[7,144,512]{2,1,0:T(8,128)(2,1)S(1)}, u32[]{:S(2)}, u32[]{:S(2)}) %collective-permute-start.6) | collective-permute-done | bytes 1032224 | tf_op jit(solution)/shard_map/ppermute | solution.py:543
  68.9 0.0 collective-permute-done.7.inner
  68.9 8.5 %smooth_power.1 = (bf16[3,14,128,512]{3,2,1,0:T(8,128)(2,1)S(1)}, f32[96,128]{1,0:T(8,128)S(1)}) custom-call(s32[1]{0:T(128)} %bitcast.me_ref, s32[1]{0:T(128)} %bitcast.3.odd_ref, bf16[4,384,144]{2,1,0:T(8,128)(2,1)S(1)} %copy-done.5, bf16[3,3,256,256]{3,2,1,0:T(8,128)(2,1)S(1)} %copy-done.4, bf16[3,8,128,512]{3,2,1,0:T(8,128)(2,1)S(1)} %smooth_own.1.own, ...), custom_call_target="tpu_custom_call" | custom-call | flops 4227858432 | bytes 22020096 | tf_op jit(solution)/shard_map/smooth_power/pallas_call | solution.py:447
  77.4 1.5 %collective-permute-start.10 = (f32[96,128]{1,0:T(8,128)S(1)}, f32[96,128]{1,0:T(8,128)S(1)}, u32[]{:S(2)}, u32[]{:S(2)}) collective-permute-start(f32[96,128]{1,0:T(8,128)S(1)} %get-tuple-element.28.refs_0_), channel_id=1, source_target_pairs={{0,24},{8,16},{16,8},{24,0},{1,25},{9,17},{17,9},{25,1},{2,26},{10... | collective-permute-start | bytes 147464 | tf_op jit(solution)/shard_map/ppermute | solution.py:75
  78.9 0.2 collective-permute-start.9
  79.1 1.0 %collective-permute-start.8 = (f32[96,128]{1,0:T(8,128)S(1)}, f32[96,128]{1,0:T(8,128)S(1)}, u32[]{:S(2)}, u32[]{:S(2)}) collective-permute-start(f32[96,128]{1,0:T(8,128)S(1)} %get-tuple-element.28.refs_0_), channel_id=1, source_target_pairs={{0,8},{8,0},{16,24},{24,16},{1,9},{9,1},{17,25},{25,17},{2,10},{10... | collective-permute-start | bytes 147464 | tf_op jit(solution)/shard_map/ppermute | solution.py:75
  80.1 1.2 %collective-permute-done.10.refs_3_ = f32[96,128]{1,0:T(8,128)S(1)} collective-permute-done((f32[96,128]{1,0:T(8,128)S(1)}, f32[96,128]{1,0:T(8,128)S(1)}, u32[]{:S(2)}, u32[]{:S(2)}) %collective-permute-start.10) | collective-permute-done | bytes 49184 | tf_op jit(solution)/shard_map/ppermute | solution.py:75
  81.3 0.6 collective-permute-done.9.refs_2_
  81.8 0.2 collective-permute-done.8.refs_1_
  82.1 0.0 copy-done.3
  82.1 7.7 %score_cells.1 = f32[8,128,512]{2,1,0:T(8,128)} custom-call(bf16[3,8,128,512]{3,2,1,0:T(8,128)(2,1)S(1)} %smooth_own.1.own, bf16[3,14,128,512]{3,2,1,0:T(8,128)(2,1)S(1)} %get-tuple-element.27.halo, s32[3,4]{1,0:T(4,128)S(1)} %copy-done.3, f32[96,128]{1,0:T(8,128)S(1)} %get-tuple-element.28.refs_0_, f32[96,128]{1,0:T(8,128)S(1)} %collective-permute-done.8.refs_1_, ...), custom_call_target="tpu_custom_call" | custom-call | flops 62914560 | bytes 12582912 | tf_op jit(solution)/shard_map/score_cells/pallas_call | solution.py:508
Async XLA Ops:
  0.0 9.2 %copy-start = (bf16[8,8,128,128]{3,2,1,0:T(8,128)(2,1)S(1)}, bf16[8,8,128,128]{3,2,1,0:T(8,128)(2,1)}, u32[]{:S(2)}) copy-start(bf16[8,8,128,128]{3,2,1,0:T(8,128)(2,1)} %param.6) | copy-start | bytes 6291460
  0.0 9.2 %copy-start.1 = (bf16[8,128,128]{2,1,0:T(8,128)(2,1)S(1)}, bf16[8,128,128]{2,1,0:T(8,128)(2,1)}, u32[]{:S(2)}) copy-start(bf16[8,128,128]{2,1,0:T(8,128)(2,1)} %param.7) | copy-start | bytes 786436
  0.0 9.2 %copy-start.2 = (s32[8]{0:T(128)S(1)}, s32[8]{0:T(128)}, u32[]{:S(2)}) copy-start(s32[8]{0:T(128)} %owner_ref.5) | copy-start | bytes 100
  2.8 15.5 %collective-permute-start = (bf16[73,32,128]{2,1,0:T(8,128)(2,1)}, bf16[73,32,128]{2,1,0:T(8,128)(2,1)S(1)}, u32[]{:S(2)}, u32[]{:S(2)}) collective-permute-start(bf16[73,32,128]{2,1,0:T(8,128)(2,1)} %pack_pieces.2), channel_id=1, source_target_pairs={{0,8},{8,0},{16,24},{24,16},{1,9},{9,1},{17,25},{25,17},{2,10},{10... | collective-permute-start | bytes 1794056 | tf_op jit(solution)/shard_map/ppermute | solution.py:75
  7.9 27.1 %collective-permute-start.1 = (bf16[73,32,128]{2,1,0:T(8,128)(2,1)}, bf16[73,32,128]{2,1,0:T(8,128)(2,1)S(1)}, u32[]{:S(2)}, u32[]{:S(2)}) collective-permute-start(bf16[73,32,128]{2,1,0:T(8,128)(2,1)} %get-tuple-element.19), channel_id=1, source_target_pairs={{0,16},{8,24},{16,0},{24,8},{1,17},{9,25},{17,1},{25,9},{2,18},{10... | collective-permute-start | bytes 1794056 | tf_op jit(solution)/shard_map/ppermute | solution.py:75
  9.2 25.8 %collective-permute-start.2 = (bf16[73,32,128]{2,1,0:T(8,128)(2,1)}, bf16[73,32,128]{2,1,0:T(8,128)(2,1)S(1)}, u32[]{:S(2)}, u32[]{:S(2)}) collective-permute-start(bf16[73,32,128]{2,1,0:T(8,128)(2,1)} %get-tuple-element.20), channel_id=1, source_target_pairs={{0,24},{8,16},{16,8},{24,0},{1,25},{9,17},{17,9},{25,1},{2,26},{10... | collective-permute-start | bytes 1794056 | tf_op jit(solution)/shard_map/ppermute | solution.py:75
  35.0 21.6 %copy-start.4 = (bf16[3,3,256,256]{3,2,1,0:T(8,128)(2,1)S(1)}, bf16[3,3,256,256]{3,2,1,0:T(8,128)(2,1)}, u32[]{:S(2)}) copy-start(bf16[3,3,256,256]{3,2,1,0:T(8,128)(2,1)} %constant.17.clone.across) | copy-start | bytes 3538948
  36.5 14.0 %collective-permute-start.3 = (bf16[10,32,512]{2,1,0:T(8,128)(2,1)S(1)}, bf16[10,32,512]{2,1,0:T(8,128)(2,1)S(1)}, u32[]{:S(2)}, u32[]{:S(2)}) collective-permute-start(bf16[10,32,512]{2,1,0:T(8,128)(2,1)S(1)} %get-tuple-element.22), channel_id=1, source_target_pairs={{0,8},{8,0},{16,24},{24,16},{1,9},{9,1},{17,25},{25,17},{2,10},{10... | collective-permute-start | bytes 983048 | tf_op jit(solution)/shard_map/ppermute | solution.py:75
  36.9 13.6 %collective-permute-start.4 = (bf16[10,32,512]{2,1,0:T(8,128)(2,1)S(1)}, bf16[10,32,512]{2,1,0:T(8,128)(2,1)S(1)}, u32[]{:S(2)}, u32[]{:S(2)}) collective-permute-start(bf16[10,32,512]{2,1,0:T(8,128)(2,1)S(1)} %get-tuple-element.23), channel_id=1, source_target_pairs={{0,16},{8,24},{16,0},{24,8},{1,17},{9,25},{17,1},{25,9},{2,18},{10... | collective-permute-start | bytes 983048 | tf_op jit(solution)/shard_map/ppermute | solution.py:75
  38.0 12.4 %collective-permute-start.5 = (bf16[8,32,512]{2,1,0:T(8,128)(2,1)S(1)}, bf16[8,32,512]{2,1,0:T(8,128)(2,1)S(1)}, u32[]{:S(2)}, u32[]{:S(2)}) collective-permute-start(bf16[8,32,512]{2,1,0:T(8,128)(2,1)S(1)} %get-tuple-element.24), channel_id=1, source_target_pairs={{0,24},{8,16},{16,8},{24,0},{1,25},{9,17},{17,9},{25,1},{2,26},{10... | collective-permute-start | bytes 786440 | tf_op jit(solution)/shard_map/ppermute | solution.py:75
  50.7 18.2 %collective-permute-start.6 = (bf16[7,144,512]{2,1,0:T(8,128)(2,1)S(1)}, bf16[7,144,512]{2,1,0:T(8,128)(2,1)S(1)}, u32[]{:S(2)}, u32[]{:S(2)}) collective-permute-start(bf16[7,144,512]{2,1,0:T(8,128)(2,1)S(1)} %get-tuple-element.25), channel_id=1, source_target_pairs={{1,2},{3,4},{5,6},{2,1},{4,3},{6,5},{9,10},{11,12},{13,14},{10,9},... | collective-permute-start | bytes 3096584 | tf_op jit(solution)/shard_map/ppermute | solution.py:543
  56.6 12.3 %collective-permute-start.7 = (bf16[7,144,512]{2,1,0:T(8,128)(2,1)S(1)}, bf16[7,144,512]{2,1,0:T(8,128)(2,1)S(1)}, u32[]{:S(2)}, u32[]{:S(2)}) collective-permute-start(bf16[7,144,512]{2,1,0:T(8,128)(2,1)S(1)} %get-tuple-element.26), channel_id=1, source_target_pairs={{0,1},{2,3},{4,5},{6,7},{1,0},{3,2},{5,4},{7,6},{8,9},{10,11},{12,... | collective-permute-start | bytes 3096584 | tf_op jit(solution)/shard_map/ppermute | solution.py:543
  56.7 1.1 %copy-start.5 = (bf16[4,384,144]{2,1,0:T(8,128)(2,1)S(1)}, bf16[4,384,144]{2,1,0:T(8,128)(2,1)}, u32[]{:S(2)}) copy-start(bf16[4,384,144]{2,1,0:T(8,128)(2,1)} %constant.18.clone.down) | copy-start | bytes 1327108
  60.0 22.0 %copy-start.3 = (s32[3,4]{1,0:T(4,128)S(1)}, s32[3,4]{1,0:T(4,128)}, u32[]{:S(2)}) copy-start(s32[3,4]{1,0:T(4,128)} %clips.1) | copy-start | bytes 148
  77.4 3.9 %collective-permute-start.10 = (f32[96,128]{1,0:T(8,128)S(1)}, f32[96,128]{1,0:T(8,128)S(1)}, u32[]{:S(2)}, u32[]{:S(2)}) collective-permute-start(f32[96,128]{1,0:T(8,128)S(1)} %get-tuple-element.28.refs_0_), channel_id=1, source_target_pairs={{0,24},{8,16},{16,8},{24,0},{1,25},{9,17},{17,9},{25,1},{2,26},{10... | collective-permute-start | bytes 147464 | tf_op jit(solution)/shard_map/ppermute | solution.py:75
  78.9 2.9 %collective-permute-start.9 = (f32[96,128]{1,0:T(8,128)S(1)}, f32[96,128]{1,0:T(8,128)S(1)}, u32[]{:S(2)}, u32[]{:S(2)}) collective-permute-start(f32[96,128]{1,0:T(8,128)S(1)} %get-tuple-element.28.refs_0_), channel_id=1, source_target_pairs={{0,16},{8,24},{16,0},{24,8},{1,17},{9,25},{17,1},{25,9},{2,18},{10... | collective-permute-start | bytes 147464 | tf_op jit(solution)/shard_map/ppermute | solution.py:75
  79.1 2.9 %collective-permute-start.8 = (f32[96,128]{1,0:T(8,128)S(1)}, f32[96,128]{1,0:T(8,128)S(1)}, u32[]{:S(2)}, u32[]{:S(2)}) collective-permute-start(f32[96,128]{1,0:T(8,128)S(1)} %get-tuple-element.28.refs_0_), channel_id=1, source_target_pairs={{0,8},{8,0},{16,24},{24,16},{1,9},{9,1},{17,25},{25,17},{2,10},{10... | collective-permute-start | bytes 147464 | tf_op jit(solution)/shard_map/ppermute | solution.py:75
